TPU v7x, 128 devices: a whole 4x4x4 slice. The times are simulated.
128 devices in a mesh: dp: 16 (over z, x_hi, core), tensor: 8 (over x_lo, y).
Axes of the slice: x: 4 (x_hi: 2, x_lo: 2; x = x_hi * 2 + x_lo), y: 4, z: 4, core: 2. Of those that a mesh axis runs over, the one named last changes fastest.
Arguments:
- queries: bfloat16 [2048, 8192], P('dp', 'tensor'), may hold values from -130 to 130
- new_key: bfloat16 [2048, 1024], P('dp', 'tensor'), may hold values from -5 to 5
- new_value: bfloat16 [2048, 1024], P('dp', 'tensor'), may hold values from -5 to 5
- cache_keys: bfloat16 [2048, 8, 128, 128], P('dp', 'tensor'), may hold values from -5 to 5
- cache_values: bfloat16 [2048, 8, 128, 128], P('dp', 'tensor'), may hold values from -5 to 5
- lengths: int32 [2048], P('dp'), may hold values from 2 to 128, as said below
- prefix_keys: bfloat16 [32, 8, 2048, 128], P('dp', 'tensor'), may hold values from -5 to 5
- prefix_values: bfloat16 [32, 8, 2048, 128], P('dp', 'tensor'), may hold values from -5 to 5
- prompt_ids: int32 [2048], P('dp'), may hold values from 0 to 31, as said below
- cluster_ids: int32 [2048], P('dp'), may hold values from 0 to 15
- out_weight: bfloat16 [8192, 8192], P('tensor', 'dp'), may hold values from -0.25 to 0.25
- residual: bfloat16 [2048, 8192], P('tensor', 'dp'), may hold values from -4 to 4
- norm_gain: bfloat16 [8192], P('dp'), may hold values from 0.099609375 to 1.8984375
- up_weight: bfloat16 [8192, 4096], P('dp'), may hold values from -0.09375 to 0.09375
- head_weight: bfloat16 [4096], replicated, may hold values from -0.09375 to 0.09375
Outputs:
- hidden: bfloat16 [2048, 8192], P('tensor', 'dp')
- scores: float32 [2048], P('tensor')
- votes: float32 [32, 16], replicated
Inputs may be any that keep to these rules, and one draw needn't show every extreme that they name: `lengths`: live slots of a row; some row in every draw has all 128. `prompt_ids`: rows k * 128 to (k + 1) * 128 - 1 belong to prompts k * 2 to (k + 1) * 2 - 1.
All inputs are finite; a program needn't handle non-finite values.
Results may differ from a plain program's by a relative error of at most 0.015.
Values may be sent and summed in bfloat16 or wider, within the bound.
No kernel may reach another device: no remote copies, remote signals or barrier semaphores. Data moves between devices by JAX's collectives and lax.ppermute only.
A program may use at most 128 MiB of HBM per device.

v0:
```python
import math

import jax
import jax.numpy as jnp
from jax import lax
from jax.sharding import PartitionSpec as P

D = 8192
CLUSTERS = 16


eps = 1e-05


def attend(
    queries,
    new_key,
    new_value,
    cache_keys,
    cache_values,
    lengths,
    prefix_keys,
    prefix_values,
    local_prompt,
):
    rows_blk = queries.shape[0]
    kv_heads = cache_keys.shape[1]
    head_dim = cache_keys.shape[3]
    groups = queries.shape[1] // (kv_heads * head_dim)
    prompts_blk = prefix_keys.shape[0]
    gen_len = cache_keys.shape[2]
    score_scale = 1.0 / math.sqrt(head_dim)
    grouped = queries.reshape(rows_blk, kv_heads, groups, head_dim)
    pre_scores = (
        jnp.einsum("rkgd,pkjd->rkgpj", grouped, prefix_keys, preferred_element_type=jnp.float32)
        * score_scale
    )
    pre_ok = (local_prompt[:, None] == jnp.arange(prompts_blk, dtype=jnp.int32)[None, :])[
        :, None, None, :, None
    ]
    gen_scores = (
        jnp.einsum("rkgd,rkjd->rkgj", grouped, cache_keys, preferred_element_type=jnp.float32)
        * score_scale
    )
    gen_ok = (jnp.arange(gen_len, dtype=jnp.int32)[None, :] < lengths[:, None])[:, None, None, :]
    own_key = new_key.reshape(rows_blk, kv_heads, head_dim)
    own_scores = (
        jnp.einsum("rkgd,rkd->rkg", grouped, own_key, preferred_element_type=jnp.float32)
        * score_scale
    )
    pre_scores = jnp.where(pre_ok, pre_scores, -1e30)
    gen_scores = jnp.where(gen_ok, gen_scores, -1e30)
    row_top = jnp.maximum(
        jnp.maximum(jnp.max(pre_scores, axis=(3, 4)), jnp.max(gen_scores, axis=3)), own_scores
    )
    pre_exp = jnp.exp(pre_scores - row_top[..., None, None])
    gen_exp = jnp.exp(gen_scores - row_top[..., None])
    own_exp = jnp.exp(own_scores - row_top)
    denominator = jnp.sum(pre_exp, axis=(3, 4)) + jnp.sum(gen_exp, axis=3) + own_exp
    pre_w = (pre_exp / denominator[..., None, None]).astype(jnp.bfloat16)
    gen_w = (gen_exp / denominator[..., None]).astype(jnp.bfloat16)
    own_w = (own_exp / denominator).astype(jnp.bfloat16)
    own_val = new_value.reshape(rows_blk, kv_heads, head_dim).astype(jnp.float32)
    result = jnp.einsum(
        "rkgpj,pkjd->rkgd", pre_w, prefix_values, preferred_element_type=jnp.float32
    )
    result = result + jnp.einsum(
        "rkgj,rkjd->rkgd", gen_w, cache_values, preferred_element_type=jnp.float32
    )
    result = result + own_w.astype(jnp.float32)[..., None] * own_val[:, :, None, :]
    return result.reshape(rows_blk, kv_heads * groups * head_dim).astype(jnp.bfloat16)


def body(
    queries,
    new_key,
    new_value,
    cache_keys,
    cache_values,
    lengths,
    prefix_keys,
    prefix_values,
    prompt_ids,
    cluster_ids,
    out_weight,
    residual,
    norm_gain,
    up_weight,
    head_weight,
):
    prompts_dev = prefix_keys.shape[0]
    dp_index = lax.axis_index("dp")
    local_prompt = prompt_ids - dp_index * prompts_dev
    attended = attend(
        queries,
        new_key,
        new_value,
        cache_keys,
        cache_values,
        lengths,
        prefix_keys,
        prefix_values,
        local_prompt,
    )
    head_terms = jnp.dot(
        lax.all_gather(attended, "dp", axis=0, tiled=True),
        out_weight,
        preferred_element_type=jnp.float32,
    )
    mixed_out = lax.psum_scatter(head_terms, "tensor", scatter_dimension=0, tiled=True)
    hidden = (residual.astype(jnp.float32) + mixed_out).astype(jnp.bfloat16)
    rows_here = hidden.shape[0]
    first_local = lax.axis_index("tensor") * rows_here
    all_prompts, all_clusters = (
        lax.all_gather(prompt_ids, "dp", axis=0, tiled=True),
        lax.all_gather(cluster_ids, "dp", axis=0, tiled=True),
    )
    my_prompts = lax.dynamic_slice_in_dim(all_prompts, first_local, rows_here, 0)
    my_clusters = lax.dynamic_slice_in_dim(all_clusters, first_local, rows_here, 0)
    widened = hidden.astype(jnp.float32)
    squares = lax.psum(jnp.sum(widened * widened, axis=1), "dp")
    normed = (
        widened * lax.rsqrt(squares / D + eps)[:, None] * norm_gain.astype(jnp.float32)[None, :]
    ).astype(jnp.bfloat16)
    partial_up = jnp.dot(normed, up_weight, preferred_element_type=jnp.float32)
    prompts_total = prompts_dev * lax.axis_size("dp")
    pair_ids = my_prompts * CLUSTERS + my_clusters
    one_hot = (
        pair_ids[:, None] == jnp.arange(prompts_total * CLUSTERS, dtype=jnp.int32)[None, :]
    ).astype(jnp.float32)
    head_wide = head_weight.astype(jnp.float32)
    summed_up = lax.psum(partial_up, "dp")
    scores = jnp.sum(jax.nn.silu(summed_up) * head_wide[None, :], axis=1)
    vote_terms = jnp.dot(scores, one_hot, precision=lax.Precision.HIGHEST)
    vote_sums = lax.psum(vote_terms, "tensor")
    return (hidden, scores, vote_sums.reshape(prompts_total, CLUSTERS))


def solution(mesh):
    placed = (
        P("dp", "tensor"),
        P("dp", "tensor"),
        P("dp", "tensor"),
        P("dp", "tensor", None, None),
        P("dp", "tensor", None, None),
        P("dp"),
        P("dp", "tensor", None, None),
        P("dp", "tensor", None, None),
        P("dp"),
        P("dp"),
        P("tensor", "dp"),
        P("tensor", "dp"),
        P("dp"),
        P("dp", None),
        P(),
    )
    return jax.shard_map(
        body,
        mesh=mesh,
        in_specs=placed,
        out_specs=(P("tensor", "dp"), P("tensor"), P()),
        check_vma=False,
    )
```

profile of v0, /device:TPU:0, one launch (start us, length us, event | category | flops | bytes accessed | tf_op | source)
XLA Modules:
  0.0 401.8 jit_solution(6961407428536975936)
XLA Ops:
  7.2 0.0 copy-start
  7.2 0.0 copy-start.2
  7.2 0.0 copy-start.11
  7.2 0.0 all-gather.4.cloned.1.call-start
  7.3 0.7 broadcast_subtract_fusion
  8.0 1.0 copy.60
  9.0 0.7 iota_compare_fusion.2
  9.8 4.5 %fusion.47 = (f32[128,8]{1,0:T(8,128)S(1)}, f32[128,8,128]{2,1,0:T(8,128)S(1)}) fusion(bf16[128,8,128]{2,1,0:T(8,128)(2,1)S(1)} %bitcast.117, bf16[128,1,128,128]{3,2,1,0:T(8,128)(2,1)} %param.18, pred[128,128]{1,0:T(8,128)(4,1)S(1)} %iota_compare_fusion.2), kind=kOutput, calls=%fused_computation.55 | convolution fusion | flops 33946624 | bytes 5001216 | tf_op jit(solution)/shard_map/rkgd,rkjd->rkgj/dot_general | solution.py:42
  14.3 0.1 copy.43
  14.4 0.0 copy-done.11
  14.4 0.3 fusion.42
  14.7 0.0 copy-done
  14.7 0.0 copy-done.2
  14.7 7.0 %fusion.1 = (f32[128,8]{0,1:T(8,128)S(1)}, f32[2,2048,128,8]{2,1,3,0:T(8,128)}) fusion(pred[128,2]{0,1:T(4,128)(4,1)S(1)} %iota_compare_fusion.3, bf16[2,1,2048,128]{3,2,1,0:T(8,128)(2,1)S(1)} %copy-done, bf16[128,1024]{1,0:T(8,128)(2,1)S(1)} %copy-done.2), kind=kOutput, calls=%fused_computation.4 | convolution fusion | flops 1086323712 | bytes 18092288 | tf_op jit(solution)/shard_map/rkgd,pkjd->rkgpj/dot_general | solution.py:35
  21.7 0.1 copy.44
  21.8 9.0 %fusion = f32[128,8]{0,1:T(8,128)S(1)} fusion(f32[2,2048,128,8]{2,1,3,0:T(8,128)} %get-tuple-element.17, f32[128,8]{0,1:T(8,128)S(1)} %maximum_maximum_fusion, pred[128,2]{0,1:T(4,128)(4,1)S(1)} %iota_compare_fusion.3), kind=kLoop, calls=%fused_computation.3 | loop fusion | flops 16776192 | bytes 16785664 | tf_op jit(solution)/shard_map/reduce_sum | solution.py:59
  30.9 0.0 copy-start.4
  30.9 0.0 copy-start.10
  30.9 0.4 fusion.33
  31.3 0.1 copy.48
  31.5 3.4 fusion.4
  34.9 0.2 copy.49
  35.1 0.0 copy-done.4
  35.1 0.1 copy.50
  35.3 0.0 copy-done.10
  35.3 8.7 %fusion.23 = bf16[128,1,8,128]{0,3,2,1:T(8,128)(2,1)} fusion(f32[128,8]{0,1:T(8,128)S(1)} %get-tuple-element.15, f32[128,8]{0,1:T(8,128)S(1)} %maximum_maximum_fusion, f32[2,2048,128,8]{2,1,3,0:T(8,128)} %get-tuple-element.17, pred[128,2]{0,1:T(4,128)(4,1)S(1)} %iota_compare_fusion.3, bf16[2,1,2048,128]{3,2,1,0:T(8,128)(2,1)S(1)} %copy-done.10, ...), kind=kOutput, calls=%fused_computation.17 | convolution fusion | flops 1095237632 | bytes 18690304 | tf_op jit(solution)/shard_map/rkgpj,pkjd->rkgd/dot_general | solution.py:64
  44.0 0.0 all-gather.4.cloned.1.call-update
  44.0 0.2 reduce-scatter.2.cloned.1.call-start
  44.2 59.3 %all-gather.4.cloned.1.call-done = bf16[2048,1024]{0,1:T(8,128)(2,1)} async-done(((bf16[128,1024]{0,1:T(8,128)(2,1)}), bf16[2048,1024]{0,1:T(8,128)(2,1)}) %all-gather.4.cloned.1.call-update) | async-done | bytes 4194320 | tf_op jit(solution)/shard_map/all_gather | solution.py:106
  103.5 6.8 %fusion.48 = f32[2048,512]{1,0:T(8,128)} fusion(bf16[2048,1024]{0,1:T(8,128)(2,1)} %all-gather.4.cloned.1.call-done, bf16[1024,512]{1,0:T(8,128)(2,1)} %param.25), kind=kOutput, calls=%fused_computation.56 | convolution fusion | flops 2147483648 | bytes 9437184 | tf_op jit(solution)/shard_map/dot_general | solution.py:105
  110.3 0.0 copy-start.7
  110.3 0.0 copy-start.3
  110.3 0.0 reduce-scatter.2.cloned.1.call-update
  110.3 0.0 all-reduce.2.cloned.1.call-start
  110.4 0.6 copy-done.7
  111.0 50.2 %reduce-scatter.2.cloned.1.call-done = f32[256,512]{1,0:T(8,128)} async-done(((f32[2048,512]{1,0:T(8,128)}), f32[256,512]{1,0:T(8,128)}) %reduce-scatter.2.cloned.1.call-update) | async-done | bytes 524304 | tf_op jit(solution)/shard_map/reduce_scatter | solution.py:110
  161.2 0.0 copy-done.3
  161.2 1.2 fusion.29
  162.4 0.0 copy-start.1
  162.4 37.7 %psum.21 = f32[256]{0:T(256)S(1)} all-reduce(f32[256]{0:T(256)S(1)} %get-tuple-element.12), channel_id=1, replica_groups=mesh['dp'=16,'tensor'=8] {'dp'}, use_global_device_ids=true, to_apply=%region_6.7 | all-reduce | flops 256 | bytes 2048 | tf_op jit(solution)/shard_map/psum | solution.py:121
  200.1 5.5 %fusion.34 = f32[256,4096]{1,0:T(8,128)} fusion(bf16[512,4096]{1,0:T(8,128)(2,1)} %param.28, bf16[256,512]{1,0:T(8,128)(2,1)S(1)} %get-tuple-element.13, f32[512]{0:T(512)S(1)} %convert_element_type.54, f32[256]{0:T(256)S(1)} %add_rsqrt_fusion), kind=kOutput, calls=%fused_computation.32 | convolution fusion | flops 1074266112 | bytes 8653824 | tf_op jit(solution)/shard_map/dot_general | solution.py:125
  205.6 0.0 copy-done.1
  205.6 0.0 copy-start.5
  205.6 0.0 copy-start.8
  205.6 0.0 copy-start.9
  205.6 0.0 all-reduce.2.cloned.1.call-update
  205.6 0.7 copy-done.5
  206.3 0.0 copy-done.8
  206.3 18.9 %all-gather = s32[16,1,128]{2,1,0:T(1,128)S(1)} all-gather(s32[1,1,128]{2,1,0:T(1,128)S(1)} %bitcast.124), channel_id=1, replica_groups=mesh['dp'=16,'tensor'=8] {'dp'}, dimensions={0}, use_global_device_ids=true | all-gather | bytes 8704 | tf_op jit(solution)/shard_map/all_gather | solution.py:115
  225.1 0.0 copy-done.9
  225.2 22.4 %all-gather.1 = s32[16,1,128]{2,1,0:T(1,128)S(1)} all-gather(s32[1,1,128]{2,1,0:T(1,128)S(1)} %bitcast.125), channel_id=1, replica_groups=mesh['dp'=16,'tensor'=8] {'dp'}, dimensions={0}, use_global_device_ids=true | all-gather | bytes 8704 | tf_op jit(solution)/shard_map/all_gather | solution.py:116
  247.5 0.1 dynamic-slice_add_fusion
  247.6 110.0 %all-reduce.2.cloned.1.call-done = f32[256,4096]{1,0:T(8,128)} async-done(((f32[256,4096]{1,0:T(8,128)}), f32[256,4096]{1,0:T(8,128)}) %all-reduce.2.cloned.1.call-update) | async-done | bytes 4194320 | tf_op jit(solution)/shard_map/psum | solution.py:132
  357.6 3.4 multiply_reduce_fusion
  361.0 0.0 copy-start.6
  361.0 0.3 fusion.32
  361.3 0.1 reshape.156
  361.4 33.2 %psum.23 = f32[32,16]{1,0:T(8,128)S(1)} all-reduce(f32[32,16]{1,0:T(8,128)S(1)} %reshape.156), channel_id=1, replica_groups=mesh['dp'=16,'tensor'=8] {'tensor'}, use_global_device_ids=true, to_apply=%region_9.10 | all-reduce | flops 512 | bytes 4096 | tf_op jit(solution)/shard_map/psum | solution.py:135
  394.6 0.7 copy.51
  395.3 0.0 copy-done.6
  (8 shorter events, 0.1 us)
Async XLA Ops:
  7.2 7.5 %copy-start = (bf16[2,1,2048,128]{3,2,1,0:T(8,128)(2,1)S(1)}, bf16[2,1,2048,128]{3,2,1,0:T(8,128)(2,1)}, u32[]{:S(2)}) copy-start(bf16[2,1,2048,128]{3,2,1,0:T(8,128)(2,1)} %param.21) | copy-start | bytes 3145732
  7.2 7.5 %copy-start.2 = (bf16[128,1024]{1,0:T(8,128)(2,1)S(1)}, bf16[128,1024]{1,0:T(8,128)(2,1)}, u32[]{:S(2)}) copy-start(bf16[128,1024]{1,0:T(8,128)(2,1)} %param.15) | copy-start | bytes 786436
  7.2 7.2 %copy-start.11 = (bf16[128,128]{1,0:T(8,128)(2,1)S(1)}, bf16[128,128]{1,0:T(8,128)(2,1)}, u32[]{:S(2)}) copy-start(bf16[128,128]{1,0:T(8,128)(2,1)} %param.16) | copy-start | bytes 98308
  7.2 96.3 %all-gather.4.cloned.1.call-start = ((), (), s32[]{:S(2)}) async-start(), calls=%async_computation.1 | async-start | bytes 4456448 | tf_op jit(solution)/shard_map/all_gather | solution.py:106
  30.9 4.3 %copy-start.4 = (bf16[128,128]{1,0:T(8,128)(2,1)S(1)}, bf16[128,128]{1,0:T(8,128)(2,1)}, u32[]{:S(2)}) copy-start(bf16[128,128]{1,0:T(8,128)(2,1)} %param.17) | copy-start | bytes 98308
  30.9 4.4 %copy-start.10 = (bf16[2,1,2048,128]{3,2,1,0:T(8,128)(2,1)S(1)}, bf16[2,1,2048,128]{3,2,1,0:T(8,128)(2,1)}, u32[]{:S(2)}) copy-start(bf16[2,1,2048,128]{3,2,1,0:T(8,128)(2,1)} %param.22) | copy-start | bytes 3145732
  44.0 117.2 %reduce-scatter.2.cloned.1.call-start = ((), (), s32[]{:S(2)}) async-start(), calls=%async_computation.2 | async-start | bytes 4718592 | tf_op jit(solution)/shard_map/reduce_scatter | solution.py:110
  110.3 0.7 copy-start.7
  110.3 50.9 %copy-start.3 = (bf16[256,512]{1,0:T(8,128)(2,1)S(1)}, bf16[256,512]{1,0:T(8,128)(2,1)}, u32[]{:S(2)}) copy-start(bf16[256,512]{1,0:T(8,128)(2,1)} %param.26) | copy-start | bytes 786436
  110.3 247.3 %all-reduce.2.cloned.1.call-start = ((), (), s32[]{:S(2)}) async-start(), calls=%async_computation.3 | async-start | bytes 8388608 | tf_op jit(solution)/shard_map/psum | solution.py:132
  162.4 43.2 %copy-start.1 = (bf16[256,512]{1,0:T(8,128)(2,1)}, bf16[256,512]{1,0:T(8,128)(2,1)S(1)}, u32[]{:S(2)}) copy-start(bf16[256,512]{1,0:T(8,128)(2,1)S(1)} %get-tuple-element.13) | copy-start | bytes 786436
  205.6 0.7 copy-start.5
  205.6 0.7 copy-start.8
  205.6 19.6 %copy-start.9 = (s32[128]{0:T(128)S(1)}, s32[128]{0:T(128)}, u32[]{:S(2)}) copy-start(s32[128]{0:T(128)} %param.24) | copy-start | bytes 1540
  361.0 34.3 %copy-start.6 = (f32[256]{0:T(256)}, f32[256]{0:T(256)S(1)}, u32[]{:S(2)}) copy-start(f32[256]{0:T(256)S(1)} %multiply_reduce_fusion) | copy-start | bytes 3076
Sparse Core Ops, SparseCore 0:
  44.1 59.3 all-gather.3
  110.4 50.6 reduce-scatter.1
  205.7 151.8 all-reduce.1
where the time goes:
time: 402 us
  waiting for transfers between devices  220 us (55%)
  blocking collectives  112 us (28%)
  matrix products  36.6 us (9%)
  other arithmetic  15.6 us (4%)
  between operations  13.9 us (3%)
    psum x1, waiting for transfers between devices, body(): summed_up = lax.psum(partial_up, 'dp')  110 us
    all_gather x1, waiting for transfers between devices, body(): lax.all_gather(attended, 'dp', axis=0, tiled=True)  59.3 us
    reduce_scatter x1, waiting for transfers between devices, body(): lax.psum_scatter(head_terms, 'tensor', scatter_dimension=0, tiled=True)  50.2 us
    psum x1, blocking collectives, body(): squares = lax.psum(jnp.sum(widened * widened, axis=1), 'dp')  37.7 us
    psum x1, blocking collectives, body(): vote_sums = lax.psum(vote_terms, 'tensor')  33.2 us
    all_gather x1, blocking collectives, body(): lax.all_gather(cluster_ids, 'dp', axis=0, tiled=True)  22.4 us
    all_gather x1, blocking collectives, body(): lax.all_gather(prompt_ids, 'dp', axis=0, tiled=True)  18.9 us
    reduce_sum x1, other arithmetic, attend(): jnp.sum(pre_exp, axis=(3, 4)) + jnp.sum(gen_exp, axis=3) + own_exp  9.02 us
  transfers between devices with their start and end apart: 3, of which 3 were waited for; matrix products, arithmetic and copies ran while one was open for 0% of the time, Pallas kernels for 0%

commit v1 on v0

v1 whole, which is shorter than its diff:
```python
import math

import jax
import jax.numpy as jnp
from jax import lax
from jax.experimental import pallas as pl
from jax.experimental.pallas import tpu as pltpu
from jax.sharding import Mesh, PartitionSpec as P

D = 8192
CLUSTERS = 16
PROMPTS_DEV = 2
eps = 1e-05
AXES = ("z", "xh", "c", "xl", "yh", "yl")
DP = ("z", "xh", "c")
TP = ("xl", "yh", "yl")
BF = jnp.bfloat16
F32 = jnp.float32


def attend(
    queries,
    new_key,
    new_value,
    cache_keys,
    cache_values,
    lengths,
    prefix_keys,
    prefix_values,
    local_prompt,
):
    rows_blk = queries.shape[0]
    kv_heads = cache_keys.shape[1]
    head_dim = cache_keys.shape[3]
    groups = queries.shape[1] // (kv_heads * head_dim)
    prompts_blk = prefix_keys.shape[0]
    gen_len = cache_keys.shape[2]
    score_scale = 1.0 / math.sqrt(head_dim)
    grouped = queries.reshape(rows_blk, kv_heads, groups, head_dim)
    pre_scores = (
        jnp.einsum("rkgd,pkjd->rkgpj", grouped, prefix_keys, preferred_element_type=jnp.float32)
        * score_scale
    )
    pre_ok = (local_prompt[:, None] == jnp.arange(prompts_blk, dtype=jnp.int32)[None, :])[
        :, None, None, :, None
    ]
    gen_scores = (
        jnp.einsum("rkgd,rkjd->rkgj", grouped, cache_keys, preferred_element_type=jnp.float32)
        * score_scale
    )
    gen_ok = (jnp.arange(gen_len, dtype=jnp.int32)[None, :] < lengths[:, None])[:, None, None, :]
    own_key = new_key.reshape(rows_blk, kv_heads, head_dim)
    own_scores = (
        jnp.einsum("rkgd,rkd->rkg", grouped, own_key, preferred_element_type=jnp.float32)
        * score_scale
    )
    pre_scores = jnp.where(pre_ok, pre_scores, -1e30)
    gen_scores = jnp.where(gen_ok, gen_scores, -1e30)
    row_top = jnp.maximum(
        jnp.maximum(jnp.max(pre_scores, axis=(3, 4)), jnp.max(gen_scores, axis=3)), own_scores
    )
    pre_exp = jnp.exp(pre_scores - row_top[..., None, None])
    gen_exp = jnp.exp(gen_scores - row_top[..., None])
    own_exp = jnp.exp(own_scores - row_top)
    denominator = jnp.sum(pre_exp, axis=(3, 4)) + jnp.sum(gen_exp, axis=3) + own_exp
    pre_w = (pre_exp / denominator[..., None, None]).astype(jnp.bfloat16)
    gen_w = (gen_exp / denominator[..., None]).astype(jnp.bfloat16)
    own_w = (own_exp / denominator).astype(jnp.bfloat16)
    own_val = new_value.reshape(rows_blk, kv_heads, head_dim).astype(jnp.float32)
    result = jnp.einsum(
        "rkgpj,pkjd->rkgd", pre_w, prefix_values, preferred_element_type=jnp.float32
    )
    result = result + jnp.einsum(
        "rkgj,rkjd->rkgd", gen_w, cache_values, preferred_element_type=jnp.float32
    )
    result = result + own_w.astype(jnp.float32)[..., None] * own_val[:, :, None, :]
    return result.reshape(rows_blk, kv_heads * groups * head_dim).astype(jnp.bfloat16)


def swap(x, axis):
    return lax.ppermute(x, axis, [(0, 1), (1, 0)])


def shift(x, by):
    return lax.ppermute(x, "z", [(i, (i + by) % 4) for i in range(4)])


def proj_kernel(z_ref, here, before, after, far_a, far_b, w00, w01, w10, w11, out_ref):
    step = pl.program_id(0)

    def work(a, rows):
        own, par = a[:, :1024], a[:, 1024:]
        for j, (wo, wp) in enumerate(((w00, w10), (w01, w11))):
            acc = jnp.dot(own, wo[...], preferred_element_type=F32)
            acc = acc + jnp.dot(par, wp[...], preferred_element_type=F32)
            out_ref[0, rows, j * 512 : (j + 1) * 512] = acc.astype(BF)

    full = slice(0, 128)

    @pl.when(step == 0)
    def _():
        work(here[...], full)

    @pl.when(step == 1)
    def _():
        work(before[...], full)

    @pl.when(step == 2)
    def _():
        work(jnp.concatenate([far_a[...], far_b[...]], axis=0), full)

    @pl.when(step == 3)
    def _():
        work(after[...], full)


def project(here, before, after, far_a, far_b, w00, w01, w10, w11):
    z = lax.axis_index("z").astype(jnp.int32).reshape(1)
    whole = lambda a: pl.BlockSpec(a.shape, lambda s, z_ref: (0,) * a.ndim)
    ins = (here, before, after, far_a, far_b, w00, w01, w10, w11)
    return pl.pallas_call(
        proj_kernel,
        out_shape=jax.ShapeDtypeStruct((4, 128, 1024), BF),
        grid_spec=pltpu.PrefetchScalarGridSpec(
            num_scalar_prefetch=1,
            grid=(4,),
            in_specs=[whole(a) for a in ins],
            out_specs=pl.BlockSpec((1, 128, 1024), lambda s, z_ref: ((z_ref[0] + 4 - s) % 4, 0, 0)),
        ),
        compiler_params=pltpu.CompilerParams(vmem_limit_bytes=40 * 1024 * 1024),
        cost_estimate=pl.CostEstimate(
            flops=2 * 512 * 2048 * 1024, bytes_accessed=7 * 1024 * 1024, transcendentals=0
        ),
    )(z, *ins)


def body(
    queries,
    new_key,
    new_value,
    cache_keys,
    cache_values,
    lengths,
    prefix_keys,
    prefix_values,
    prompt_ids,
    cluster_ids,
    out_weight,
    residual,
    norm_gain,
    up_weight,
    head_weight,
):
    c = lax.axis_index("c")
    xh = lax.axis_index("xh")
    yl = lax.axis_index("yl")
    t = lax.axis_index(TP)
    dp_index = lax.axis_index(DP)
    local_prompt = prompt_ids - dp_index * PROMPTS_DEV

    w00 = out_weight
    w10 = swap(out_weight, "yl")
    w01 = swap(w00, "c")
    w11 = swap(w10, "c")
    up_par = swap(up_weight, "c")
    res_mine = lax.dynamic_slice_in_dim(residual, c * 128, 128, 0)
    res_send = lax.dynamic_slice_in_dim(residual, (1 - c) * 128, 128, 0)
    extra = swap(
        jnp.concatenate([res_send, jnp.broadcast_to(norm_gain[None, :], (16, 512))], axis=0), "c"
    )
    res_par, gain_par = extra[:128], extra[128]

    attended = attend(
        queries,
        new_key,
        new_value,
        cache_keys,
        cache_values,
        lengths,
        prefix_keys,
        prefix_values,
        local_prompt,
    )

    first = lax.ppermute(attended, ("xh", "yl"), [(0, 2), (3, 1), (1, 0), (2, 3)])
    second = lax.ppermute(attended, ("xh", "yl"), [(1, 2), (2, 1)])
    diagonal = xh == yl
    here = jnp.concatenate(
        [jnp.where(diagonal, attended, first), jnp.where(diagonal, first, second)], axis=1
    )
    before = shift(here, 1)
    after = shift(here, -1)
    far_a = shift(before[:64], 1)
    far_b = shift(after[64:], -1)
    partial = project(here, before, after, far_a, far_b, w00, w01, w10, w11)
    parts = lax.all_to_all(partial, ("xl", "yh"), 0, 0, tiled=True)
    mixed = jnp.sum(parts.astype(F32), axis=0)
    hid_mine = (res_mine.astype(F32) + mixed[:, :512]).astype(BF)
    hid_par = (res_par.astype(F32) + mixed[:, 512:]).astype(BF)
    hid_back = swap(hid_par, "c")
    hidden = jnp.where(
        c == 0,
        jnp.concatenate([hid_mine, hid_back], axis=0),
        jnp.concatenate([hid_back, hid_mine], axis=0),
    )

    wide_mine, wide_par = hid_mine.astype(F32), hid_par.astype(F32)
    squares = jnp.sum(wide_mine * wide_mine, axis=1) + jnp.sum(wide_par * wide_par, axis=1)
    gained_mine = (wide_mine * norm_gain.astype(F32)[None, :]).astype(BF)
    gained_par = (wide_par * gain_par.astype(F32)[None, :]).astype(BF)
    up = jnp.dot(gained_mine, up_weight, preferred_element_type=F32) + jnp.dot(
        gained_par, up_par, preferred_element_type=F32
    )
    sq_hi = squares.astype(BF)
    sq_lo = (squares - sq_hi.astype(F32)).astype(BF)
    tail = jnp.pad(jnp.stack([sq_hi, sq_lo], axis=1), ((0, 0), (0, 126)))
    sent = jnp.concatenate([up.astype(BF), tail], axis=1).reshape(8, 16, 4096 + 128)
    got = lax.all_to_all(sent, ("z", "xh"), 0, 0, tiled=True)
    total = jnp.sum(got.astype(F32), axis=0)
    row_sq = total[:, 4096] + total[:, 4097]
    verifier_up = total[:, :4096] * lax.rsqrt(row_sq / D + eps)[:, None]
    scores16 = jnp.sum(jax.nn.silu(verifier_up) * head_weight.astype(F32)[None, :], axis=1)

    pair = (local_prompt * CLUSTERS + cluster_ids).astype(F32)
    pair16 = lax.dynamic_slice_in_dim(pair, t * 16, 16, 0)
    mine = jnp.concatenate([scores16, pair16, jnp.zeros((96,), F32)])
    everyone = lax.all_to_all(jnp.broadcast_to(mine[None, :], (128, 128)), AXES, 0, 0, tiled=True)
    table = everyone.reshape(8, 2, 8, 128)
    all_scores = table[..., :16].transpose(2, 1, 0, 3).reshape(16, 128)
    all_pairs = table[..., 16:32].reshape(16, 128)
    hot = all_pairs[:, :, None] == jnp.arange(32, dtype=F32)[None, None, :]
    votes = jnp.sum(jnp.where(hot, all_scores[:, :, None], 0.0), axis=1)
    scores = lax.dynamic_slice_in_dim(all_scores.reshape(8, 256), t, 1, 0).reshape(256)
    return hidden, scores, votes.reshape(32, CLUSTERS)


def solution(mesh):
    fine = Mesh(mesh.devices.reshape(4, 2, 2, 2, 2, 2), AXES)
    placed = (
        P(DP, TP),
        P(DP, TP),
        P(DP, TP),
        P(DP, TP, None, None),
        P(DP, TP, None, None),
        P(DP),
        P(DP, TP, None, None),
        P(DP, TP, None, None),
        P(DP),
        P(DP),
        P(TP, DP),
        P(TP, DP),
        P(DP),
        P(DP, None),
        P(),
    )
    return jax.shard_map(
        body,
        mesh=fine,
        in_specs=placed,
        out_specs=(P(TP, DP), P(TP), P()),
        check_vma=False,
    )
```

time: 402 us -> 152 us (0.38)
  waiting for transfers between devices: 220 us -> 59.9 us
  blocking collectives: 112 us -> 0 us
  starting transfers between devices: 0.3 us -> 33.6 us
  between operations: 13.9 us -> 0.97 us
  matrix products: 36.6 us -> 30.2 us
  Pallas kernels: 0 us -> 5.04 us
    psum x1 -> x0, waiting for transfers between devices: 110 us -> none  [body(): summed_up = lax.psum(partial_up, 'dp')]
    psum x2 -> x0, blocking collectives: 71 us -> none  [the longest x1 37.7 us: body(): squares = lax.psum(jnp.sum(widened * widened, axis=1), 'dp')]
    all_gather x1 -> x0, waiting for transfers between devices: 59.3 us -> none  [body(): lax.all_gather(attended, 'dp', axis=0, tiled=True)]
    reduce_scatter x1 -> x0, waiting for transfers between devices: 50.2 us -> none  [body(): lax.psum_scatter(head_terms, 'tensor', scatter_dimension=0, tiled=True)]
    all_gather x2 -> x0, blocking collectives: 41.2 us -> none  [the longest x1 22.4 us: body(): lax.all_gather(cluster_ids, 'dp', axis=0, tiled=True)]
    all_to_all x0 -> x3, waiting for transfers between devices: none -> 37.2 us  [the longest x1 16.6 us: body(): got = lax.all_to_all(sent, ('z', 'xh'), 0, 0, tiled=True)]
    ppermute x0 -> x12, waiting for transfers between devices: none -> 22.7 us  [the longest x4 17 us: shift(): return lax.ppermute(x, 'z', [(i, (i + by) % 4) for i in range(4)])]
    all_to_all x0 -> x3, starting transfers between devices: none -> 19.1 us  [the longest x1 9.89 us: body(): got = lax.all_to_all(sent, ('z', 'xh'), 0, 0, tiled=True)]
  transfers between devices with their start and end apart: 3 -> 15, of which waited for: 3 -> 7; matrix products, arithmetic and copies ran while one was open for 0% -> 30% of each run, Pallas kernels for 0% -> 3%
where the time goes in v1:
time: 152 us; the launch traced here: 151 us
  waiting for transfers between devices  59.9 us (39%)
  starting transfers between devices  33.6 us (22%)
  matrix products  30.2 us (20%)
  other arithmetic  14.9 us (10%)
  local copies, waits for them, and re-layouts  6.24 us (4%)
  Pallas kernels  5.04 us (3%)
    ppermute x4, waiting for transfers between devices, shift(): return lax.ppermute(x, 'z', [(i, (i + by) % 4) for i in range(4)])  17 us
    all_to_all x1, waiting for transfers between devices, body(): got = lax.all_to_all(sent, ('z', 'xh'), 0, 0, tiled=True)  16.6 us
    all_to_all x1, waiting for transfers between devices, body(): parts = lax.all_to_all(partial, ('xl', 'yh'), 0, 0, tiled=True)  12 us
    all_to_all x1, starting transfers between devices, body(): got = lax.all_to_all(sent, ('z', 'xh'), 0, 0, tiled=True)  9.89 us
    reduce_sum x1, other arithmetic, attend(): jnp.sum(pre_exp, axis=(3, 4)) + jnp.sum(gen_exp, axis=3) + own_exp  9.02 us
    dot_general x1, matrix products, attend(): jnp.einsum('rkgpj,pkjd->rkgd', pre_w, prefix_values, preferred_element_ty...  8.99 us
    all_to_all x1, waiting for transfers between devices, body(): lax.all_to_all(jnp.broadcast_to(mine[None, :], (128, 128)), AXES, 0, 0, t...  8.54 us
    ppermute x4, starting transfers between devices, shift(): return lax.ppermute(x, 'z', [(i, (i + by) % 4) for i in range(4)])  7.72 us
  transfers between devices with their start and end apart: 15, of which 7 were waited for; matrix products, arithmetic and copies ran while one was open for 30% of the time, Pallas kernels for 3%

profile of v1, /device:TPU:0, one launch (start us, length us, event | category | flops | bytes accessed | tf_op | source)
XLA Modules:
  0.0 150.9 jit_solution(2334899999435781219)
XLA Ops:
  0.6 0.0 copy-start
  0.7 1.7 %collective-permute-start.7 = (bf16[1024,512]{1,0:T(8,128)(2,1)}, bf16[1024,512]{1,0:T(8,128)(2,1)S(1)}, u32[]{:S(2)}, u32[]{:S(2)}) collective-permute-start(bf16[1024,512]{1,0:T(8,128)(2,1)} %w00.1), channel_id=1, source_target_pairs={{0,1},{1,0},{2,3},{3,2},{4,5},{5,4},{6,7},{7,6},{8,9},{9,8},{10,11... | collective-permute-start | bytes 3145736 | tf_op jit(solution)/shard_map/ppermute | solution.py:81
  2.4 0.7 add_convert_fusion
  3.1 1.0 copy.115
  4.1 0.7 iota_compare_fusion.2
  4.8 4.5 %fusion.60 = (f32[128,8]{1,0:T(8,128)S(1)}, f32[128,8,128]{2,1,0:T(8,128)S(1)}) fusion(bf16[128,8,128]{2,1,0:T(8,128)(2,1)S(1)} %bitcast.129, bf16[128,1,128,128]{3,2,1,0:T(8,128)(2,1)} %param.18, pred[128,128]{1,0:T(8,128)(4,1)S(1)} %iota_compare_fusion.2), kind=kOutput, calls=%fused_computation.87 | convolution fusion | flops 33946624 | bytes 5001216 | tf_op jit(solution)/shard_map/rkgd,rkjd->rkgj/dot_general | solution.py:48
  9.4 0.1 copy.93
  9.4 0.3 fusion.47
  9.8 7.0 %fusion.1 = (f32[128,8]{0,1:T(8,128)S(1)}, f32[2,2048,128,8]{2,1,3,0:T(8,128)}) fusion(pred[128,2]{0,1:T(4,128)(4,1)S(1)} %iota_compare_fusion.3, bf16[2,1,2048,128]{3,2,1,0:T(8,128)(2,1)S(1)} %copy-done, bf16[128,1024]{1,0:T(8,128)(2,1)S(1)} %copy-done.2), kind=kOutput, calls=%fused_computation.4 | convolution fusion | flops 1086323712 | bytes 18092288 | tf_op jit(solution)/shard_map/rkgd,pkjd->rkgpj/dot_general | solution.py:41
  16.8 0.1 copy.94
  16.9 9.0 %fusion = f32[128,8]{0,1:T(8,128)S(1)} fusion(f32[2,2048,128,8]{2,1,3,0:T(8,128)} %get-tuple-element.36, f32[128,8]{0,1:T(8,128)S(1)} %maximum_maximum_fusion, pred[128,2]{0,1:T(4,128)(4,1)S(1)} %iota_compare_fusion.3), kind=kLoop, calls=%fused_computation.3 | loop fusion | flops 16776192 | bytes 16785664 | tf_op jit(solution)/shard_map/reduce_sum | solution.py:65
  26.0 0.0 copy-start.4
  26.0 0.4 fusion.32
  26.4 0.1 copy.98
  26.5 3.4 %fusion.5 = f32[128,8,128]{2,1,0:T(8,128)S(1)} fusion(bf16[128,1,128,128]{3,2,1,0:T(8,128)(2,1)} %param.19, f32[128,8,128]{2,1,0:T(8,128)S(1)} %get-tuple-element.38, f32[128,8]{1,0:T(8,128)S(1)} %copy.98, f32[128,8]{1,0:T(8,128)S(1)} %copy.94), kind=kOutput, calls=%fused_computation.9 | convolution fusion | flops 33947648 | bytes 5251072 | tf_op jit(solution)/shard_map/rkgj,rkjd->rkgd/dot_general | solution.py:73
  30.0 1.1 copy.99
  31.0 0.1 copy.100
  31.1 9.0 %fusion.25 = bf16[128,1,8,128]{0,3,2,1:T(8,128)(2,1)} fusion(f32[128,8]{0,1:T(8,128)S(1)} %get-tuple-element.28, f32[128,8]{0,1:T(8,128)S(1)} %maximum_maximum_fusion, f32[2,2048,128,8]{2,1,3,0:T(8,128)} %get-tuple-element.36, pred[128,2]{0,1:T(4,128)(4,1)S(1)} %iota_compare_fusion.3, bf16[2,1,2048,128]{3,2,1,0:T(8,128)(2,1)} %param.22, ...), kind=kOutput, calls=%fused_computation.22 | convolution fusion | flops 1095237632 | bytes 18690304 | tf_op jit(solution)/shard_map/rkgpj,pkjd->rkgd/dot_general | solution.py:70
  40.1 1.1 copy.113
  41.2 3.1 %collective-permute-start = (bf16[128,1024]{1,0:T(8,128)(2,1)S(1)}, bf16[128,1024]{1,0:T(8,128)(2,1)}, u32[]{:S(2)}, u32[]{:S(2)}) collective-permute-start(bf16[128,1024]{1,0:T(8,128)(2,1)S(1)} %copy.113), channel_id=1, source_target_pairs={{0,16},{17,1},{1,0},{16,17},{2,18},{19,3},{3,2},{18,19},{4,20},{21... | collective-permute-start | bytes 786440 | tf_op jit(solution)/shard_map/ppermute | solution.py:185
  44.3 1.4 collective-permute-start.1
  45.7 0.2 collective-permute-start.6
  45.9 0.3 collective-permute-start.8
  46.2 4.3 %collective-permute-done = bf16[128,1024]{1,0:T(8,128)(2,1)} collective-permute-done((bf16[128,1024]{1,0:T(8,128)(2,1)S(1)}, bf16[128,1024]{1,0:T(8,128)(2,1)}, u32[]{:S(2)}, u32[]{:S(2)}) %collective-permute-start) | collective-permute-done | bytes 262176 | tf_op jit(solution)/shard_map/ppermute | solution.py:185
  50.6 1.0 broadcast_select_fusion.1
  51.6 2.2 %collective-permute-start.2 = (bf16[128,2048]{1,0:T(8,128)(2,1)S(1)}, bf16[128,2048]{1,0:T(8,128)(2,1)S(1)}, u32[]{:S(2)}, u32[]{:S(2)}) collective-permute-start(bf16[128,2048]{1,0:T(8,128)(2,1)S(1)} %pad_maximum_fusion.here), channel_id=1, source_target_pairs={{0,32},{32,64},{64,96},{96,0},{1,33},{33,65},{65,97},{97,1},{2,34}... | collective-permute-start | bytes 1572872 | tf_op jit(solution)/shard_map/ppermute | solution.py:85
  53.8 2.2 %collective-permute-start.3 = (bf16[128,2048]{1,0:T(8,128)(2,1)S(1)}, bf16[128,2048]{1,0:T(8,128)(2,1)S(1)}, u32[]{:S(2)}, u32[]{:S(2)}) collective-permute-start(bf16[128,2048]{1,0:T(8,128)(2,1)S(1)} %pad_maximum_fusion.here), channel_id=1, source_target_pairs={{0,96},{32,0},{64,32},{96,64},{1,97},{33,1},{65,33},{97,65},{2,98}... | collective-permute-start | bytes 1572872 | tf_op jit(solution)/shard_map/ppermute | solution.py:85
  56.0 11.7 %collective-permute-done.2.before = bf16[128,2048]{1,0:T(8,128)(2,1)S(1)} collective-permute-done((bf16[128,2048]{1,0:T(8,128)(2,1)S(1)}, bf16[128,2048]{1,0:T(8,128)(2,1)S(1)}, u32[]{:S(2)}, u32[]{:S(2)}) %collective-permute-start.2) | collective-permute-done | bytes 524320 | tf_op jit(solution)/shard_map/ppermute | solution.py:85
  67.7 0.1 collective-permute-start.4
  67.9 3.3 %collective-permute-start.5 = (bf16[64,2048]{1,0:T(8,128)(2,1)S(1)}, bf16[64,2048]{1,0:T(8,128)(2,1)S(1)}, u32[]{:S(2)}, u32[]{:S(2)}) collective-permute-start(bf16[64,2048]{1,0:T(8,128)(2,1)S(1)} %slice.45), channel_id=1, source_target_pairs={{0,96},{32,0},{64,32},{96,64},{1,97},{33,1},{65,33},{97,65},{2,98}... | collective-permute-start | bytes 786440 | tf_op jit(solution)/shard_map/ppermute | solution.py:85
  71.1 5.3 %collective-permute-done.4.far_a = bf16[64,2048]{1,0:T(8,128)(2,1)S(1)} collective-permute-done((bf16[64,2048]{1,0:T(8,128)(2,1)S(1)}, bf16[64,2048]{1,0:T(8,128)(2,1)S(1)}, u32[]{:S(2)}, u32[]{:S(2)}) %collective-permute-start.4) | collective-permute-done | bytes 262176 | tf_op jit(solution)/shard_map/ppermute | solution.py:85
  76.4 0.0 copy-start.3
  76.4 5.0 %shard_map.166 = bf16[4,128,1024]{2,1,0:T(8,128)(2,1)} custom-call(s32[1]{0:T(128)} %bitcast.z_ref, bf16[128,2048]{1,0:T(8,128)(2,1)S(1)} %pad_maximum_fusion.here, bf16[128,2048]{1,0:T(8,128)(2,1)S(1)} %collective-permute-done.2.before, bf16[128,2048]{1,0:T(8,128)(2,1)S(1)} %collective-permute-done.3.after, ...), custom_call_target="tpu_custom_call" | custom-call | flops 2147483648 | bytes 7340032 | tf_op jit(solution)/shard_map/pallas_call | solution.py:121
  81.5 4.7 %all-to-all-start = ((bf16[4,128,1024]{2,1,0:T(8,128)(2,1)}), bf16[4,128,1024]{2,1,0:T(8,128)(2,1)S(1)}, u32[]{:S(2)}, u32[]{:S(2)}) async-start(bf16[4,128,1024]{2,1,0:T(8,128)(2,1)} %shard_map.166), calls=%async_computation | async-start | bytes 2097152 | tf_op jit(solution)/shard_map/all_to_all | solution.py:196
  86.2 0.1 collective-permute-start.9
  86.3 1.3 collective-permute-done.9
  87.6 12.0 %all-to-all-done = bf16[4,128,1024]{2,1,0:T(8,128)(2,1)S(1)} async-done(((bf16[4,128,1024]{2,1,0:T(8,128)(2,1)}), bf16[4,128,1024]{2,1,0:T(8,128)(2,1)S(1)}, u32[]{:S(2)}, u32[]{:S(2)}) %all-to-all-start) | async-done | bytes 1048608 | tf_op jit(solution)/shard_map/all_to_all | solution.py:196
  99.6 0.2 convert_reduce_fusion.1
  99.8 0.2 fusion.34
  100.0 0.1 copy.102
  100.2 2.9 %fusion.43 = f32[128,4096]{1,0:T(8,128)S(1)} fusion(bf16[512,4096]{1,0:T(8,128)(2,1)} %param.28, bf16[128,512]{1,0:T(8,128)(2,1)S(1)} %get-tuple-element.24, f32[512]{0:T(512)S(1)} %convert_element_type.118), kind=kOutput, calls=%fused_computation.55 | convolution fusion | flops 537067520 | bytes 6424576 | tf_op jit(solution)/shard_map/dot_general | solution.py:211
  103.1 0.0 copy-start.5
  103.1 3.0 %fusion.4 = bf16[128,4096]{1,0:T(8,128)(2,1)S(1)} fusion(f32[128,4096]{1,0:T(8,128)S(1)} %fusion.43, bf16[512,4096]{1,0:T(8,128)(2,1)} %collective-permute-done.11, bf16[128,512]{1,0:T(8,128)(2,1)S(1)} %get-tuple-element.30, f32[512]{0:T(512)S(1)} %bitcast.133), kind=kOutput, calls=%fused_computation.8 | convolution fusion | flops 538116096 | bytes 7473152 | tf_op jit(solution)/shard_map/dot_general | solution.py:211
  106.1 1.1 fusion.28
  107.2 9.9 %all-to-all-start.1 = ((bf16[8,16,4224]{2,1,0:T(8,128)(2,1)}), bf16[8,16,4224]{2,1,0:T(8,128)(2,1)S(1)}, u32[]{:S(2)}, u32[]{:S(2)}) async-start(bf16[8,16,4224]{2,1,0:T(8,128)(2,1)} %bitcast.22), calls=%async_computation.1 | async-start | bytes 2162688 | tf_op jit(solution)/shard_map/all_to_all | solution.py:218
  117.1 0.1 dynamic_slice.14
  117.2 0.0 collective-permute-start.10
  117.2 16.6 %all-to-all-done.1 = bf16[8,16,4224]{2,1,0:T(8,128)(2,1)S(1)} async-done(((bf16[8,16,4224]{2,1,0:T(8,128)(2,1)}), bf16[8,16,4224]{2,1,0:T(8,128)(2,1)S(1)}, u32[]{:S(2)}, u32[]{:S(2)}) %all-to-all-start.1) | async-done | bytes 1081376 | tf_op jit(solution)/shard_map/all_to_all | solution.py:218
  133.8 0.1 convert_reduce_fusion
  134.0 0.2 fusion.52
  134.2 0.3 multiply_reduce_fusion
  134.4 0.1 pad_maximum_fusion.3
  134.5 0.7 broadcast_in_dim.76
  135.2 4.5 %all-to-all-start.2 = ((f32[128,1,128]{2,1,0:T(1,128)}), f32[128,1,128]{2,1,0:T(1,128)S(1)}, u32[]{:S(2)}, u32[]{:S(2)}) async-start(f32[128,1,128]{2,1,0:T(1,128)} %broadcast_in_dim.76), calls=%async_computation.2 | async-start | bytes 131072 | tf_op jit(solution)/shard_map/all_to_all | solution.py:227
  139.7 0.8 maximum_select_fusion
  140.5 8.5 %all-to-all-done.2 = f32[128,1,128]{2,1,0:T(1,128)S(1)} async-done(((f32[128,1,128]{2,1,0:T(1,128)}), f32[128,1,128]{2,1,0:T(1,128)S(1)}, u32[]{:S(2)}, u32[]{:S(2)}) %all-to-all-start.2) | async-done | bytes 65568 | tf_op jit(solution)/shard_map/all_to_all | solution.py:227
  149.0 0.1 fusion.59
  149.1 0.1 broadcast_in_dim.77
  149.2 0.1 reshape_reshape.3
  149.3 0.1 eq.43
  149.4 0.2 select_reduce_fusion
  149.5 0.1 reshape.212
  149.6 0.7 copy.105
  150.3 0.6 constant_dynamic-slice_fusion
  (40 shorter events, 0.3 us)
Async XLA Ops:
  0.6 9.2 %copy-start = (bf16[2,1,2048,128]{3,2,1,0:T(8,128)(2,1)S(1)}, bf16[2,1,2048,128]{3,2,1,0:T(8,128)(2,1)}, u32[]{:S(2)}) copy-start(bf16[2,1,2048,128]{3,2,1,0:T(8,128)(2,1)} %param.21) | copy-start | bytes 3145732
  0.6 9.2 %copy-start.2 = (bf16[128,1024]{1,0:T(8,128)(2,1)S(1)}, bf16[128,1024]{1,0:T(8,128)(2,1)}, u32[]{:S(2)}) copy-start(bf16[128,1024]{1,0:T(8,128)(2,1)} %param.15) | copy-start | bytes 786436
  0.7 8.8 %copy-start.7 = (bf16[128,128]{1,0:T(8,128)(2,1)S(1)}, bf16[128,128]{1,0:T(8,128)(2,1)}, u32[]{:S(2)}) copy-start(bf16[128,128]{1,0:T(8,128)(2,1)} %param.16) | copy-start | bytes 98308
  0.7 45.3 %collective-permute-start.7 = (bf16[1024,512]{1,0:T(8,128)(2,1)}, bf16[1024,512]{1,0:T(8,128)(2,1)S(1)}, u32[]{:S(2)}, u32[]{:S(2)}) collective-permute-start(bf16[1024,512]{1,0:T(8,128)(2,1)} %w00.1), channel_id=1, source_target_pairs={{0,1},{1,0},{2,3},{3,2},{4,5},{5,4},{6,7},{7,6},{8,9},{9,8},{10,11... | collective-permute-start | bytes 3145736 | tf_op jit(solution)/shard_map/ppermute | solution.py:81
  2.4 100.7 %collective-permute-start.11 = (bf16[512,4096]{1,0:T(8,128)(2,1)}, bf16[512,4096]{1,0:T(8,128)(2,1)}, u32[]{:S(2)}, u32[]{:S(2)}) collective-permute-start(bf16[512,4096]{1,0:T(8,128)(2,1)} %param.28), channel_id=1, source_target_pairs={{0,8},{8,0},{1,9},{9,1},{2,10},{10,2},{3,11},{11,3},{4,12},{12,4},... | collective-permute-start | bytes 12582920 | tf_op jit(solution)/shard_map/ppermute | solution.py:81
  26.0 5.1 %copy-start.4 = (bf16[128,128]{1,0:T(8,128)(2,1)S(1)}, bf16[128,128]{1,0:T(8,128)(2,1)}, u32[]{:S(2)}) copy-start(bf16[128,128]{1,0:T(8,128)(2,1)} %param.17) | copy-start | bytes 98308
  31.1 14.6 %copy-start.1 = (bf16[1024,512]{1,0:T(8,128)(2,1)S(1)}, bf16[1024,512]{1,0:T(8,128)(2,1)}, u32[]{:S(2)}) copy-start(bf16[1024,512]{1,0:T(8,128)(2,1)} %w00.1) | copy-start | bytes 3145732
  41.2 9.3 %collective-permute-start = (bf16[128,1024]{1,0:T(8,128)(2,1)S(1)}, bf16[128,1024]{1,0:T(8,128)(2,1)}, u32[]{:S(2)}, u32[]{:S(2)}) collective-permute-start(bf16[128,1024]{1,0:T(8,128)(2,1)S(1)} %copy.113), channel_id=1, source_target_pairs={{0,16},{17,1},{1,0},{16,17},{2,18},{19,3},{3,2},{18,19},{4,20},{21... | collective-permute-start | bytes 786440 | tf_op jit(solution)/shard_map/ppermute | solution.py:185
  44.3 6.2 %collective-permute-start.1 = (bf16[128,1024]{1,0:T(8,128)(2,1)S(1)}, bf16[128,1024]{1,0:T(8,128)(2,1)}, u32[]{:S(2)}, u32[]{:S(2)}) collective-permute-start(bf16[128,1024]{1,0:T(8,128)(2,1)S(1)} %copy.113), channel_id=1, source_target_pairs={{1,16},{16,1},{3,18},{18,3},{5,20},{20,5},{7,22},{22,7},{9,24},{24... | collective-permute-start | bytes 786440 | tf_op jit(solution)/shard_map/ppermute | solution.py:186
  45.7 30.7 %collective-permute-start.6 = (bf16[1024,512]{1,0:T(8,128)(2,1)S(1)}, bf16[1024,512]{1,0:T(8,128)(2,1)}, u32[]{:S(2)}, u32[]{:S(2)}) collective-permute-start(bf16[1024,512]{1,0:T(8,128)(2,1)S(1)} %copy-done.1), channel_id=1, source_target_pairs={{0,8},{8,0},{1,9},{9,1},{2,10},{10,2},{3,11},{11,3},{4,12},{12,4},... | collective-permute-start | bytes 3145736 | tf_op jit(solution)/shard_map/ppermute | solution.py:81
  45.9 30.5 %collective-permute-start.8 = (bf16[1024,512]{1,0:T(8,128)(2,1)S(1)}, bf16[1024,512]{1,0:T(8,128)(2,1)S(1)}, u32[]{:S(2)}, u32[]{:S(2)}) collective-permute-start(bf16[1024,512]{1,0:T(8,128)(2,1)S(1)} %collective-permute-done.7.w10), channel_id=1, source_target_pairs={{0,8},{8,0},{1,9},{9,1},{2,10},{10,2},{3,11},{11,3},{4,12},{12,4},... | collective-permute-start | bytes 3145736 | tf_op jit(solution)/shard_map/ppermute | solution.py:81
  51.6 16.1 %collective-permute-start.2 = (bf16[128,2048]{1,0:T(8,128)(2,1)S(1)}, bf16[128,2048]{1,0:T(8,128)(2,1)S(1)}, u32[]{:S(2)}, u32[]{:S(2)}) collective-permute-start(bf16[128,2048]{1,0:T(8,128)(2,1)S(1)} %pad_maximum_fusion.here), channel_id=1, source_target_pairs={{0,32},{32,64},{64,96},{96,0},{1,33},{33,65},{65,97},{97,1},{2,34}... | collective-permute-start | bytes 1572872 | tf_op jit(solution)/shard_map/ppermute | solution.py:85
  53.8 14.1 %collective-permute-start.3 = (bf16[128,2048]{1,0:T(8,128)(2,1)S(1)}, bf16[128,2048]{1,0:T(8,128)(2,1)S(1)}, u32[]{:S(2)}, u32[]{:S(2)}) collective-permute-start(bf16[128,2048]{1,0:T(8,128)(2,1)S(1)} %pad_maximum_fusion.here), channel_id=1, source_target_pairs={{0,96},{32,0},{64,32},{96,64},{1,97},{33,1},{65,33},{97,65},{2,98}... | collective-permute-start | bytes 1572872 | tf_op jit(solution)/shard_map/ppermute | solution.py:85
  67.7 8.7 %collective-permute-start.4 = (bf16[64,2048]{1,0:T(8,128)(2,1)S(1)}, bf16[64,2048]{1,0:T(8,128)(2,1)S(1)}, u32[]{:S(2)}, u32[]{:S(2)}) collective-permute-start(bf16[64,2048]{1,0:T(8,128)(2,1)S(1)} %slice.44), channel_id=1, source_target_pairs={{0,32},{32,64},{64,96},{96,0},{1,33},{33,65},{65,97},{97,1},{2,34}... | collective-permute-start | bytes 786440 | tf_op jit(solution)/shard_map/ppermute | solution.py:85
  67.9 8.5 %collective-permute-start.5 = (bf16[64,2048]{1,0:T(8,128)(2,1)S(1)}, bf16[64,2048]{1,0:T(8,128)(2,1)S(1)}, u32[]{:S(2)}, u32[]{:S(2)}) collective-permute-start(bf16[64,2048]{1,0:T(8,128)(2,1)S(1)} %slice.45), channel_id=1, source_target_pairs={{0,96},{32,0},{64,32},{96,64},{1,97},{33,1},{65,33},{97,65},{2,98}... | collective-permute-start | bytes 786440 | tf_op jit(solution)/shard_map/ppermute | solution.py:85
  76.4 9.7 %copy-start.3 = (bf16[256,512]{1,0:T(8,128)(2,1)S(1)}, bf16[256,512]{1,0:T(8,128)(2,1)}, u32[]{:S(2)}) copy-start(bf16[256,512]{1,0:T(8,128)(2,1)} %param.26) | copy-start | bytes 786436
  76.4 9.7 %copy-start.6 = (bf16[512]{0:T(512)(128)(2,1)S(1)}, bf16[512]{0:T(512)(128)(2,1)}, u32[]{:S(2)}) copy-start(bf16[512]{0:T(512)(128)(2,1)} %param.27) | copy-start | bytes 3076
  81.5 18.2 %all-to-all-start = ((bf16[4,128,1024]{2,1,0:T(8,128)(2,1)}), bf16[4,128,1024]{2,1,0:T(8,128)(2,1)S(1)}, u32[]{:S(2)}, u32[]{:S(2)}) async-start(bf16[4,128,1024]{2,1,0:T(8,128)(2,1)} %shard_map.166), calls=%async_computation | async-start | bytes 2097152 | tf_op jit(solution)/shard_map/all_to_all | solution.py:196
  86.2 1.5 collective-permute-start.9
  103.1 14.0 %copy-start.5 = (bf16[4096]{0:T(1024)(128)(2,1)S(1)}, bf16[4096]{0:T(1024)(128)(2,1)}, u32[]{:S(2)}) copy-start(bf16[4096]{0:T(1024)(128)(2,1)} %param.29) | copy-start | bytes 24580
  107.2 26.7 %all-to-all-start.1 = ((bf16[8,16,4224]{2,1,0:T(8,128)(2,1)}), bf16[8,16,4224]{2,1,0:T(8,128)(2,1)S(1)}, u32[]{:S(2)}, u32[]{:S(2)}) async-start(bf16[8,16,4224]{2,1,0:T(8,128)(2,1)} %bitcast.22), calls=%async_computation.1 | async-start | bytes 2162688 | tf_op jit(solution)/shard_map/all_to_all | solution.py:218
  117.2 22.6 %collective-permute-start.10 = (bf16[128,512]{1,0:T(8,128)(2,1)S(1)}, bf16[128,512]{1,0:T(8,128)(2,1)S(1)}, u32[]{:S(2)}, u32[]{:S(2)}) collective-permute-start(bf16[128,512]{1,0:T(8,128)(2,1)S(1)} %get-tuple-element.30), channel_id=1, source_target_pairs={{0,8},{8,0},{1,9},{9,1},{2,10},{10,2},{3,11},{11,3},{4,12},{12,4},... | collective-permute-start | bytes 393224 | tf_op jit(solution)/shard_map/ppermute | solution.py:81
  135.2 13.8 %all-to-all-start.2 = ((f32[128,1,128]{2,1,0:T(1,128)}), f32[128,1,128]{2,1,0:T(1,128)S(1)}, u32[]{:S(2)}, u32[]{:S(2)}) async-start(f32[128,1,128]{2,1,0:T(1,128)} %broadcast_in_dim.76), calls=%async_computation.2 | async-start | bytes 131072 | tf_op jit(solution)/shard_map/all_to_all | solution.py:227

commit v2 on v1

--- a/solution.py
+++ b/solution.py
@@ -1,3 +1,4 @@
+import functools
 import math
 
 import jax
@@ -16,65 +17,164 @@
 TP = ("xl", "yh", "yl")
 BF = jnp.bfloat16
 F32 = jnp.float32
-
-
-def attend(
-    queries,
-    new_key,
-    new_value,
-    cache_keys,
-    cache_values,
-    lengths,
-    prefix_keys,
-    prefix_values,
-    local_prompt,
-):
-    rows_blk = queries.shape[0]
-    kv_heads = cache_keys.shape[1]
-    head_dim = cache_keys.shape[3]
-    groups = queries.shape[1] // (kv_heads * head_dim)
-    prompts_blk = prefix_keys.shape[0]
-    gen_len = cache_keys.shape[2]
-    score_scale = 1.0 / math.sqrt(head_dim)
-    grouped = queries.reshape(rows_blk, kv_heads, groups, head_dim)
-    pre_scores = (
-        jnp.einsum("rkgd,pkjd->rkgpj", grouped, prefix_keys, preferred_element_type=jnp.float32)
-        * score_scale
-    )
-    pre_ok = (local_prompt[:, None] == jnp.arange(prompts_blk, dtype=jnp.int32)[None, :])[
-        :, None, None, :, None
-    ]
-    gen_scores = (
-        jnp.einsum("rkgd,rkjd->rkgj", grouped, cache_keys, preferred_element_type=jnp.float32)
-        * score_scale
-    )
-    gen_ok = (jnp.arange(gen_len, dtype=jnp.int32)[None, :] < lengths[:, None])[:, None, None, :]
-    own_key = new_key.reshape(rows_blk, kv_heads, head_dim)
-    own_scores = (
-        jnp.einsum("rkgd,rkd->rkg", grouped, own_key, preferred_element_type=jnp.float32)
-        * score_scale
-    )
-    pre_scores = jnp.where(pre_ok, pre_scores, -1e30)
-    gen_scores = jnp.where(gen_ok, gen_scores, -1e30)
-    row_top = jnp.maximum(
-        jnp.maximum(jnp.max(pre_scores, axis=(3, 4)), jnp.max(gen_scores, axis=3)), own_scores
-    )
-    pre_exp = jnp.exp(pre_scores - row_top[..., None, None])
-    gen_exp = jnp.exp(gen_scores - row_top[..., None])
-    own_exp = jnp.exp(own_scores - row_top)
-    denominator = jnp.sum(pre_exp, axis=(3, 4)) + jnp.sum(gen_exp, axis=3) + own_exp
-    pre_w = (pre_exp / denominator[..., None, None]).astype(jnp.bfloat16)
-    gen_w = (gen_exp / denominator[..., None]).astype(jnp.bfloat16)
-    own_w = (own_exp / denominator).astype(jnp.bfloat16)
-    own_val = new_value.reshape(rows_blk, kv_heads, head_dim).astype(jnp.float32)
-    result = jnp.einsum(
-        "rkgpj,pkjd->rkgd", pre_w, prefix_values, preferred_element_type=jnp.float32
-    )
-    result = result + jnp.einsum(
-        "rkgj,rkjd->rkgd", gen_w, cache_values, preferred_element_type=jnp.float32
-    )
-    result = result + own_w.astype(jnp.float32)[..., None] * own_val[:, :, None, :]
-    return result.reshape(rows_blk, kv_heads * groups * head_dim).astype(jnp.bfloat16)
+SCALE2 = math.log2(math.e) / math.sqrt(128)
+NEG = -1e30
+NT = (((1,), (1,)), ((), ()))
+
+
+def attn_kernel(rows, tile, ids_hbm, ids2_hbm, lens_hbm, q_hbm, nk_hbm, nv_hbm, pk_hbm, pv_hbm, ck_hbm, cv_hbm,
+                out_ref, ids_s, ids_v, lens_v, q_ref, nk_ref, nv_ref, pk, pv, ck, cv, qs, nks, nvs, lens, acc,
+                mbuf, lbuf, s_scr, sem_i, sem_p, sem_k, sem_v):
+    small = [pltpu.make_async_copy(h, v, sem_i.at[i]) for i, (h, v) in enumerate((
+        (ids_hbm, ids_s), (ids2_hbm, ids_v), (lens_hbm, lens_v), (q_hbm, q_ref), (nk_hbm, nk_ref), (nv_hbm, nv_ref)))]
+    for cp in small:
+        cp.start()
+    heads = q_ref.shape[1] // 128
+    tiles = rows // tile
+    ctile = 16
+    ctiles = rows // ctile
+    keys = pk.shape[1]
+    pre = [pltpu.make_async_copy(h.at[p], v.at[p], sem_p.at[p, i])
+           for p in range(2) for i, (h, v) in enumerate(((pk_hbm, pk), (pv_hbm, pv)))]
+    for cp in pre:
+        cp.start()
+
+    small[0].wait()
+
+    def place(r, counts):
+        c0, c1 = counts
+        p = ids_s[r] & 1
+        to = jnp.where(p == 0, c0, rows - 1 - c1)
+        blk = to // ctile
+        pltpu.make_async_copy(ck_hbm.at[r], ck.at[to], sem_k.at[blk]).start()
+        pltpu.make_async_copy(cv_hbm.at[r], cv.at[to], sem_v.at[blk]).start()
+        return c0 + 1 - p, c1 + p
+
+    n0, _ = lax.fori_loop(0, rows, place, (jnp.int32(0), jnp.int32(0)), unroll=8)
+
+    for cp in small[1:]:
+        cp.wait()
+    second = (ids_v[...] & 1)
+    ones = jnp.broadcast_to(second, (rows, rows)).astype(F32).astype(BF)
+    ri = lax.broadcasted_iota(jnp.int32, (rows, rows), 0)
+    ci = lax.broadcasted_iota(jnp.int32, (rows, rows), 1)
+    upper = (ri < ci).astype(F32).astype(BF)
+    before1 = jnp.dot(ones, upper, preferred_element_type=F32)
+    pos = jnp.where(jnp.broadcast_to(second, (rows, rows)) == 0, ci.astype(F32) - before1, rows - 1 - before1)
+    perm32 = (pos == ri.astype(F32)).astype(F32)
+    perm = perm32.astype(BF)
+    unperm = perm32.T.astype(BF)
+    qs[...] = jnp.dot(perm, q_ref[...], preferred_element_type=F32).astype(BF)
+    nks[...] = jnp.dot(perm, nk_ref[...], preferred_element_type=F32)
+    nvs[...] = jnp.dot(perm, nv_ref[...], preferred_element_type=F32)
+    lb = jnp.broadcast_to(lens_v[...], (128, rows)).astype(F32).astype(BF)
+    lens[...] = lax.dot_general(perm, lb, NT, preferred_element_type=F32)
+
+    for cp in pre:
+        cp.wait()
+    edge = jnp.minimum(n0 // tile, tiles - 1)
+    chunk = 512
+
+    def prefix(item, _):
+        p = (item > edge).astype(jnp.int32)
+        row0 = pl.multiple_of((item - p) * tile, tile)
+        qt = jnp.concatenate([qs[pl.ds(row0, tile), h * 128:(h + 1) * 128] for h in range(heads)], axis=0)
+        top = None
+        for k in range(0, keys, chunk):
+            s = lax.dot_general(qt, pk[p, k:k + chunk], NT, preferred_element_type=F32)
+            s_scr[:, k:k + chunk] = s
+            for j in range(0, chunk, 128):
+                top = s[:, j:j + 128] if top is None else jnp.maximum(top, s[:, j:j + 128])
+        m = jnp.max(top, axis=1, keepdims=True)
+        mb = jnp.broadcast_to(m, (heads * tile, 128))
+        l = jnp.zeros((heads * tile, 128), F32)
+        o = jnp.zeros((heads * tile, 128), F32)
+        for k in range(0, keys, chunk):
+            ps = []
+            for j in range(0, chunk, 128):
+                e = jnp.exp2((s_scr[:, k + j:k + j + 128] - mb) * SCALE2)
+                l = l + e
+                ps.append(e.astype(BF))
+            o = o + jnp.dot(jnp.concatenate(ps, axis=1), pv[p, k:k + chunk], preferred_element_type=F32)
+        lsum = jnp.broadcast_to(jnp.sum(l, axis=1, keepdims=True), (heads * tile, 128))
+        at = row0 + lax.broadcasted_iota(jnp.int32, (tile, 128), 0)
+        mine = (at < n0) == (p == 0)
+        for h in range(heads):
+            hs = slice(h * tile, (h + 1) * tile)
+            cs = slice(h * 128, (h + 1) * 128)
+            rs = pl.ds(row0, tile)
+            acc[rs, cs] = jnp.where(mine, o[hs], acc[rs, cs])
+            mbuf[rs, cs] = jnp.where(mine, mb[hs], mbuf[rs, cs])
+            lbuf[rs, cs] = jnp.where(mine, lsum[hs], lbuf[rs, cs])
+        return 0
+
+    lax.fori_loop(0, tiles + 1, prefix, 0)
+
+    mrow = lax.broadcasted_iota(jnp.int32, (heads * ctile, 128), 0) % ctile
+    lane = lax.broadcasted_iota(jnp.int32, (heads * ctile, 128), 1).astype(F32)
+
+    def cached(b, _):
+        r0 = pl.multiple_of(b * ctile, ctile)
+        rs = pl.ds(r0, ctile)
+        pltpu.make_async_copy(ck_hbm.at[pl.ds(0, ctile)], ck.at[rs], sem_k.at[b]).wait()
+        pltpu.make_async_copy(cv_hbm.at[pl.ds(0, ctile)], cv.at[rs], sem_v.at[b]).wait()
+        heads_of = lambda ref: jnp.concatenate([ref[rs, h * 128:(h + 1) * 128] for h in range(heads)], axis=0)
+        rep = lambda x: jnp.concatenate([x] * heads, axis=0)
+        qt = heads_of(qs)
+        kt = ck[rs].reshape(ctile * 128, 128)
+        vt = cv[rs].reshape(ctile * 128, 128)
+        s = lax.dot_general(qt, kt, NT, preferred_element_type=F32)
+        sc = s[:, :128]
+        for r in range(1, ctile):
+            sc = jnp.where(mrow == r, s[:, r * 128:(r + 1) * 128], sc)
+        sc = jnp.where(lane < rep(lens[rs]), sc, NEG)
+        so = jnp.sum(qt.astype(F32) * rep(nks[rs]), axis=1, keepdims=True)
+        mp = heads_of(mbuf)
+        m = jnp.maximum(jnp.maximum(mp, jnp.max(sc, axis=1, keepdims=True)), so)
+        ap = jnp.exp2((mp - m) * SCALE2)
+        e = jnp.exp2((sc - m) * SCALE2)
+        eo = jnp.exp2((so - m) * SCALE2)
+        eb = e.astype(BF).astype(F32)
+        pe = jnp.concatenate([jnp.where(mrow == r, eb, 0.0).astype(BF) for r in range(ctile)], axis=1)
+        oc = jnp.dot(pe, vt, preferred_element_type=F32)
+        l = ap * heads_of(lbuf) + jnp.sum(e, axis=1, keepdims=True) + eo
+        o = (ap * heads_of(acc) + oc + eo * rep(nvs[rs])) / l
+        for h in range(heads):
+            qs[rs, h * 128:(h + 1) * 128] = o[h * ctile:(h + 1) * ctile].astype(BF)
+        return 0
+
+    lax.fori_loop(0, ctiles, cached, 0)
+    out_ref[...] = jnp.dot(unperm, qs[...], preferred_element_type=F32).astype(BF)
+
+
+def attend(queries, new_key, new_value, ck, cv, lengths, pk, pv, prompt_ids, tile=32):
+    rows = queries.shape[0]
+    width = queries.shape[1]
+    keys = pk.shape[2]
+    heads = width // 128
+    V = pl.BlockSpec(memory_space=pltpu.VMEM)
+    A = pl.BlockSpec(memory_space=pl.ANY)
+    S = pl.BlockSpec(memory_space=pltpu.SMEM)
+    return pl.pallas_call(
+        functools.partial(attn_kernel, rows, tile),
+        out_shape=jax.ShapeDtypeStruct((rows, width), BF),
+        in_specs=[A] * 10,
+        out_specs=V,
+        scratch_shapes=[
+            pltpu.SMEM((rows,), jnp.int32), pltpu.VMEM((1, rows), jnp.int32), pltpu.VMEM((1, rows), jnp.int32),
+            pltpu.VMEM((rows, width), BF), pltpu.VMEM((rows, 128), BF), pltpu.VMEM((rows, 128), BF),
+            pltpu.VMEM((2, keys, 128), BF), pltpu.VMEM((2, keys, 128), BF),
+            pltpu.VMEM((rows, 128, 128), BF), pltpu.VMEM((rows, 128, 128), BF),
+            pltpu.VMEM((rows, width), BF), pltpu.VMEM((rows, 128), F32), pltpu.VMEM((rows, 128), F32),
+            pltpu.VMEM((rows, 128), F32),
+            pltpu.VMEM((rows, width), F32), pltpu.VMEM((rows, width), F32), pltpu.VMEM((rows, width), F32),
+            pltpu.VMEM((heads * tile, keys), F32),
+            pltpu.SemaphoreType.DMA((6,)), pltpu.SemaphoreType.DMA((2, 2)), pltpu.SemaphoreType.DMA((rows // 16,)), pltpu.SemaphoreType.DMA((rows // 16,)),
+        ],
+        compiler_params=pltpu.CompilerParams(vmem_limit_bytes=58 * 1024 * 1024),
+        cost_estimate=pl.CostEstimate(flops=2*2*1024*2048*128*2, bytes_accessed=11*1024*1024, transcendentals=2*1024*1024),
+    )(prompt_ids, prompt_ids.reshape(1, rows), lengths.reshape(1, rows), queries, new_key, new_value,
+      pk.reshape(2, keys, 128), pv.reshape(2, keys, 128), ck.reshape(rows, 128, 128), cv.reshape(rows, 128, 128))
 
 
 def swap(x, axis):
@@ -179,7 +279,7 @@
         lengths,
         prefix_keys,
         prefix_values,
-        local_prompt,
+        prompt_ids,
     )
 
     first = lax.ppermute(attended, ("xh", "yl"), [(0, 2), (3, 1), (1, 0), (2, 3)])

time: 152 us -> 133 us (0.88)
  matrix products: 30.2 us -> 5.91 us
  Pallas kernels: 5.04 us -> 19.2 us
  other arithmetic: 14.9 us -> 4.09 us
  waiting for transfers between devices: 59.9 us -> 65.7 us
  local copies, waits for them, and re-layouts: 6.24 us -> 3.33 us
    dot_general x5 -> x0, matrix products: 24.3 us -> none  [the longest x1 8.99 us: attend(): jnp.einsum('rkgpj,pkjd->rkgd', pre_w, prefix_values, preferred_element_ty...]
    pallas_call x0 -> x1, Pallas kernels: none -> 13.6 us  [attend(): pl.pallas_call(functools.partial(attn_kernel, rows, tile), out_shape=jax....]
    ppermute x6, waiting for transfers between devices: 1.36 us -> 12 us  [swap(): return lax.ppermute(x, axis, [(0, 1), (1, 0)])]
    reduce_sum x2 -> x0, other arithmetic: 9.4 us -> none  [the longest x1 9.02 us: attend(): jnp.sum(pre_exp, axis=(3, 4)) + jnp.sum(gen_exp, axis=3) + own_exp]
    ppermute x1, waiting for transfers between devices: 4.34 us -> 0.63 us  [body(): lax.ppermute(attended, ('xh', 'yl'), [(0, 2), (3, 1), (1, 0), (2, 3)])]
  transfers between devices with their start and end apart: 15 -> 15, of which waited for: 7 -> 9; matrix products, arithmetic and copies ran while one was open for 30% -> 6% of each run, Pallas kernels for 3% -> 15%
where the time goes in v2:
time: 133 us; the launch traced here: 132 us
  waiting for transfers between devices  65.7 us (49%)
  starting transfers between devices  32.6 us (25%)
  Pallas kernels  19.2 us (14%)
  matrix products  5.91 us (4%)
  other arithmetic  4.09 us (3%)
  local copies, waits for them, and re-layouts  3.33 us (3%)
    ppermute x4, waiting for transfers between devices, shift(): return lax.ppermute(x, 'z', [(i, (i + by) % 4) for i in range(4)])  16.6 us
    all_to_all x1, waiting for transfers between devices, body(): got = lax.all_to_all(sent, ('z', 'xh'), 0, 0, tiled=True)  16.6 us
    pallas_call x1, Pallas kernels, attend(): pl.pallas_call(functools.partial(attn_kernel, rows, tile), out_shape=jax....  13.6 us
    ppermute x6, waiting for transfers between devices, swap(): return lax.ppermute(x, axis, [(0, 1), (1, 0)])  12 us
    all_to_all x1, waiting for transfers between devices, body(): parts = lax.all_to_all(partial, ('xl', 'yh'), 0, 0, tiled=True)  11.4 us
    all_to_all x1, starting transfers between devices, body(): got = lax.all_to_all(sent, ('z', 'xh'), 0, 0, tiled=True)  9.52 us
    all_to_all x1, waiting for transfers between devices, body(): lax.all_to_all(jnp.broadcast_to(mine[None, :], (128, 128)), AXES, 0, 0, t...  8.47 us
    ppermute x4, starting transfers between devices, shift(): return lax.ppermute(x, 'z', [(i, (i + by) % 4) for i in range(4)])  7.64 us
  transfers between devices with their start and end apart: 15, of which 9 were waited for; matrix products, arithmetic and copies ran while one was open for 6% of the time, Pallas kernels for 15%

profile of v2, /device:TPU:0, one launch (start us, length us, event | category | flops | bytes accessed | tf_op | source)
XLA Modules:
  0.0 131.7 jit_solution(9371533692410086089)
XLA Ops:
  0.6 1.7 %collective-permute-start.7 = (bf16[1024,512]{1,0:T(8,128)(2,1)}, bf16[1024,512]{1,0:T(8,128)(2,1)}, u32[]{:S(2)}, u32[]{:S(2)}) collective-permute-start(bf16[1024,512]{1,0:T(8,128)(2,1)} %w00.1), channel_id=1, source_target_pairs={{0,1},{1,0},{2,3},{3,2},{4,5},{5,4},{6,7},{7,6},{8,9},{9,8},{10,11... | collective-permute-start | bytes 3145736 | tf_op jit(solution)/shard_map/ppermute | solution.py:181
  2.4 0.0 collective-permute-start.11
  2.4 13.6 %shard_map.166 = bf16[128,1024]{1,0:T(8,128)(2,1)} custom-call(s32[128]{0:T(128)} %ids_hbm.1, s32[1,128]{1,0:T(1,128)} %bitcast.34, s32[1,128]{1,0:T(1,128)} %bitcast.36, bf16[128,1024]{1,0:T(8,128)(2,1)} %q_hbm.1, bf16[128,128]{1,0:T(8,128)(2,1)} %nk_hbm.1, bf16[128,128]{1,0:T(8,128)(2,1)} %nv_hbm.1, bf16[2,2048,128]{2,1,0:T(8,128)(2,1)} %bitcast.30, ...), custom_call_target="tpu_custom_call" | custom-call | flops 2147483648 | bytes 11534336 | tf_op jit(solution)/shard_map/pallas_call | solution.py:158
  16.0 3.1 %collective-permute-start = (bf16[128,1024]{1,0:T(8,128)(2,1)}, bf16[128,1024]{1,0:T(8,128)(2,1)S(1)}, u32[]{:S(2)}, u32[]{:S(2)}) collective-permute-start(bf16[128,1024]{1,0:T(8,128)(2,1)} %shard_map.166), channel_id=1, source_target_pairs={{0,16},{17,1},{1,0},{16,17},{2,18},{19,3},{3,2},{18,19},{4,20},{21... | collective-permute-start | bytes 786440 | tf_op jit(solution)/shard_map/ppermute | solution.py:285
  19.1 0.7 collective-permute-start.1
  19.8 0.0 copy-done
  19.8 0.3 collective-permute-start.6
  20.1 10.6 %collective-permute-done.7.w10 = bf16[1024,512]{1,0:T(8,128)(2,1)} collective-permute-done((bf16[1024,512]{1,0:T(8,128)(2,1)}, bf16[1024,512]{1,0:T(8,128)(2,1)}, u32[]{:S(2)}, u32[]{:S(2)}) %collective-permute-start.7) | collective-permute-done | bytes 1048608 | tf_op jit(solution)/shard_map/ppermute | solution.py:181
  30.7 0.0 collective-permute-start.8
  30.7 0.6 collective-permute-done
  31.4 0.0 collective-permute-done.1
  31.4 1.0 broadcast_select_fusion.1
  32.4 2.1 %collective-permute-start.2 = (bf16[128,2048]{1,0:T(8,128)(2,1)S(1)}, bf16[128,2048]{1,0:T(8,128)(2,1)S(1)}, u32[]{:S(2)}, u32[]{:S(2)}) collective-permute-start(bf16[128,2048]{1,0:T(8,128)(2,1)S(1)} %pad_maximum_fusion.here), channel_id=1, source_target_pairs={{0,32},{32,64},{64,96},{96,0},{1,33},{33,65},{65,97},{97,1},{2,34}... | collective-permute-start | bytes 1572872 | tf_op jit(solution)/shard_map/ppermute | solution.py:185
  34.6 2.2 %collective-permute-start.3 = (bf16[128,2048]{1,0:T(8,128)(2,1)S(1)}, bf16[128,2048]{1,0:T(8,128)(2,1)S(1)}, u32[]{:S(2)}, u32[]{:S(2)}) collective-permute-start(bf16[128,2048]{1,0:T(8,128)(2,1)S(1)} %pad_maximum_fusion.here), channel_id=1, source_target_pairs={{0,96},{32,0},{64,32},{96,64},{1,97},{33,1},{65,33},{97,65},{2,98}... | collective-permute-start | bytes 1572872 | tf_op jit(solution)/shard_map/ppermute | solution.py:185
  36.8 11.7 %collective-permute-done.2.before = bf16[128,2048]{1,0:T(8,128)(2,1)S(1)} collective-permute-done((bf16[128,2048]{1,0:T(8,128)(2,1)S(1)}, bf16[128,2048]{1,0:T(8,128)(2,1)S(1)}, u32[]{:S(2)}, u32[]{:S(2)}) %collective-permute-start.2) | collective-permute-done | bytes 524320 | tf_op jit(solution)/shard_map/ppermute | solution.py:185
  48.5 0.1 collective-permute-start.4
  48.6 0.0 collective-permute-done.3.after
  48.6 0.7 slice.45
  49.3 3.2 %collective-permute-start.5 = (bf16[64,2048]{1,0:T(8,128)(2,1)}, bf16[64,2048]{1,0:T(8,128)(2,1)S(1)}, u32[]{:S(2)}, u32[]{:S(2)}) collective-permute-start(bf16[64,2048]{1,0:T(8,128)(2,1)} %slice.45), channel_id=1, source_target_pairs={{0,96},{32,0},{64,32},{96,64},{1,97},{33,1},{65,33},{97,65},{2,98}... | collective-permute-start | bytes 786440 | tf_op jit(solution)/shard_map/ppermute | solution.py:185
  52.5 4.6 %collective-permute-done.4.far_a = bf16[64,2048]{1,0:T(8,128)(2,1)S(1)} collective-permute-done((bf16[64,2048]{1,0:T(8,128)(2,1)S(1)}, bf16[64,2048]{1,0:T(8,128)(2,1)S(1)}, u32[]{:S(2)}, u32[]{:S(2)}) %collective-permute-start.4) | collective-permute-done | bytes 262176 | tf_op jit(solution)/shard_map/ppermute | solution.py:185
  57.1 0.3 collective-permute-done.5.far_b
  57.4 0.0 collective-permute-done.6.w01
  57.4 0.0 collective-permute-done.8.w11
  57.5 5.6 %shard_map.167 = bf16[4,128,1024]{2,1,0:T(8,128)(2,1)} custom-call(s32[1]{0:T(128)} %bitcast.z_ref, bf16[128,2048]{1,0:T(8,128)(2,1)S(1)} %pad_maximum_fusion.here, bf16[128,2048]{1,0:T(8,128)(2,1)S(1)} %collective-permute-done.2.before, bf16[128,2048]{1,0:T(8,128)(2,1)S(1)} %collective-permute-done.3.after, ...), custom_call_target="tpu_custom_call" | custom-call | flops 2147483648 | bytes 7340032 | tf_op jit(solution)/shard_map/pallas_call | solution.py:221
  63.1 4.9 %all-to-all-start = ((bf16[4,128,1024]{2,1,0:T(8,128)(2,1)}), bf16[4,128,1024]{2,1,0:T(8,128)(2,1)S(1)}, u32[]{:S(2)}, u32[]{:S(2)}) async-start(bf16[4,128,1024]{2,1,0:T(8,128)(2,1)} %shard_map.167), calls=%async_computation | async-start | bytes 2097152 | tf_op jit(solution)/shard_map/all_to_all | solution.py:296
  68.0 0.0 copy-done.1
  68.0 0.0 copy-done.4
  68.0 0.1 collective-permute-start.9
  68.1 1.3 %collective-permute-done.9 = bf16[144,512]{1,0:T(8,128)(2,1)S(1)} collective-permute-done((bf16[144,512]{1,0:T(8,128)(2,1)S(1)}, bf16[144,512]{1,0:T(8,128)(2,1)S(1)}, u32[]{:S(2)}, u32[]{:S(2)}) %collective-permute-start.9) | collective-permute-done | bytes 147488 | tf_op jit(solution)/shard_map/ppermute | solution.py:181
  69.5 11.4 %all-to-all-done = bf16[4,128,1024]{2,1,0:T(8,128)(2,1)S(1)} async-done(((bf16[4,128,1024]{2,1,0:T(8,128)(2,1)}), bf16[4,128,1024]{2,1,0:T(8,128)(2,1)S(1)}, u32[]{:S(2)}, u32[]{:S(2)}) %all-to-all-start) | async-done | bytes 1048608 | tf_op jit(solution)/shard_map/all_to_all | solution.py:296
  80.8 0.2 convert_reduce_fusion.1
  81.0 0.2 fusion.4
  81.2 0.1 copy.36
  81.4 2.9 %fusion.10 = f32[128,4096]{1,0:T(8,128)S(1)} fusion(bf16[512,4096]{1,0:T(8,128)(2,1)} %param.28, bf16[128,512]{1,0:T(8,128)(2,1)S(1)} %get-tuple-element.21, f32[512]{0:T(512)S(1)} %convert_element_type.86), kind=kOutput, calls=%fused_computation.28 | convolution fusion | flops 537067520 | bytes 6424576 | tf_op jit(solution)/shard_map/dot_general | solution.py:311
  84.3 0.0 collective-permute-done.11
  84.3 3.0 %fusion = bf16[128,4096]{1,0:T(8,128)(2,1)S(1)} fusion(f32[128,4096]{1,0:T(8,128)S(1)} %fusion.10, bf16[512,4096]{1,0:T(8,128)(2,1)} %collective-permute-done.11, bf16[128,512]{1,0:T(8,128)(2,1)S(1)} %get-tuple-element.23, f32[512]{0:T(512)S(1)} %bitcast.33), kind=kOutput, calls=%fused_computation.1 | convolution fusion | flops 538116096 | bytes 7473152 | tf_op jit(solution)/shard_map/dot_general | solution.py:311
  87.3 0.0 copy-start.2
  87.3 0.0 copy-start.3
  87.3 0.0 copy-start.5
  87.3 1.1 fusion.2
  88.4 9.5 %all-to-all-start.1 = ((bf16[8,16,4224]{2,1,0:T(8,128)(2,1)}), bf16[8,16,4224]{2,1,0:T(8,128)(2,1)S(1)}, u32[]{:S(2)}, u32[]{:S(2)}) async-start(bf16[8,16,4224]{2,1,0:T(8,128)(2,1)} %bitcast.9), calls=%async_computation.1 | async-start | bytes 2162688 | tf_op jit(solution)/shard_map/all_to_all | solution.py:318
  97.9 0.0 copy-done.2
  97.9 0.0 copy-done.3
  97.9 0.0 copy-done.5
  98.0 0.1 dynamic_slice.14
  98.0 0.0 collective-permute-start.10
  98.1 16.6 %all-to-all-done.1 = bf16[8,16,4224]{2,1,0:T(8,128)(2,1)S(1)} async-done(((bf16[8,16,4224]{2,1,0:T(8,128)(2,1)}), bf16[8,16,4224]{2,1,0:T(8,128)(2,1)S(1)}, u32[]{:S(2)}, u32[]{:S(2)}) %all-to-all-start.1) | async-done | bytes 1081376 | tf_op jit(solution)/shard_map/all_to_all | solution.py:318
  114.7 0.1 convert_reduce_fusion
  114.8 0.2 fusion.17
  115.0 0.3 multiply_reduce_fusion
  115.3 0.1 pad_maximum_fusion.3
  115.4 0.7 broadcast_in_dim.36
  116.0 4.6 %all-to-all-start.2 = ((f32[128,1,128]{2,1,0:T(1,128)}), f32[128,1,128]{2,1,0:T(1,128)S(1)}, u32[]{:S(2)}, u32[]{:S(2)}) async-start(f32[128,1,128]{2,1,0:T(1,128)} %broadcast_in_dim.36), calls=%async_computation.2 | async-start | bytes 131072 | tf_op jit(solution)/shard_map/all_to_all | solution.py:327
  120.6 0.0 collective-permute-done.10
  120.7 0.8 maximum_select_fusion
  121.4 8.5 %all-to-all-done.2 = f32[128,1,128]{2,1,0:T(1,128)S(1)} async-done(((f32[128,1,128]{2,1,0:T(1,128)}), f32[128,1,128]{2,1,0:T(1,128)S(1)}, u32[]{:S(2)}, u32[]{:S(2)}) %all-to-all-start.2) | async-done | bytes 65568 | tf_op jit(solution)/shard_map/all_to_all | solution.py:327
  129.9 0.1 fusion.21
  130.0 0.1 broadcast_in_dim.37
  130.1 0.1 reshape_reshape.3
  130.2 0.1 eq.23
  130.3 0.2 select_reduce_fusion
  130.4 0.1 reshape.93
  130.5 0.7 copy.39
  131.2 0.6 constant_dynamic-slice_fusion
  (17 shorter events, 0.2 us)
Async XLA Ops:
  0.6 30.1 %collective-permute-start.7 = (bf16[1024,512]{1,0:T(8,128)(2,1)}, bf16[1024,512]{1,0:T(8,128)(2,1)}, u32[]{:S(2)}, u32[]{:S(2)}) collective-permute-start(bf16[1024,512]{1,0:T(8,128)(2,1)} %w00.1), channel_id=1, source_target_pairs={{0,1},{1,0},{2,3},{3,2},{4,5},{5,4},{6,7},{7,6},{8,9},{9,8},{10,11... | collective-permute-start | bytes 3145736 | tf_op jit(solution)/shard_map/ppermute | solution.py:181
  2.4 81.9 %collective-permute-start.11 = (bf16[512,4096]{1,0:T(8,128)(2,1)}, bf16[512,4096]{1,0:T(8,128)(2,1)}, u32[]{:S(2)}, u32[]{:S(2)}) collective-permute-start(bf16[512,4096]{1,0:T(8,128)(2,1)} %param.28), channel_id=1, source_target_pairs={{0,8},{8,0},{1,9},{9,1},{2,10},{10,2},{3,11},{11,3},{4,12},{12,4},... | collective-permute-start | bytes 12582920 | tf_op jit(solution)/shard_map/ppermute | solution.py:181
  2.4 17.4 %copy-start = (bf16[1024,512]{1,0:T(8,128)(2,1)S(1)}, bf16[1024,512]{1,0:T(8,128)(2,1)}, u32[]{:S(2)}) copy-start(bf16[1024,512]{1,0:T(8,128)(2,1)} %w00.1) | copy-start | bytes 3145732
  16.0 15.3 %collective-permute-start = (bf16[128,1024]{1,0:T(8,128)(2,1)}, bf16[128,1024]{1,0:T(8,128)(2,1)S(1)}, u32[]{:S(2)}, u32[]{:S(2)}) collective-permute-start(bf16[128,1024]{1,0:T(8,128)(2,1)} %shard_map.166), channel_id=1, source_target_pairs={{0,16},{17,1},{1,0},{16,17},{2,18},{19,3},{3,2},{18,19},{4,20},{21... | collective-permute-start | bytes 786440 | tf_op jit(solution)/shard_map/ppermute | solution.py:285
  19.1 12.2 %collective-permute-start.1 = (bf16[128,1024]{1,0:T(8,128)(2,1)}, bf16[128,1024]{1,0:T(8,128)(2,1)S(1)}, u32[]{:S(2)}, u32[]{:S(2)}) collective-permute-start(bf16[128,1024]{1,0:T(8,128)(2,1)} %shard_map.166), channel_id=1, source_target_pairs={{1,16},{16,1},{3,18},{18,3},{5,20},{20,5},{7,22},{22,7},{9,24},{24... | collective-permute-start | bytes 786440 | tf_op jit(solution)/shard_map/ppermute | solution.py:286
  19.8 37.6 %collective-permute-start.6 = (bf16[1024,512]{1,0:T(8,128)(2,1)S(1)}, bf16[1024,512]{1,0:T(8,128)(2,1)}, u32[]{:S(2)}, u32[]{:S(2)}) collective-permute-start(bf16[1024,512]{1,0:T(8,128)(2,1)S(1)} %copy-done), channel_id=1, source_target_pairs={{0,8},{8,0},{1,9},{9,1},{2,10},{10,2},{3,11},{11,3},{4,12},{12,4},... | collective-permute-start | bytes 3145736 | tf_op jit(solution)/shard_map/ppermute | solution.py:181
  30.7 26.7 %collective-permute-start.8 = (bf16[1024,512]{1,0:T(8,128)(2,1)}, bf16[1024,512]{1,0:T(8,128)(2,1)}, u32[]{:S(2)}, u32[]{:S(2)}) collective-permute-start(bf16[1024,512]{1,0:T(8,128)(2,1)} %collective-permute-done.7.w10), channel_id=1, source_target_pairs={{0,8},{8,0},{1,9},{9,1},{2,10},{10,2},{3,11},{11,3},{4,12},{12,4},... | collective-permute-start | bytes 3145736 | tf_op jit(solution)/shard_map/ppermute | solution.py:181
  32.4 16.1 %collective-permute-start.2 = (bf16[128,2048]{1,0:T(8,128)(2,1)S(1)}, bf16[128,2048]{1,0:T(8,128)(2,1)S(1)}, u32[]{:S(2)}, u32[]{:S(2)}) collective-permute-start(bf16[128,2048]{1,0:T(8,128)(2,1)S(1)} %pad_maximum_fusion.here), channel_id=1, source_target_pairs={{0,32},{32,64},{64,96},{96,0},{1,33},{33,65},{65,97},{97,1},{2,34}... | collective-permute-start | bytes 1572872 | tf_op jit(solution)/shard_map/ppermute | solution.py:185
  34.6 14.0 %collective-permute-start.3 = (bf16[128,2048]{1,0:T(8,128)(2,1)S(1)}, bf16[128,2048]{1,0:T(8,128)(2,1)S(1)}, u32[]{:S(2)}, u32[]{:S(2)}) collective-permute-start(bf16[128,2048]{1,0:T(8,128)(2,1)S(1)} %pad_maximum_fusion.here), channel_id=1, source_target_pairs={{0,96},{32,0},{64,32},{96,64},{1,97},{33,1},{65,33},{97,65},{2,98}... | collective-permute-start | bytes 1572872 | tf_op jit(solution)/shard_map/ppermute | solution.py:185
  48.5 8.6 %collective-permute-start.4 = (bf16[64,2048]{1,0:T(8,128)(2,1)S(1)}, bf16[64,2048]{1,0:T(8,128)(2,1)S(1)}, u32[]{:S(2)}, u32[]{:S(2)}) collective-permute-start(bf16[64,2048]{1,0:T(8,128)(2,1)S(1)} %slice.44), channel_id=1, source_target_pairs={{0,32},{32,64},{64,96},{96,0},{1,33},{33,65},{65,97},{97,1},{2,34}... | collective-permute-start | bytes 786440 | tf_op jit(solution)/shard_map/ppermute | solution.py:185
  49.3 8.1 %collective-permute-start.5 = (bf16[64,2048]{1,0:T(8,128)(2,1)}, bf16[64,2048]{1,0:T(8,128)(2,1)S(1)}, u32[]{:S(2)}, u32[]{:S(2)}) collective-permute-start(bf16[64,2048]{1,0:T(8,128)(2,1)} %slice.45), channel_id=1, source_target_pairs={{0,96},{32,0},{64,32},{96,64},{1,97},{33,1},{65,33},{97,65},{2,98}... | collective-permute-start | bytes 786440 | tf_op jit(solution)/shard_map/ppermute | solution.py:185
  63.1 4.9 %copy-start.1 = (bf16[256,512]{1,0:T(8,128)(2,1)S(1)}, bf16[256,512]{1,0:T(8,128)(2,1)}, u32[]{:S(2)}) copy-start(bf16[256,512]{1,0:T(8,128)(2,1)} %param.26) | copy-start | bytes 786436
  63.1 4.9 %copy-start.4 = (bf16[512]{0:T(512)(128)(2,1)S(1)}, bf16[512]{0:T(512)(128)(2,1)}, u32[]{:S(2)}) copy-start(bf16[512]{0:T(512)(128)(2,1)} %param.27) | copy-start | bytes 3076
  63.1 17.8 %all-to-all-start = ((bf16[4,128,1024]{2,1,0:T(8,128)(2,1)}), bf16[4,128,1024]{2,1,0:T(8,128)(2,1)S(1)}, u32[]{:S(2)}, u32[]{:S(2)}) async-start(bf16[4,128,1024]{2,1,0:T(8,128)(2,1)} %shard_map.167), calls=%async_computation | async-start | bytes 2097152 | tf_op jit(solution)/shard_map/all_to_all | solution.py:296
  68.0 1.5 %collective-permute-start.9 = (bf16[144,512]{1,0:T(8,128)(2,1)S(1)}, bf16[144,512]{1,0:T(8,128)(2,1)S(1)}, u32[]{:S(2)}, u32[]{:S(2)}) collective-permute-start(bf16[144,512]{1,0:T(8,128)(2,1)S(1)} %pad_maximum_fusion.1), channel_id=1, source_target_pairs={{0,8},{8,0},{1,9},{9,1},{2,10},{10,2},{3,11},{11,3},{4,12},{12,4},... | collective-permute-start | bytes 442376 | tf_op jit(solution)/shard_map/ppermute | solution.py:181
  87.3 10.6 %copy-start.2 = (bf16[4096]{0:T(1024)(128)(2,1)S(1)}, bf16[4096]{0:T(1024)(128)(2,1)}, u32[]{:S(2)}) copy-start(bf16[4096]{0:T(1024)(128)(2,1)} %param.29) | copy-start | bytes 24580
  87.3 10.6 %copy-start.3 = (s32[128]{0:T(128)S(1)}, s32[128]{0:T(128)}, u32[]{:S(2)}) copy-start(s32[128]{0:T(128)} %ids_hbm.1) | copy-start | bytes 1540
  87.3 10.6 %copy-start.5 = (s32[128]{0:T(128)S(1)}, s32[128]{0:T(128)}, u32[]{:S(2)}) copy-start(s32[128]{0:T(128)} %param.24) | copy-start | bytes 1540
  88.4 26.3 %all-to-all-start.1 = ((bf16[8,16,4224]{2,1,0:T(8,128)(2,1)}), bf16[8,16,4224]{2,1,0:T(8,128)(2,1)S(1)}, u32[]{:S(2)}, u32[]{:S(2)}) async-start(bf16[8,16,4224]{2,1,0:T(8,128)(2,1)} %bitcast.9), calls=%async_computation.1 | async-start | bytes 2162688 | tf_op jit(solution)/shard_map/all_to_all | solution.py:318
  98.0 22.6 %collective-permute-start.10 = (bf16[128,512]{1,0:T(8,128)(2,1)S(1)}, bf16[128,512]{1,0:T(8,128)(2,1)S(1)}, u32[]{:S(2)}, u32[]{:S(2)}) collective-permute-start(bf16[128,512]{1,0:T(8,128)(2,1)S(1)} %get-tuple-element.23), channel_id=1, source_target_pairs={{0,8},{8,0},{1,9},{9,1},{2,10},{10,2},{3,11},{11,3},{4,12},{12,4},... | collective-permute-start | bytes 393224 | tf_op jit(solution)/shard_map/ppermute | solution.py:181
  116.0 13.9 %all-to-all-start.2 = ((f32[128,1,128]{2,1,0:T(1,128)}), f32[128,1,128]{2,1,0:T(1,128)S(1)}, u32[]{:S(2)}, u32[]{:S(2)}) async-start(f32[128,1,128]{2,1,0:T(1,128)} %broadcast_in_dim.36), calls=%async_computation.2 | async-start | bytes 131072 | tf_op jit(solution)/shard_map/all_to_all | solution.py:327

commit v3 on v2

--- a/solution.py
+++ b/solution.py
@@ -19,6 +19,7 @@
 F32 = jnp.float32
 SCALE2 = math.log2(math.e) / math.sqrt(128)
 NEG = -1e30
+LIMIT = 63 * 1024 * 1024
 NT = (((1,), (1,)), ((), ()))
 
 
@@ -171,8 +172,8 @@
             pltpu.VMEM((heads * tile, keys), F32),
             pltpu.SemaphoreType.DMA((6,)), pltpu.SemaphoreType.DMA((2, 2)), pltpu.SemaphoreType.DMA((rows // 16,)), pltpu.SemaphoreType.DMA((rows // 16,)),
         ],
-        compiler_params=pltpu.CompilerParams(vmem_limit_bytes=58 * 1024 * 1024),
-        cost_estimate=pl.CostEstimate(flops=2*2*1024*2048*128*2, bytes_accessed=11*1024*1024, transcendentals=2*1024*1024),
+        compiler_params=pltpu.CompilerParams(vmem_limit_bytes=LIMIT),
+        cost_estimate=pl.CostEstimate(flops=16 * 10**9, bytes_accessed=11 * 1024 * 1024, transcendentals=2 * 1024 * 1024),
     )(prompt_ids, prompt_ids.reshape(1, rows), lengths.reshape(1, rows), queries, new_key, new_value,
       pk.reshape(2, keys, 128), pv.reshape(2, keys, 128), ck.reshape(rows, 128, 128), cv.reshape(rows, 128, 128))
 
@@ -185,53 +186,266 @@
     return lax.ppermute(x, "z", [(i, (i + by) % 4) for i in range(4)])
 
 
-def proj_kernel(z_ref, here, before, after, far_a, far_b, w00, w01, w10, w11, out_ref):
-    step = pl.program_id(0)
-
-    def work(a, rows):
-        own, par = a[:, :1024], a[:, 1024:]
-        for j, (wo, wp) in enumerate(((w00, w10), (w01, w11))):
-            acc = jnp.dot(own, wo[...], preferred_element_type=F32)
-            acc = acc + jnp.dot(par, wp[...], preferred_element_type=F32)
-            out_ref[0, rows, j * 512 : (j + 1) * 512] = acc.astype(BF)
-
-    full = slice(0, 128)
-
-    @pl.when(step == 0)
-    def _():
-        work(here[...], full)
-
-    @pl.when(step == 1)
-    def _():
-        work(before[...], full)
-
-    @pl.when(step == 2)
-    def _():
-        work(jnp.concatenate([far_a[...], far_b[...]], axis=0), full)
-
-    @pl.when(step == 3)
-    def _():
-        work(after[...], full)
-
-
-def project(here, before, after, far_a, far_b, w00, w01, w10, w11):
-    z = lax.axis_index("z").astype(jnp.int32).reshape(1)
-    whole = lambda a: pl.BlockSpec(a.shape, lambda s, z_ref: (0,) * a.ndim)
-    ins = (here, before, after, far_a, far_b, w00, w01, w10, w11)
+def tiny(mib, flops=1024, **kw):
+    return dict(
+        compiler_params=pltpu.CompilerParams(vmem_limit_bytes=mib * 1024 * 1024),
+        cost_estimate=pl.CostEstimate(flops=flops, bytes_accessed=1024, transcendentals=0),
+        **kw,
+    )
+
+
+def hold_kernel(*refs):
+    pass
+
+
+def hold(x, *tokens):
+    A = pl.BlockSpec(memory_space=pl.ANY)
     return pl.pallas_call(
-        proj_kernel,
-        out_shape=jax.ShapeDtypeStruct((4, 128, 1024), BF),
-        grid_spec=pltpu.PrefetchScalarGridSpec(
-            num_scalar_prefetch=1,
-            grid=(4,),
-            in_specs=[whole(a) for a in ins],
-            out_specs=pl.BlockSpec((1, 128, 1024), lambda s, z_ref: ((z_ref[0] + 4 - s) % 4, 0, 0)),
+        hold_kernel,
+        out_shape=jax.ShapeDtypeStruct(x.shape, x.dtype),
+        in_specs=[A] * (1 + len(tokens)),
+        out_specs=A,
+        input_output_aliases={0: 0},
+        **tiny(4),
+    )(x, *tokens)
+
+
+def proj_kernel(steps, *refs):
+    count = len(steps)
+    rows, weights = refs[:count], refs[count : count + 4]
+    out, w, chunks, sems = refs[-4:]
+    loads = [
+        pltpu.make_async_copy(src, w.at[:, j * 512 : (j + 1) * 512], sems.at[j])
+        for j, src in enumerate(weights)
+    ]
+    for load in loads:
+        load.start()
+    a = jnp.concatenate([row[...] for row in rows], axis=0)
+    z = lax.axis_index("z")
+    xh = lax.axis_index("xh")
+    leave = []
+    for j in range(4):
+        loads[j].wait()
+        total = jnp.dot(a, w[:, j * 512 : (j + 1) * 512], preferred_element_type=F32).astype(BF)
+        total = total.reshape(count, 2, 64, 512)
+        for i in range(count):
+            chunks[j // 2, i, :, :, (j % 2) * 512 : (j % 2 + 1) * 512] = total[i]
+        if j % 2:
+            for i, step in enumerate(steps):
+                first = ((xh ^ (j // 2)) * 4 + ((z - step) & 3)) * 2
+                leave.append(
+                    pltpu.make_async_copy(chunks.at[j // 2, i], out.at[pl.ds(first, 2)], sems.at[4 + j // 2 * count + i])
+                )
+                leave[-1].start()
+    for copy in leave:
+        copy.wait()
+
+
+def project(steps, *ins):
+    count = len(steps)
+    more = len(ins) > count + 4
+    V = pl.BlockSpec(memory_space=pltpu.VMEM)
+    A = pl.BlockSpec(memory_space=pl.ANY)
+    return pl.pallas_call(
+        functools.partial(proj_kernel, steps),
+        out_shape=jax.ShapeDtypeStruct((16, 64, 1024), BF),
+        in_specs=[V] * count + [A] * (len(ins) - count),
+        out_specs=A,
+        input_output_aliases={count + 4: 0} if more else {},
+        scratch_shapes=[
+            pltpu.VMEM((1024, 2048), BF),
+            pltpu.VMEM((2, count, 2, 64, 1024), BF),
+            pltpu.SemaphoreType.DMA((4 + 2 * count,)),
+        ],
+        **tiny(40, 0 if more else 4 * 10**9),
+    )(*ins)
+
+
+def up_kernel(
+    parts, res, extra, res_y, gain, up_mine, up_par,
+    hm_ref, hp_ref, sent_ref, parts_v, res_v, gain_v, gain2_v, w, sems,
+):
+    c = lax.axis_index("c")
+    yl = lax.axis_index("yl")
+    here = pl.ds(pl.multiple_of(yl * 64, 64), 64)
+    there = pl.ds(pl.multiple_of(64 - yl * 64, 64), 64)
+    small = [
+        pltpu.make_async_copy(src, dst, sems.at[i // 4, i % 4])
+        for i, (src, dst) in enumerate((
+            (parts.at[:8], parts_v.at[:8]), (parts.at[8:], parts_v.at[8:]),
+            (res.at[pl.ds(pl.multiple_of(c * 128 + yl * 64, 64), 64)], res_v.at[here, :512]),
+            (extra.at[here], res_v.at[here, 512:]),
+            (res_y, res_v.at[there]),
+            (gain, gain_v), (extra.at[128:], gain2_v),
+        ))
+    ]
+    for copy in small:
+        copy.start()
+    loads = []
+    for j in range(4):
+        cols = slice(j * 1024, (j + 1) * 1024)
+        loads.append((
+            pltpu.make_async_copy(up_mine.at[:, cols], w.at[0:512, cols], sems.at[2, j]),
+            pltpu.make_async_copy(up_par.at[:, cols], w.at[512:1024, cols], sems.at[3, j]),
+        ))
+        for load in loads[-1]:
+            load.start()
+    for copy in small:
+        copy.wait()
+
+    def summed(first):
+        total = parts_v[first].astype(F32)
+        for i in range(1, 8):
+            total = total + parts_v[first + i].astype(F32)
+        return total
+
+    mixed = jnp.concatenate([summed(0), summed(8)], axis=0)
+    hid = (res_v[...].astype(F32) + mixed).astype(BF)
+    hm_ref[...] = hid[:, :512]
+    hp_ref[...] = hid[:, 512:]
+    wide = hid.astype(F32)
+    squares = jnp.sum(wide * wide, axis=1, keepdims=True)
+    hi = squares.astype(BF).astype(F32)
+    lane = lax.broadcasted_iota(jnp.int32, (128, 128), 1)
+    sent_ref[:, 4096:] = jnp.where(lane == 0, hi, jnp.where(lane == 1, squares - hi, 0.0)).astype(BF)
+    gains = jnp.concatenate([gain_v[0:1], gain2_v[0:1]], axis=1).astype(F32)
+    gained = (wide * gains).astype(BF)
+    for j in range(4):
+        cols = slice(j * 1024, (j + 1) * 1024)
+        for load in loads[j]:
+            load.wait()
+        sent_ref[:, cols] = jnp.dot(gained, w[:, cols], preferred_element_type=F32).astype(BF)
+
+
+def verify_up(*ins):
+    V = pl.BlockSpec(memory_space=pltpu.VMEM)
+    A = pl.BlockSpec(memory_space=pl.ANY)
+    return pl.pallas_call(
+        up_kernel,
+        out_shape=(
+            jax.ShapeDtypeStruct((128, 512), BF),
+            jax.ShapeDtypeStruct((128, 512), BF),
+            jax.ShapeDtypeStruct((128, 4096 + 128), BF),
         ),
-        compiler_params=pltpu.CompilerParams(vmem_limit_bytes=40 * 1024 * 1024),
-        cost_estimate=pl.CostEstimate(
-            flops=2 * 512 * 2048 * 1024, bytes_accessed=7 * 1024 * 1024, transcendentals=0
-        ),
-    )(z, *ins)
+        in_specs=[A] * 7,
+        out_specs=(V, V, V),
+        scratch_shapes=[
+            pltpu.VMEM((16, 64, 1024), BF),
+            pltpu.VMEM((128, 1024), BF),
+            pltpu.VMEM((16, 512), BF),
+            pltpu.VMEM((16, 512), BF),
+            pltpu.VMEM((1024, 4096), BF),
+            pltpu.SemaphoreType.DMA((4, 4)),
+        ],
+        **tiny(58),
+    )(*ins)
+
+
+def score_kernel(got_hbm, head_hbm, prompts_hbm, clusters_hbm, out_ref, got, head, prompts, clusters, sems):
+    copies = [
+        pltpu.make_async_copy(src, dst, sems.at[i])
+        for i, (src, dst) in enumerate((
+            (got_hbm, got), (head_hbm, head), (prompts_hbm, prompts), (clusters_hbm, clusters)
+        ))
+    ]
+    for copy in copies:
+        copy.start()
+    for copy in copies:
+        copy.wait()
+
+    def summed(cols):
+        total = got[0, :, cols].astype(F32)
+        for i in range(1, 8):
+            total = total + got[i, :, cols].astype(F32)
+        return total
+
+    tail = summed(slice(4096, 4224))
+    squares = tail[:, 0:1] + tail[:, 1:2]
+    factor = lax.rsqrt(squares / D + eps)
+    acc = jnp.zeros((16, 512), F32)
+    for j in range(0, 4096, 512):
+        cols = slice(j, j + 512)
+        up = summed(cols) * factor
+        acc = acc + up / (1.0 + jnp.exp(-up)) * head[0:1, cols].astype(F32)
+    scores = jnp.sum(acc, axis=1, keepdims=True)
+    row = lax.broadcasted_iota(jnp.int32, (16, 128), 0)
+    lane = lax.broadcasted_iota(jnp.int32, (16, 128), 1)
+    line = jnp.sum(jnp.where(row == lane, scores, 0.0), axis=0, keepdims=True)
+    pair = ((prompts[...] & 1) * CLUSTERS + clusters[...]).astype(F32)
+    t = lax.axis_index(TP)
+    pair = pltpu.roll(jnp.broadcast_to(pair, (8, 128)), (144 - t * 16) & 127, 1)[0:1]
+    lane = lane[0:1]
+    mine = jnp.where(lane < 16, line, jnp.where(lane < 32, pair, 0.0))
+    out_ref[...] = jnp.broadcast_to(mine.reshape(1, 1, 128), (128, 1, 128))
+
+
+def score(got, head_weight, prompt_ids, cluster_ids):
+    V = pl.BlockSpec(memory_space=pltpu.VMEM)
+    A = pl.BlockSpec(memory_space=pl.ANY)
+    return pl.pallas_call(
+        score_kernel,
+        out_shape=jax.ShapeDtypeStruct((128, 1, 128), F32),
+        in_specs=[A] * 4,
+        out_specs=V,
+        scratch_shapes=[
+            pltpu.VMEM((8, 16, 4096 + 128), BF),
+            pltpu.VMEM((1, 4096), BF),
+            pltpu.VMEM((1, 128), jnp.int32),
+            pltpu.VMEM((1, 128), jnp.int32),
+            pltpu.SemaphoreType.DMA((4,)),
+        ],
+        **tiny(40),
+    )(got, head_weight.reshape(1, 4096), prompt_ids.reshape(1, 128), cluster_ids.reshape(1, 128))
+
+
+def vote_kernel(all_hbm, scores_ref, votes_ref, x3, x, sem):
+    copy = pltpu.make_async_copy(all_hbm, x3, sem)
+    copy.start()
+    copy.wait()
+    x[...] = x3[...].reshape(128, 128)
+    t = lax.axis_index(TP)
+    lane8 = lax.broadcasted_iota(jnp.int32, (8, 128), 1)
+    lane = lax.broadcasted_iota(jnp.int32, (16, 32), 1)
+    row = lax.broadcasted_iota(jnp.int32, (16, 32), 0)
+
+    def scores_of(zx, c):
+        base = (zx & 1) * 64 + c * 8 + (zx >> 1) * 2
+        return jnp.concatenate(
+            [x[pl.ds(base, 4, stride=16), :], x[pl.ds(base + 1, 4, stride=16), :]], axis=0
+        )
+
+    for c in range(2):
+        block = jnp.where(lane8 < 16, scores_of(t, c), 0.0)
+        spread = block[0:1]
+        for i in range(1, 8):
+            spread = spread + pltpu.roll(block, 16 * i, 1)[i : i + 1]
+        scores_ref[c : c + 1, :] = spread
+    live = (lane8 >= 16) & (lane8 < 32)
+    votes = jnp.zeros((16, 32), F32)
+    for zx in range(8):
+        for c in range(2):
+            dp = zx * 2 + c
+            ids = jnp.where(live, x[dp * 8 : dp * 8 + 8, :], -1.0)
+            vals = pltpu.roll(scores_of(zx, c), 16, 1)
+            for p in range(2):
+                for k in range(CLUSTERS):
+                    hit = jnp.where(ids == float(p * CLUSTERS + k), vals, 0.0)
+                    one = jnp.sum(jnp.sum(hit, axis=0, keepdims=True), axis=1, keepdims=True)
+                    votes = jnp.where((row == k) & (lane == dp * 2 + p), one, votes)
+    votes_ref[...] = votes
+
+
+def tally(everyone):
+    V = pl.BlockSpec(memory_space=pltpu.VMEM)
+    A = pl.BlockSpec(memory_space=pl.ANY)
+    return pl.pallas_call(
+        vote_kernel,
+        out_shape=(jax.ShapeDtypeStruct((2, 128), F32), jax.ShapeDtypeStruct((CLUSTERS, 32), F32)),
+        in_specs=[A],
+        out_specs=(V, V),
+        scratch_shapes=[pltpu.VMEM((128, 1, 128), F32), pltpu.VMEM((128, 128), F32), pltpu.SemaphoreType.DMA],
+        **tiny(40),
+    )(everyone)
 
 
 def body(
@@ -252,25 +466,16 @@
     head_weight,
 ):
     c = lax.axis_index("c")
-    xh = lax.axis_index("xh")
     yl = lax.axis_index("yl")
-    t = lax.axis_index(TP)
-    dp_index = lax.axis_index(DP)
-    local_prompt = prompt_ids - dp_index * PROMPTS_DEV
-
-    w00 = out_weight
-    w10 = swap(out_weight, "yl")
-    w01 = swap(w00, "c")
-    w11 = swap(w10, "c")
+
+    def rows_of(x, first, count):
+        return lax.dynamic_slice_in_dim(x, first, count, 0)
+
+    w10 = swap(out_weight, "xh")
     up_par = swap(up_weight, "c")
-    res_mine = lax.dynamic_slice_in_dim(residual, c * 128, 128, 0)
-    res_send = lax.dynamic_slice_in_dim(residual, (1 - c) * 128, 128, 0)
-    extra = swap(
-        jnp.concatenate([res_send, jnp.broadcast_to(norm_gain[None, :], (16, 512))], axis=0), "c"
-    )
-    res_par, gain_par = extra[:128], extra[128]
-
-    attended = attend(
+    w01 = swap(out_weight, "c")
+
+    part = attend(
         queries,
         new_key,
         new_value,
@@ -282,56 +487,42 @@
         prompt_ids,
     )
 
-    first = lax.ppermute(attended, ("xh", "yl"), [(0, 2), (3, 1), (1, 0), (2, 3)])
-    second = lax.ppermute(attended, ("xh", "yl"), [(1, 2), (2, 1)])
-    diagonal = xh == yl
-    here = jnp.concatenate(
-        [jnp.where(diagonal, attended, first), jnp.where(diagonal, first, second)], axis=1
-    )
-    before = shift(here, 1)
-    after = shift(here, -1)
-    far_a = shift(before[:64], 1)
-    far_b = shift(after[64:], -1)
-    partial = project(here, before, after, far_a, far_b, w00, w01, w10, w11)
-    parts = lax.all_to_all(partial, ("xl", "yh"), 0, 0, tiled=True)
-    mixed = jnp.sum(parts.astype(F32), axis=0)
-    hid_mine = (res_mine.astype(F32) + mixed[:, :512]).astype(BF)
-    hid_par = (res_par.astype(F32) + mixed[:, 512:]).astype(BF)
+    part = hold(part, up_par, w01)
+    before, after = shift(part, 1), shift(part, 3)
+    far = shift(before, 1)
+    gain = jnp.broadcast_to(norm_gain[None, :], (16, 512))
+    extra = swap(jnp.concatenate([rows_of(residual, (1 - c) * 128, 128), gain], axis=0), "c")
+    res_y = swap(
+        jnp.concatenate(
+            [rows_of(residual, c * 128 + (1 - yl) * 64, 64), rows_of(extra, (1 - yl) * 64, 64)], axis=1
+        ),
+        "yl",
+    )
+    w10 = hold(w10, before, after)
+    w11 = swap(w10, "c")
+
+    weights = (out_weight, w01, w10, w11)
+    partial = project((0, 1, 3), part, before, after, *weights)
+    partial = project((2,), far, *weights, partial)
+    parts = lax.all_to_all(partial, ("xh", "xl", "yh", "yl"), 0, 0, tiled=True)
+    hid_mine, hid_par, sent = verify_up(parts, residual, extra, res_y, gain, up_weight, up_par)
+    got = lax.all_to_all(sent.reshape(8, 16, 4096 + 128), ("z", "xh"), 0, 0, tiled=True)
+
     hid_back = swap(hid_par, "c")
+    away = jnp.concatenate([rows_of(hid_mine, (1 - yl) * 64, 64), rows_of(hid_back, (1 - yl) * 64, 64)], axis=1)
+    home = jnp.concatenate([rows_of(hid_mine, yl * 64, 64), rows_of(hid_back, yl * 64, 64)], axis=1)
+    came = swap(away, "yl")
+    block = jnp.where(
+        yl == 0, jnp.concatenate([home, came], axis=0), jnp.concatenate([came, home], axis=0)
+    )
+    mine, back = block[:, :512], block[:, 512:]
     hidden = jnp.where(
-        c == 0,
-        jnp.concatenate([hid_mine, hid_back], axis=0),
-        jnp.concatenate([hid_back, hid_mine], axis=0),
-    )
-
-    wide_mine, wide_par = hid_mine.astype(F32), hid_par.astype(F32)
-    squares = jnp.sum(wide_mine * wide_mine, axis=1) + jnp.sum(wide_par * wide_par, axis=1)
-    gained_mine = (wide_mine * norm_gain.astype(F32)[None, :]).astype(BF)
-    gained_par = (wide_par * gain_par.astype(F32)[None, :]).astype(BF)
-    up = jnp.dot(gained_mine, up_weight, preferred_element_type=F32) + jnp.dot(
-        gained_par, up_par, preferred_element_type=F32
-    )
-    sq_hi = squares.astype(BF)
-    sq_lo = (squares - sq_hi.astype(F32)).astype(BF)
-    tail = jnp.pad(jnp.stack([sq_hi, sq_lo], axis=1), ((0, 0), (0, 126)))
-    sent = jnp.concatenate([up.astype(BF), tail], axis=1).reshape(8, 16, 4096 + 128)
-    got = lax.all_to_all(sent, ("z", "xh"), 0, 0, tiled=True)
-    total = jnp.sum(got.astype(F32), axis=0)
-    row_sq = total[:, 4096] + total[:, 4097]
-    verifier_up = total[:, :4096] * lax.rsqrt(row_sq / D + eps)[:, None]
-    scores16 = jnp.sum(jax.nn.silu(verifier_up) * head_weight.astype(F32)[None, :], axis=1)
-
-    pair = (local_prompt * CLUSTERS + cluster_ids).astype(F32)
-    pair16 = lax.dynamic_slice_in_dim(pair, t * 16, 16, 0)
-    mine = jnp.concatenate([scores16, pair16, jnp.zeros((96,), F32)])
-    everyone = lax.all_to_all(jnp.broadcast_to(mine[None, :], (128, 128)), AXES, 0, 0, tiled=True)
-    table = everyone.reshape(8, 2, 8, 128)
-    all_scores = table[..., :16].transpose(2, 1, 0, 3).reshape(16, 128)
-    all_pairs = table[..., 16:32].reshape(16, 128)
-    hot = all_pairs[:, :, None] == jnp.arange(32, dtype=F32)[None, None, :]
-    votes = jnp.sum(jnp.where(hot, all_scores[:, :, None], 0.0), axis=1)
-    scores = lax.dynamic_slice_in_dim(all_scores.reshape(8, 256), t, 1, 0).reshape(256)
-    return hidden, scores, votes.reshape(32, CLUSTERS)
+        c == 0, jnp.concatenate([mine, back], axis=0), jnp.concatenate([back, mine], axis=0)
+    )
+
+    line = score(got, head_weight, prompt_ids, cluster_ids)
+    scores, votes = tally(lax.all_to_all(line, AXES, 0, 0, tiled=True))
+    return hidden, scores.reshape(256), votes.T
 
 
 def solution(mesh):

time: 133 us -> 128 us (0.962)
  Pallas kernels: 19.2 us -> 30.2 us
  matrix products: 5.91 us -> 0 us
  starting transfers between devices: 32.6 us -> 29.1 us
  waiting for transfers between devices: 65.7 us -> 62.4 us
  other arithmetic: 4.09 us -> 0.85 us
    ppermute x6 -> x8, waiting for transfers between devices: 12 us -> 37.9 us  [swap(): return lax.ppermute(x, axis, [(0, 1), (1, 0)])]
    all_to_all x3, waiting for transfers between devices: 36.4 us -> 20.3 us  [the longest x1 8.94 us: body(): lax.all_to_all(sent.reshape(8, 16, 4096 + 128), ('z', 'xh'), 0, 0, tiled=...]
    ppermute x4 -> x3, waiting for transfers between devices: 16.6 us -> 4.19 us  [shift(): return lax.ppermute(x, 'z', [(i, (i + by) % 4) for i in range(4)])]
    pallas_call x1 -> x7, Pallas kernels: 5.6 us -> 16.7 us  [the longest x2 7.2 us: project(): pl.pallas_call(functools.partial(proj_kernel, steps), out_shape=jax.Shape...]
    dot_general x2 -> x0, matrix products: 5.91 us -> none  [the longest x1 3 us: body(): jnp.dot(gained_par, up_par, preferred_element_type=F32)]
    ppermute x6 -> x8, starting transfers between devices: 2.15 us -> 6.47 us  [swap(): return lax.ppermute(x, axis, [(0, 1), (1, 0)])]
    ppermute x2 -> x0, starting transfers between devices: 3.77 us -> none  [the longest x1 3.11 us: body(): lax.ppermute(attended, ('xh', 'yl'), [(0, 2), (3, 1), (1, 0), (2, 3)])]
    unnamed x13 -> x30, local copies, waits for them, and re-layouts: 0.7 us -> 3.08 us
  transfers between devices with their start and end apart: 15 -> 14, of which waited for: 9 -> 11; matrix products, arithmetic and copies ran while one was open for 6% -> 1% of each run, Pallas kernels for 15% -> 14%
where the time goes in v3:
time: 128 us; the launch traced here: 127 us
  waiting for transfers between devices  62.4 us (49%)
  Pallas kernels  30.2 us (24%)
  starting transfers between devices  29.1 us (23%)
  local copies, waits for them, and re-layouts  3.18 us (2%)
    ppermute x8, waiting for transfers between devices, swap(): return lax.ppermute(x, axis, [(0, 1), (1, 0)])  37.9 us
    pallas_call x1, Pallas kernels, attend(): pl.pallas_call(functools.partial(attn_kernel, rows, tile), out_shape=jax....  13.5 us
    all_to_all x1, waiting for transfers between devices, body(): lax.all_to_all(sent.reshape(8, 16, 4096 + 128), ('z', 'xh'), 0, 0, tiled=...  8.94 us
    all_to_all x1, waiting for transfers between devices, body(): scores, votes = tally(lax.all_to_all(line, AXES, 0, 0, tiled=True))  8.51 us
    pallas_call x2, Pallas kernels, project(): pl.pallas_call(functools.partial(proj_kernel, steps), out_shape=jax.Shape...  7.2 us
    all_to_all x1, starting transfers between devices, body(): parts = lax.all_to_all(partial, ('xh', 'xl', 'yh', 'yl'), 0, 0, tiled=True)  7.16 us
    ppermute x8, starting transfers between devices, swap(): return lax.ppermute(x, axis, [(0, 1), (1, 0)])  6.47 us
    all_to_all x1, starting transfers between devices, body(): scores, votes = tally(lax.all_to_all(line, AXES, 0, 0, tiled=True))  6.44 us
  transfers between devices with their start and end apart: 14, of which 11 were waited for; matrix products, arithmetic and copies ran while one was open for 1% of the time, Pallas kernels for 14%

profile of v3, /device:TPU:0, one launch (start us, length us, event | category | flops | bytes accessed | tf_op | source)
XLA Modules:
  0.0 126.7 jit_solution(18233097150527559546)
XLA Ops:
  0.6 0.1 collective-permute-start
  0.7 0.5 collective-permute-start.1
  1.2 3.1 %collective-permute-start.4 = (bf16[1024,512]{1,0:T(8,128)(2,1)}, bf16[1024,512]{1,0:T(8,128)(2,1)}, u32[]{:S(2)}, u32[]{:S(2)}) collective-permute-start(bf16[1024,512]{1,0:T(8,128)(2,1)} %refs_1_.1), channel_id=1, source_target_pairs={{0,16},{16,0},{1,17},{17,1},{2,18},{18,2},{3,19},{19,3},{4,20},{20... | collective-permute-start | bytes 3145736 | tf_op jit(solution)/shard_map/ppermute | solution.py:182
  4.3 13.5 %shard_map.166.refs_0_ = bf16[128,1024]{1,0:T(8,128)(2,1)} custom-call(s32[128]{0:T(128)} %ids_hbm.1, s32[1,128]{1,0:T(1,128)} %bitcast.10, s32[1,128]{1,0:T(1,128)} %bitcast.20, bf16[128,1024]{1,0:T(8,128)(2,1)} %q_hbm.1, bf16[128,128]{1,0:T(8,128)(2,1)} %nk_hbm.1, bf16[128,128]{1,0:T(8,128)(2,1)} %nv_hbm.1, bf16[2,2048,128]{2,1,0:T(8,128)(2,1)} %bitcast.16, ...), custom_call_target="tpu_custom_call" | custom-call | flops 16000000000 | bytes 11534336 | tf_op jit(solution)/shard_map/pallas_call | solution.py:159
  17.8 0.0 collective-permute-done.1.refs_2_.refs_4_
  17.8 0.0 collective-permute-done.refs_1_.up_par
  17.9 0.0 copy-start.1
  17.9 0.9 copy-done.1
  18.8 0.0 copy-start
  18.8 1.9 %collective-permute-start.2 = (bf16[128,1024]{1,0:T(8,128)(2,1)S(1)}, bf16[128,1024]{1,0:T(8,128)(2,1)S(1)}, u32[]{:S(2)}, u32[]{:S(2)}) collective-permute-start(bf16[128,1024]{1,0:T(8,128)(2,1)S(1)} %shard_map.167.refs_0_), channel_id=1, source_target_pairs={{0,32},{32,64},{64,96},{96,0},{1,33},{33,65},{65,97},{97,1},{2,34}... | collective-permute-start | bytes 786440 | tf_op jit(solution)/shard_map/ppermute | solution.py:186
  20.7 2.1 %collective-permute-start.5 = (bf16[128,1024]{1,0:T(8,128)(2,1)S(1)}, bf16[128,1024]{1,0:T(8,128)(2,1)S(1)}, u32[]{:S(2)}, u32[]{:S(2)}) collective-permute-start(bf16[128,1024]{1,0:T(8,128)(2,1)S(1)} %shard_map.167.refs_0_), channel_id=1, source_target_pairs={{0,96},{32,0},{64,32},{96,64},{1,97},{33,1},{65,33},{97,65},{2,98}... | collective-permute-start | bytes 786440 | tf_op jit(solution)/shard_map/ppermute | solution.py:186
  22.9 0.0 copy-start.2
  22.9 0.7 copy-done.2
  23.6 4.6 %collective-permute-done.4.refs_0_ = bf16[1024,512]{1,0:T(8,128)(2,1)} collective-permute-done((bf16[1024,512]{1,0:T(8,128)(2,1)}, bf16[1024,512]{1,0:T(8,128)(2,1)}, u32[]{:S(2)}, u32[]{:S(2)}) %collective-permute-start.4) | collective-permute-done | bytes 1048608 | tf_op jit(solution)/shard_map/ppermute | solution.py:182
  28.2 0.0 copy-start.3
  28.2 0.9 collective-permute-done.2.refs_1_
  29.1 0.0 collective-permute-done.5.refs_2_
  29.1 0.0 collective-permute-start.6
  29.1 1.3 collective-permute-start.3
  30.4 1.6 %collective-permute-done.6.refs_6_.refs_4_ = bf16[1024,512]{1,0:T(8,128)(2,1)S(1)} collective-permute-done((bf16[1024,512]{1,0:T(8,128)(2,1)}, bf16[1024,512]{1,0:T(8,128)(2,1)S(1)}, u32[]{:S(2)}, u32[]{:S(2)}) %collective-permute-start.6) | collective-permute-done | bytes 1048608 | tf_op jit(solution)/shard_map/ppermute | solution.py:182
  32.0 0.0 copy-done
  32.0 0.0 copy-done.3
  32.0 4.1 %shard_map.169.refs_5_ = bf16[16,64,1024]{2,1,0:T(8,128)(2,1)} custom-call(bf16[128,1024]{1,0:T(8,128)(2,1)S(1)} %copy-done.3, bf16[128,1024]{1,0:T(8,128)(2,1)S(1)} %collective-permute-done.2.refs_1_, bf16[128,1024]{1,0:T(8,128)(2,1)S(1)} %collective-permute-done.5.refs_2_, bf16[1024,512]{1,0:T(8,128)(2,1)S(1)} %copy-done, ...), custom_call_target="tpu_custom_call" | custom-call | flops 4000000000 | bytes 1024 | tf_op jit(solution)/shard_map/pallas_call | solution.py:249
  36.1 3.3 %collective-permute-done.3.refs_0_ = bf16[128,1024]{1,0:T(8,128)(2,1)S(1)} collective-permute-done((bf16[128,1024]{1,0:T(8,128)(2,1)S(1)}, bf16[128,1024]{1,0:T(8,128)(2,1)S(1)}, u32[]{:S(2)}, u32[]{:S(2)}) %collective-permute-start.3) | collective-permute-done | bytes 262176 | tf_op jit(solution)/shard_map/ppermute | solution.py:186
  39.4 3.1 %shard_map.170 = bf16[16,64,1024]{2,1,0:T(8,128)(2,1)} custom-call(bf16[128,1024]{1,0:T(8,128)(2,1)S(1)} %collective-permute-done.3.refs_0_, bf16[1024,512]{1,0:T(8,128)(2,1)S(1)} %copy-done, bf16[1024,512]{1,0:T(8,128)(2,1)} %collective-permute-done.1.refs_2_.refs_4_, bf16[1024,512]{1,0:T(8,128)(2,1)} %shard_map.168.refs_5_.refs_3_, ...), custom_call_target="tpu_custom_call", output_to_operand_aliasing={{}: (5, {})} | custom-call | bytes 1024 | tf_op jit(solution)/shard_map/pallas_call | solution.py:249
  42.5 0.0 copy-start.7
  42.5 0.0 copy-start.13
  42.5 7.2 %all-to-all-start = ((bf16[16,64,1024]{2,1,0:T(8,128)(2,1)}), bf16[16,64,1024]{2,1,0:T(8,128)(2,1)S(1)}, u32[]{:S(2)}, u32[]{:S(2)}) async-start(bf16[16,64,1024]{2,1,0:T(8,128)(2,1)} %shard_map.170), calls=%async_computation | async-start | bytes 4194304 | tf_op jit(solution)/shard_map/all_to_all | solution.py:507
  49.7 0.0 copy-done.7
  49.7 0.0 copy-done.13
  49.8 0.0 copy-start.9
  49.8 0.1 collective-permute-start.7
  49.9 1.3 %collective-permute-done.7.extra = bf16[144,512]{1,0:T(8,128)(2,1)S(1)} collective-permute-done((bf16[144,512]{1,0:T(8,128)(2,1)S(1)}, bf16[144,512]{1,0:T(8,128)(2,1)S(1)}, u32[]{:S(2)}, u32[]{:S(2)}) %collective-permute-start.7) | collective-permute-done | bytes 147488 | tf_op jit(solution)/shard_map/ppermute | solution.py:182
  51.2 0.0 copy-start.8
  51.3 2.0 %collective-permute-start.8 = (bf16[64,1024]{1,0:T(8,128)(2,1)S(1)}, bf16[64,1024]{1,0:T(8,128)(2,1)S(1)}, u32[]{:S(2)}, u32[]{:S(2)}) collective-permute-start(bf16[64,1024]{1,0:T(8,128)(2,1)S(1)} %pad_maximum_fusion.1), channel_id=1, source_target_pairs={{0,1},{1,0},{2,3},{3,2},{4,5},{5,4},{6,7},{7,6},{8,9},{9,8},{10,11... | collective-permute-start | bytes 393224 | tf_op jit(solution)/shard_map/ppermute | solution.py:182
  53.3 24.0 %collective-permute-done.8.res_y = bf16[64,1024]{1,0:T(8,128)(2,1)S(1)} collective-permute-done((bf16[64,1024]{1,0:T(8,128)(2,1)S(1)}, bf16[64,1024]{1,0:T(8,128)(2,1)S(1)}, u32[]{:S(2)}, u32[]{:S(2)}) %collective-permute-start.8) | collective-permute-done | bytes 131104 | tf_op jit(solution)/shard_map/ppermute | solution.py:182
  77.2 2.8 %all-to-all-done.parts = bf16[16,64,1024]{2,1,0:T(8,128)(2,1)S(1)} async-done(((bf16[16,64,1024]{2,1,0:T(8,128)(2,1)}), bf16[16,64,1024]{2,1,0:T(8,128)(2,1)S(1)}, u32[]{:S(2)}, u32[]{:S(2)}) %all-to-all-start) | async-done | bytes 2097184 | tf_op jit(solution)/shard_map/all_to_all | solution.py:507
  80.1 0.0 copy-done.9
  80.1 0.0 copy-done.8
  80.1 0.0 copy-done.10
  80.1 0.0 copy-start.6
  80.1 1.4 %copy-done.6 = bf16[16,64,1024]{2,1,0:T(8,128)(2,1)} copy-done((bf16[16,64,1024]{2,1,0:T(8,128)(2,1)}, bf16[16,64,1024]{2,1,0:T(8,128)(2,1)S(1)}, u32[]{:S(2)}) %copy-start.6) | copy-done | bytes 2097176
  81.5 5.7 %shard_map.171 = (bf16[128,512]{1,0:T(8,128)(2,1)}, bf16[128,512]{1,0:T(8,128)(2,1)}, bf16[128,4224]{1,0:T(8,128)(2,1)}) custom-call(bf16[16,64,1024]{2,1,0:T(8,128)(2,1)} %copy-done.6, bf16[256,512]{1,0:T(8,128)(2,1)} %res.1, bf16[144,512]{1,0:T(8,128)(2,1)} %copy-done.8, bf16[64,1024]{1,0:T(8,128)(2,1)} %copy-done.10, bf16[16,512]{1,0:T(8,128)(2,1)} %copy-done.9, ...), custom_call_target="tpu_custom_call" | custom-call | flops 1024 | bytes 1024 | tf_op jit(solution)/shard_map/pallas_call | solution.py:323
  87.2 0.0 copy-start.14
  87.2 0.0 copy-start.11
  87.2 0.0 copy-start.12
  87.2 0.0 copy-start.4
  87.2 0.0 copy-start.5
  87.3 3.7 %all-to-all-start.1 = ((bf16[8,16,4224]{2,1,0:T(8,128)(2,1)}), bf16[8,16,4224]{2,1,0:T(8,128)(2,1)S(1)}, u32[]{:S(2)}, u32[]{:S(2)}) async-start(bf16[8,16,4224]{2,1,0:T(8,128)(2,1)} %bitcast.13), calls=%async_computation.1 | async-start | bytes 2162688 | tf_op jit(solution)/shard_map/all_to_all | solution.py:509
  91.0 0.0 copy-done.14
  91.0 0.1 collective-permute-start.9
  91.1 0.0 copy-done.11
  91.1 1.3 %collective-permute-done.9 = bf16[128,512]{1,0:T(8,128)(2,1)S(1)} collective-permute-done((bf16[128,512]{1,0:T(8,128)(2,1)S(1)}, bf16[128,512]{1,0:T(8,128)(2,1)S(1)}, u32[]{:S(2)}, u32[]{:S(2)}) %collective-permute-start.9) | collective-permute-done | bytes 131104 | tf_op jit(solution)/shard_map/ppermute | solution.py:182
  92.5 0.6 collective-permute-start.10
  93.1 0.0 copy-done.12
  93.1 5.0 %collective-permute-done.10 = bf16[64,1024]{1,0:T(8,128)(2,1)S(1)} collective-permute-done((bf16[64,1024]{1,0:T(8,128)(2,1)S(1)}, bf16[64,1024]{1,0:T(8,128)(2,1)S(1)}, u32[]{:S(2)}, u32[]{:S(2)}) %collective-permute-start.10) | collective-permute-done | bytes 131104 | tf_op jit(solution)/shard_map/ppermute | solution.py:182
  98.2 8.9 %all-to-all-done.1.got_hbm = bf16[8,16,4224]{2,1,0:T(8,128)(2,1)S(1)} async-done(((bf16[8,16,4224]{2,1,0:T(8,128)(2,1)}), bf16[8,16,4224]{2,1,0:T(8,128)(2,1)S(1)}, u32[]{:S(2)}, u32[]{:S(2)}) %all-to-all-start.1) | async-done | bytes 1081376 | tf_op jit(solution)/shard_map/all_to_all | solution.py:509
  107.1 0.0 copy-done.4
  107.1 0.0 copy-done.5
  107.1 1.2 shard_map.172
  108.4 6.4 %all-to-all-start.2 = ((f32[128,1,128]{2,1,0:T(1,128)}), f32[128,1,128]{2,1,0:T(1,128)S(1)}, u32[]{:S(2)}, u32[]{:S(2)}) async-start(f32[128,1,128]{2,1,0:T(1,128)} %shard_map.172), calls=%async_computation.2 | async-start | bytes 131072 | tf_op jit(solution)/shard_map/all_to_all | solution.py:524
  114.8 0.8 maximum_select_fusion.1
  115.6 8.5 %all-to-all-done.2.all_hbm = f32[128,1,128]{2,1,0:T(1,128)S(1)} async-done(((f32[128,1,128]{2,1,0:T(1,128)}), f32[128,1,128]{2,1,0:T(1,128)S(1)}, u32[]{:S(2)}, u32[]{:S(2)}) %all-to-all-start.2) | async-done | bytes 65568 | tf_op jit(solution)/shard_map/all_to_all | solution.py:524
  124.1 2.6 %shard_map.173 = (f32[2,128]{1,0:T(2,128)}, f32[16,32]{1,0:T(8,128)}) custom-call(f32[128,1,128]{2,1,0:T(1,128)S(1)} %all-to-all-done.2.all_hbm), custom_call_target="tpu_custom_call" | custom-call | flops 1024 | bytes 1024 | tf_op jit(solution)/shard_map/pallas_call | solution.py:441
  (15 shorter events, 0.2 us)
Async XLA Ops:
  0.6 17.2 %collective-permute-start = (bf16[512,4096]{1,0:T(8,128)(2,1)}, bf16[512,4096]{1,0:T(8,128)(2,1)}, u32[]{:S(2)}, u32[]{:S(2)}) collective-permute-start(bf16[512,4096]{1,0:T(8,128)(2,1)} %up_mine.1), channel_id=1, source_target_pairs={{0,8},{8,0},{1,9},{9,1},{2,10},{10,2},{3,11},{11,3},{4,12},{12,4},... | collective-permute-start | bytes 12582920 | tf_op jit(solution)/shard_map/ppermute | solution.py:182
  0.7 17.1 %collective-permute-start.1 = (bf16[1024,512]{1,0:T(8,128)(2,1)}, bf16[1024,512]{1,0:T(8,128)(2,1)}, u32[]{:S(2)}, u32[]{:S(2)}) collective-permute-start(bf16[1024,512]{1,0:T(8,128)(2,1)} %refs_1_.1), channel_id=1, source_target_pairs={{0,8},{8,0},{1,9},{9,1},{2,10},{10,2},{3,11},{11,3},{4,12},{12,4},... | collective-permute-start | bytes 3145736 | tf_op jit(solution)/shard_map/ppermute | solution.py:182
  1.2 27.0 %collective-permute-start.4 = (bf16[1024,512]{1,0:T(8,128)(2,1)}, bf16[1024,512]{1,0:T(8,128)(2,1)}, u32[]{:S(2)}, u32[]{:S(2)}) collective-permute-start(bf16[1024,512]{1,0:T(8,128)(2,1)} %refs_1_.1), channel_id=1, source_target_pairs={{0,16},{16,0},{1,17},{17,1},{2,18},{18,2},{3,19},{19,3},{4,20},{20... | collective-permute-start | bytes 3145736 | tf_op jit(solution)/shard_map/ppermute | solution.py:182
  17.9 1.0 copy-start.1
  18.8 13.2 %copy-start = (bf16[1024,512]{1,0:T(8,128)(2,1)S(1)}, bf16[1024,512]{1,0:T(8,128)(2,1)}, u32[]{:S(2)}) copy-start(bf16[1024,512]{1,0:T(8,128)(2,1)} %refs_1_.1) | copy-start | bytes 3145732
  18.8 10.3 %collective-permute-start.2 = (bf16[128,1024]{1,0:T(8,128)(2,1)S(1)}, bf16[128,1024]{1,0:T(8,128)(2,1)S(1)}, u32[]{:S(2)}, u32[]{:S(2)}) collective-permute-start(bf16[128,1024]{1,0:T(8,128)(2,1)S(1)} %shard_map.167.refs_0_), channel_id=1, source_target_pairs={{0,32},{32,64},{64,96},{96,0},{1,33},{33,65},{65,97},{97,1},{2,34}... | collective-permute-start | bytes 786440 | tf_op jit(solution)/shard_map/ppermute | solution.py:186
  20.7 8.4 %collective-permute-start.5 = (bf16[128,1024]{1,0:T(8,128)(2,1)S(1)}, bf16[128,1024]{1,0:T(8,128)(2,1)S(1)}, u32[]{:S(2)}, u32[]{:S(2)}) collective-permute-start(bf16[128,1024]{1,0:T(8,128)(2,1)S(1)} %shard_map.167.refs_0_), channel_id=1, source_target_pairs={{0,96},{32,0},{64,32},{96,64},{1,97},{33,1},{65,33},{97,65},{2,98}... | collective-permute-start | bytes 786440 | tf_op jit(solution)/shard_map/ppermute | solution.py:186
  22.9 0.7 copy-start.2
  28.2 3.8 %copy-start.3 = (bf16[128,1024]{1,0:T(8,128)(2,1)S(1)}, bf16[128,1024]{1,0:T(8,128)(2,1)}, u32[]{:S(2)}) copy-start(bf16[128,1024]{1,0:T(8,128)(2,1)} %copy-done.2) | copy-start | bytes 786436
  29.1 2.9 %collective-permute-start.6 = (bf16[1024,512]{1,0:T(8,128)(2,1)}, bf16[1024,512]{1,0:T(8,128)(2,1)S(1)}, u32[]{:S(2)}, u32[]{:S(2)}) collective-permute-start(bf16[1024,512]{1,0:T(8,128)(2,1)} %shard_map.168.refs_5_.refs_3_), channel_id=1, source_target_pairs={{0,8},{8,0},{1,9},{9,1},{2,10},{10,2},{3,11},{11,3},{4,12},{12,4},... | collective-permute-start | bytes 3145736 | tf_op jit(solution)/shard_map/ppermute | solution.py:182
  29.1 10.3 %collective-permute-start.3 = (bf16[128,1024]{1,0:T(8,128)(2,1)S(1)}, bf16[128,1024]{1,0:T(8,128)(2,1)S(1)}, u32[]{:S(2)}, u32[]{:S(2)}) collective-permute-start(bf16[128,1024]{1,0:T(8,128)(2,1)S(1)} %collective-permute-done.2.refs_1_), channel_id=1, source_target_pairs={{0,32},{32,64},{64,96},{96,0},{1,33},{33,65},{65,97},{97,1},{2,34}... | collective-permute-start | bytes 786440 | tf_op jit(solution)/shard_map/ppermute | solution.py:186
  42.5 7.2 %copy-start.7 = (bf16[256,512]{1,0:T(8,128)(2,1)S(1)}, bf16[256,512]{1,0:T(8,128)(2,1)}, u32[]{:S(2)}) copy-start(bf16[256,512]{1,0:T(8,128)(2,1)} %res.1) | copy-start | bytes 786436
  42.5 7.2 %copy-start.13 = (bf16[512]{0:T(512)(128)(2,1)S(1)}, bf16[512]{0:T(512)(128)(2,1)}, u32[]{:S(2)}) copy-start(bf16[512]{0:T(512)(128)(2,1)} %param.27) | copy-start | bytes 3076
  42.5 37.6 %all-to-all-start = ((bf16[16,64,1024]{2,1,0:T(8,128)(2,1)}), bf16[16,64,1024]{2,1,0:T(8,128)(2,1)S(1)}, u32[]{:S(2)}, u32[]{:S(2)}) async-start(bf16[16,64,1024]{2,1,0:T(8,128)(2,1)} %shard_map.170), calls=%async_computation | async-start | bytes 4194304 | tf_op jit(solution)/shard_map/all_to_all | solution.py:507
  49.8 30.3 %copy-start.9 = (bf16[16,512]{1,0:T(8,128)(2,1)}, bf16[16,512]{1,0:T(8,128)(2,1)S(1)}, u32[]{:S(2)}) copy-start(bf16[16,512]{1,0:T(8,128)(2,1)S(1)} %broadcast_in_dim.2.gain) | copy-start | bytes 49156
  49.8 1.5 %collective-permute-start.7 = (bf16[144,512]{1,0:T(8,128)(2,1)S(1)}, bf16[144,512]{1,0:T(8,128)(2,1)S(1)}, u32[]{:S(2)}, u32[]{:S(2)}) collective-permute-start(bf16[144,512]{1,0:T(8,128)(2,1)S(1)} %pad_maximum_fusion), channel_id=1, source_target_pairs={{0,8},{8,0},{1,9},{9,1},{2,10},{10,2},{3,11},{11,3},{4,12},{12,4},... | collective-permute-start | bytes 442376 | tf_op jit(solution)/shard_map/ppermute | solution.py:182
  51.2 28.9 %copy-start.8 = (bf16[144,512]{1,0:T(8,128)(2,1)}, bf16[144,512]{1,0:T(8,128)(2,1)S(1)}, u32[]{:S(2)}) copy-start(bf16[144,512]{1,0:T(8,128)(2,1)S(1)} %collective-permute-done.7.extra) | copy-start | bytes 442372
  51.3 26.0 %collective-permute-start.8 = (bf16[64,1024]{1,0:T(8,128)(2,1)S(1)}, bf16[64,1024]{1,0:T(8,128)(2,1)S(1)}, u32[]{:S(2)}, u32[]{:S(2)}) collective-permute-start(bf16[64,1024]{1,0:T(8,128)(2,1)S(1)} %pad_maximum_fusion.1), channel_id=1, source_target_pairs={{0,1},{1,0},{2,3},{3,2},{4,5},{5,4},{6,7},{7,6},{8,9},{9,8},{10,11... | collective-permute-start | bytes 393224 | tf_op jit(solution)/shard_map/ppermute | solution.py:182
  77.2 2.9 %copy-start.10 = (bf16[64,1024]{1,0:T(8,128)(2,1)}, bf16[64,1024]{1,0:T(8,128)(2,1)S(1)}, u32[]{:S(2)}) copy-start(bf16[64,1024]{1,0:T(8,128)(2,1)S(1)} %collective-permute-done.8.res_y) | copy-start | bytes 393220
  80.1 1.4 %copy-start.6 = (bf16[16,64,1024]{2,1,0:T(8,128)(2,1)}, bf16[16,64,1024]{2,1,0:T(8,128)(2,1)S(1)}, u32[]{:S(2)}) copy-start(bf16[16,64,1024]{2,1,0:T(8,128)(2,1)S(1)} %all-to-all-done.parts) | copy-start | bytes 6291460
  87.2 3.8 %copy-start.14 = (bf16[128,512]{1,0:T(8,128)(2,1)S(1)}, bf16[128,512]{1,0:T(8,128)(2,1)}, u32[]{:S(2)}) copy-start(bf16[128,512]{1,0:T(8,128)(2,1)} %get-tuple-element.9) | copy-start | bytes 393220
  87.2 3.9 %copy-start.11 = (bf16[128,512]{1,0:T(8,128)(2,1)S(1)}, bf16[128,512]{1,0:T(8,128)(2,1)}, u32[]{:S(2)}) copy-start(bf16[128,512]{1,0:T(8,128)(2,1)} %get-tuple-element.8) | copy-start | bytes 393220
  87.2 5.9 %copy-start.12 = (bf16[4096]{0:T(1024)(128)(2,1)S(1)}, bf16[4096]{0:T(1024)(128)(2,1)}, u32[]{:S(2)}) copy-start(bf16[4096]{0:T(1024)(128)(2,1)} %param.29) | copy-start | bytes 24580
  87.2 19.9 %copy-start.4 = (s32[128]{0:T(128)S(1)}, s32[128]{0:T(128)}, u32[]{:S(2)}) copy-start(s32[128]{0:T(128)} %ids_hbm.1) | copy-start | bytes 1540
  87.2 19.9 %copy-start.5 = (s32[128]{0:T(128)S(1)}, s32[128]{0:T(128)}, u32[]{:S(2)}) copy-start(s32[128]{0:T(128)} %param.24) | copy-start | bytes 1540
  87.3 19.9 %all-to-all-start.1 = ((bf16[8,16,4224]{2,1,0:T(8,128)(2,1)}), bf16[8,16,4224]{2,1,0:T(8,128)(2,1)S(1)}, u32[]{:S(2)}, u32[]{:S(2)}) async-start(bf16[8,16,4224]{2,1,0:T(8,128)(2,1)} %bitcast.13), calls=%async_computation.1 | async-start | bytes 2162688 | tf_op jit(solution)/shard_map/all_to_all | solution.py:509
  91.0 1.4 %collective-permute-start.9 = (bf16[128,512]{1,0:T(8,128)(2,1)S(1)}, bf16[128,512]{1,0:T(8,128)(2,1)S(1)}, u32[]{:S(2)}, u32[]{:S(2)}) collective-permute-start(bf16[128,512]{1,0:T(8,128)(2,1)S(1)} %copy-done.14), channel_id=1, source_target_pairs={{0,8},{8,0},{1,9},{9,1},{2,10},{10,2},{3,11},{11,3},{4,12},{12,4},... | collective-permute-start | bytes 393224 | tf_op jit(solution)/shard_map/ppermute | solution.py:182
  92.5 5.6 %collective-permute-start.10 = (bf16[64,1024]{1,0:T(8,128)(2,1)S(1)}, bf16[64,1024]{1,0:T(8,128)(2,1)S(1)}, u32[]{:S(2)}, u32[]{:S(2)}) collective-permute-start(bf16[64,1024]{1,0:T(8,128)(2,1)S(1)} %pad_maximum_fusion.2), channel_id=1, source_target_pairs={{0,1},{1,0},{2,3},{3,2},{4,5},{5,4},{6,7},{7,6},{8,9},{9,8},{10,11... | collective-permute-start | bytes 393224 | tf_op jit(solution)/shard_map/ppermute | solution.py:182
  108.4 15.7 %all-to-all-start.2 = ((f32[128,1,128]{2,1,0:T(1,128)}), f32[128,1,128]{2,1,0:T(1,128)S(1)}, u32[]{:S(2)}, u32[]{:S(2)}) async-start(f32[128,1,128]{2,1,0:T(1,128)} %shard_map.172), calls=%async_computation.2 | async-start | bytes 131072 | tf_op jit(solution)/shard_map/all_to_all | solution.py:524

commit v4 on v3

--- a/solution.py
+++ b/solution.py
@@ -198,7 +198,7 @@
     pass
 
 
-def hold(x, *tokens):
+def hold(x, *tokens, mib=4):
     A = pl.BlockSpec(memory_space=pl.ANY)
     return pl.pallas_call(
         hold_kernel,
@@ -206,7 +206,7 @@
         in_specs=[A] * (1 + len(tokens)),
         out_specs=A,
         input_output_aliases={0: 0},
-        **tiny(4),
+        **tiny(mib),
     )(x, *tokens)
 
 
@@ -257,12 +257,12 @@
             pltpu.VMEM((2, count, 2, 64, 1024), BF),
             pltpu.SemaphoreType.DMA((4 + 2 * count,)),
         ],
-        **tiny(40, 0 if more else 4 * 10**9),
+        **tiny(48, 0),
     )(*ins)
 
 
 def up_kernel(
-    parts, res, extra, res_y, gain, up_mine, up_par,
+    parts, res, extra, res_y, gain, gain_par, up_mine, up_par,
     hm_ref, hp_ref, sent_ref, parts_v, res_v, gain_v, gain2_v, w, sems,
 ):
     c = lax.axis_index("c")
@@ -276,7 +276,7 @@
             (res.at[pl.ds(pl.multiple_of(c * 128 + yl * 64, 64), 64)], res_v.at[here, :512]),
             (extra.at[here], res_v.at[here, 512:]),
             (res_y, res_v.at[there]),
-            (gain, gain_v), (extra.at[128:], gain2_v),
+            (gain, gain_v), (gain_par, gain2_v),
         ))
     ]
     for copy in small:
@@ -327,7 +327,7 @@
             jax.ShapeDtypeStruct((128, 512), BF),
             jax.ShapeDtypeStruct((128, 4096 + 128), BF),
         ),
-        in_specs=[A] * 7,
+        in_specs=[A] * 8,
         out_specs=(V, V, V),
         scratch_shapes=[
             pltpu.VMEM((16, 64, 1024), BF),
@@ -337,7 +337,7 @@
             pltpu.VMEM((1024, 4096), BF),
             pltpu.SemaphoreType.DMA((4, 4)),
         ],
-        **tiny(58),
+        **tiny(48),
     )(*ins)
 
 
@@ -398,15 +398,21 @@
     )(got, head_weight.reshape(1, 4096), prompt_ids.reshape(1, 128), cluster_ids.reshape(1, 128))
 
 
-def vote_kernel(all_hbm, scores_ref, votes_ref, x3, x, sem):
+def vote_kernel(all_hbm, scores_ref, votes_ref, x3, x, vals, ids, votes, sem):
     copy = pltpu.make_async_copy(all_hbm, x3, sem)
     copy.start()
     copy.wait()
     x[...] = x3[...].reshape(128, 128)
     t = lax.axis_index(TP)
     lane8 = lax.broadcasted_iota(jnp.int32, (8, 128), 1)
-    lane = lax.broadcasted_iota(jnp.int32, (16, 32), 1)
-    row = lax.broadcasted_iota(jnp.int32, (16, 32), 0)
+    row8 = lax.broadcasted_iota(jnp.int32, (8, 128), 0)
+    lane = lax.broadcasted_iota(jnp.int32, (16, 128), 1)
+    place = lane8 // 16 == row8
+
+    def line(block, first):
+        front = pltpu.roll(block, 128 - first, 1) if first else block
+        rolled = pltpu.roll(front, 0, 1, stride=16, stride_axis=0)
+        return jnp.sum(jnp.where(place, rolled, 0.0), axis=0, keepdims=True)
 
     def scores_of(zx, c):
         base = (zx & 1) * 64 + c * 8 + (zx >> 1) * 2
@@ -415,24 +421,20 @@
         )
 
     for c in range(2):
-        block = jnp.where(lane8 < 16, scores_of(t, c), 0.0)
-        spread = block[0:1]
-        for i in range(1, 8):
-            spread = spread + pltpu.roll(block, 16 * i, 1)[i : i + 1]
-        scores_ref[c : c + 1, :] = spread
-    live = (lane8 >= 16) & (lane8 < 32)
-    votes = jnp.zeros((16, 32), F32)
+        scores_ref[c : c + 1, :] = line(scores_of(t, c), 0)
     for zx in range(8):
         for c in range(2):
             dp = zx * 2 + c
-            ids = jnp.where(live, x[dp * 8 : dp * 8 + 8, :], -1.0)
-            vals = pltpu.roll(scores_of(zx, c), 16, 1)
-            for p in range(2):
-                for k in range(CLUSTERS):
-                    hit = jnp.where(ids == float(p * CLUSTERS + k), vals, 0.0)
-                    one = jnp.sum(jnp.sum(hit, axis=0, keepdims=True), axis=1, keepdims=True)
-                    votes = jnp.where((row == k) & (lane == dp * 2 + p), one, votes)
-    votes_ref[...] = votes
+            vals[dp : dp + 1, :] = line(scores_of(zx, c), 0)
+            ids[dp : dp + 1, :] = line(x[dp * 8 : dp * 8 + 8, :], 16)
+    votes[...] = jnp.zeros((128, 128), F32)
+    for p in range(2):
+        acc = jnp.zeros((16, 128), F32)
+        for k in range(CLUSTERS):
+            hit = jnp.where(ids[...] == float(p * CLUSTERS + k), vals[...], 0.0)
+            acc = jnp.where(lane == k, jnp.sum(hit, axis=1, keepdims=True), acc)
+        votes[pl.ds(p, 16, stride=2), :] = acc
+    votes_ref[...] = votes[...].T[:CLUSTERS, :32]
 
 
 def tally(everyone):
@@ -443,7 +445,14 @@
         out_shape=(jax.ShapeDtypeStruct((2, 128), F32), jax.ShapeDtypeStruct((CLUSTERS, 32), F32)),
         in_specs=[A],
         out_specs=(V, V),
-        scratch_shapes=[pltpu.VMEM((128, 1, 128), F32), pltpu.VMEM((128, 128), F32), pltpu.SemaphoreType.DMA],
+        scratch_shapes=[
+            pltpu.VMEM((128, 1, 128), F32),
+            pltpu.VMEM((128, 128), F32),
+            pltpu.VMEM((16, 128), F32),
+            pltpu.VMEM((16, 128), F32),
+            pltpu.VMEM((128, 128), F32),
+            pltpu.SemaphoreType.DMA,
+        ],
         **tiny(40),
     )(everyone)
 
@@ -487,25 +496,27 @@
         prompt_ids,
     )
 
-    part = hold(part, up_par, w01)
+    part = hold(part, up_par, w01, mib=63)
     before, after = shift(part, 1), shift(part, 3)
     far = shift(before, 1)
     gain = jnp.broadcast_to(norm_gain[None, :], (16, 512))
-    extra = swap(jnp.concatenate([rows_of(residual, (1 - c) * 128, 128), gain], axis=0), "c")
+    gain_par = swap(gain, "c")
+    later = hold(residual, part)
+    extra = swap(rows_of(later, (1 - c) * 128, 128), "c")
     res_y = swap(
         jnp.concatenate(
-            [rows_of(residual, c * 128 + (1 - yl) * 64, 64), rows_of(extra, (1 - yl) * 64, 64)], axis=1
+            [rows_of(later, c * 128 + (1 - yl) * 64, 64), rows_of(extra, (1 - yl) * 64, 64)], axis=1
         ),
         "yl",
     )
-    w10 = hold(w10, before, after)
+    w10 = hold(w10, before, after, res_y)
     w11 = swap(w10, "c")
 
     weights = (out_weight, w01, w10, w11)
     partial = project((0, 1, 3), part, before, after, *weights)
     partial = project((2,), far, *weights, partial)
     parts = lax.all_to_all(partial, ("xh", "xl", "yh", "yl"), 0, 0, tiled=True)
-    hid_mine, hid_par, sent = verify_up(parts, residual, extra, res_y, gain, up_weight, up_par)
+    hid_mine, hid_par, sent = verify_up(parts, residual, extra, res_y, gain, gain_par, up_weight, up_par)
     got = lax.all_to_all(sent.reshape(8, 16, 4096 + 128), ("z", "xh"), 0, 0, tiled=True)
 
     hid_back = swap(hid_par, "c")

time: 128 us -> 122 us (0.953)
  starting transfers between devices: 29.1 us -> 26.2 us
  local copies, waits for them, and re-layouts: 3.18 us -> 1.09 us
  Pallas kernels: 30.2 us -> 28.5 us
    all_to_all x1, waiting for transfers between devices: 2.85 us -> 29.1 us  [body(): parts = lax.all_to_all(partial, ('xh', 'xl', 'yh', 'yl'), 0, 0, tiled=True)]
    ppermute x8 -> x9, waiting for transfers between devices: 37.9 us -> 12.9 us  [swap(): return lax.ppermute(x, axis, [(0, 1), (1, 0)])]
    unnamed x30 -> x17, local copies, waits for them, and re-layouts: 3.08 us -> 1 us
    all_to_all x1, starting transfers between devices: 6.44 us -> 4.59 us  [body(): scores, votes = tally(lax.all_to_all(line, AXES, 0, 0, tiled=True))]
    pallas_call x1, Pallas kernels: 2.58 us -> 1.06 us  [tally(): pl.pallas_call(vote_kernel, out_shape=(jax.ShapeDtypeStruct((2, 128), F32...]
    ppermute x8 -> x9, starting transfers between devices: 6.47 us -> 6.24 us  [swap(): return lax.ppermute(x, axis, [(0, 1), (1, 0)])]
  transfers between devices with their start and end apart: 14 -> 15, of which waited for: 11 -> 11; matrix products, arithmetic and copies ran while one was open for 1% -> 1% of each run, Pallas kernels for 14% -> 15%
where the time goes in v4:
time: 122 us; the launch traced here: 120 us
  waiting for transfers between devices  62.9 us (52%)
  Pallas kernels  28.5 us (23%)
  starting transfers between devices  26.2 us (21%)
    all_to_all x1, waiting for transfers between devices, body(): parts = lax.all_to_all(partial, ('xh', 'xl', 'yh', 'yl'), 0, 0, tiled=True)  29.1 us
    pallas_call x1, Pallas kernels, attend(): pl.pallas_call(functools.partial(attn_kernel, rows, tile), out_shape=jax....  13.6 us
    ppermute x9, waiting for transfers between devices, swap(): return lax.ppermute(x, axis, [(0, 1), (1, 0)])  12.9 us
    all_to_all x1, waiting for transfers between devices, body(): scores, votes = tally(lax.all_to_all(line, AXES, 0, 0, tiled=True))  8.51 us
    all_to_all x1, waiting for transfers between devices, body(): lax.all_to_all(sent.reshape(8, 16, 4096 + 128), ('z', 'xh'), 0, 0, tiled=...  7.96 us
    pallas_call x2, Pallas kernels, project(): pl.pallas_call(functools.partial(proj_kernel, steps), out_shape=jax.Shape...  7.19 us
    ppermute x9, starting transfers between devices, swap(): return lax.ppermute(x, axis, [(0, 1), (1, 0)])  6.24 us
    all_to_all x1, starting transfers between devices, body(): parts = lax.all_to_all(partial, ('xh', 'xl', 'yh', 'yl'), 0, 0, tiled=True)  6.18 us
  transfers between devices with their start and end apart: 15, of which 11 were waited for; matrix products, arithmetic and copies ran while one was open for 1% of the time, Pallas kernels for 15%

profile of v4, /device:TPU:0, one launch (start us, length us, event | category | flops | bytes accessed | tf_op | source)
XLA Modules:
  0.0 120.4 jit_solution(16117389730861393751)
XLA Ops:
  0.6 0.1 collective-permute-start
  0.7 0.5 collective-permute-start.1
  1.2 3.1 %collective-permute-start.4 = (bf16[1024,512]{1,0:T(8,128)(2,1)}, bf16[1024,512]{1,0:T(8,128)(2,1)}, u32[]{:S(2)}, u32[]{:S(2)}) collective-permute-start(bf16[1024,512]{1,0:T(8,128)(2,1)} %refs_1_.1), channel_id=1, source_target_pairs={{0,16},{16,0},{1,17},{17,1},{2,18},{18,2},{3,19},{19,3},{4,20},{20... | collective-permute-start | bytes 3145736 | tf_op jit(solution)/shard_map/ppermute | solution.py:182
  4.3 0.0 copy-start.3
  4.3 13.6 %shard_map.166.refs_0_ = bf16[128,1024]{1,0:T(8,128)(2,1)} custom-call(s32[128]{0:T(128)} %ids_hbm.1, s32[1,128]{1,0:T(1,128)} %bitcast.10, s32[1,128]{1,0:T(1,128)} %bitcast.19, bf16[128,1024]{1,0:T(8,128)(2,1)} %q_hbm.1, bf16[128,128]{1,0:T(8,128)(2,1)} %nk_hbm.1, bf16[128,128]{1,0:T(8,128)(2,1)} %nv_hbm.1, bf16[2,2048,128]{2,1,0:T(8,128)(2,1)} %bitcast.15, ...), custom_call_target="tpu_custom_call" | custom-call | flops 16000000000 | bytes 11534336 | tf_op jit(solution)/shard_map/pallas_call | solution.py:159
  18.0 0.0 copy-done.3
  18.0 0.0 collective-permute-done.1.refs_2_.refs_4_
  18.0 0.0 collective-permute-done.refs_1_.up_par
  18.0 0.0 copy-start.1
  18.1 0.9 copy-done.1
  19.0 0.0 copy-start
  19.0 0.0 copy-start.2
  19.0 0.1 collective-permute-start.6
  19.1 2.0 %collective-permute-start.2 = (bf16[128,1024]{1,0:T(8,128)(2,1)}, bf16[128,1024]{1,0:T(8,128)(2,1)S(1)}, u32[]{:S(2)}, u32[]{:S(2)}) collective-permute-start(bf16[128,1024]{1,0:T(8,128)(2,1)} %shard_map.167.refs_1_.refs_0_), channel_id=1, source_target_pairs={{0,32},{32,64},{64,96},{96,0},{1,33},{33,65},{65,97},{97,1},{2,34}... | collective-permute-start | bytes 786440 | tf_op jit(solution)/shard_map/ppermute | solution.py:186
  21.1 2.2 %collective-permute-start.5 = (bf16[128,1024]{1,0:T(8,128)(2,1)}, bf16[128,1024]{1,0:T(8,128)(2,1)S(1)}, u32[]{:S(2)}, u32[]{:S(2)}) collective-permute-start(bf16[128,1024]{1,0:T(8,128)(2,1)} %shard_map.167.refs_1_.refs_0_), channel_id=1, source_target_pairs={{0,96},{32,0},{64,32},{96,64},{1,97},{33,1},{65,33},{97,65},{2,98}... | collective-permute-start | bytes 786440 | tf_op jit(solution)/shard_map/ppermute | solution.py:186
  23.3 0.0 collective-permute-done.6.extra
  23.4 1.6 %collective-permute-start.7 = (bf16[64,1024]{1,0:T(8,128)(2,1)S(1)}, bf16[64,1024]{1,0:T(8,128)(2,1)S(1)}, u32[]{:S(2)}, u32[]{:S(2)}) collective-permute-start(bf16[64,1024]{1,0:T(8,128)(2,1)S(1)} %pad_maximum_fusion), channel_id=1, source_target_pairs={{0,1},{1,0},{2,3},{3,2},{4,5},{5,4},{6,7},{7,6},{8,9},{9,8},{10,11... | collective-permute-start | bytes 393224 | tf_op jit(solution)/shard_map/ppermute | solution.py:182
  25.0 3.2 %collective-permute-done.4.refs_0_ = bf16[1024,512]{1,0:T(8,128)(2,1)} collective-permute-done((bf16[1024,512]{1,0:T(8,128)(2,1)}, bf16[1024,512]{1,0:T(8,128)(2,1)}, u32[]{:S(2)}, u32[]{:S(2)}) %collective-permute-start.4) | collective-permute-done | bytes 1048608 | tf_op jit(solution)/shard_map/ppermute | solution.py:182
  28.2 0.7 collective-permute-done.7.refs_3_.res_y
  28.9 1.4 %collective-permute-done.2.refs_1_ = bf16[128,1024]{1,0:T(8,128)(2,1)S(1)} collective-permute-done((bf16[128,1024]{1,0:T(8,128)(2,1)}, bf16[128,1024]{1,0:T(8,128)(2,1)S(1)}, u32[]{:S(2)}, u32[]{:S(2)}) %collective-permute-start.2) | collective-permute-done | bytes 262176 | tf_op jit(solution)/shard_map/ppermute | solution.py:186
  30.3 0.0 collective-permute-done.5.refs_2_
  30.3 0.0 collective-permute-start.8
  30.3 1.3 %collective-permute-start.3 = (bf16[128,1024]{1,0:T(8,128)(2,1)S(1)}, bf16[128,1024]{1,0:T(8,128)(2,1)S(1)}, u32[]{:S(2)}, u32[]{:S(2)}) collective-permute-start(bf16[128,1024]{1,0:T(8,128)(2,1)S(1)} %collective-permute-done.2.refs_1_), channel_id=1, source_target_pairs={{0,32},{32,64},{64,96},{96,0},{1,33},{33,65},{65,97},{97,1},{2,34}... | collective-permute-start | bytes 786440 | tf_op jit(solution)/shard_map/ppermute | solution.py:186
  31.6 1.6 %collective-permute-done.8.refs_6_.refs_4_ = bf16[1024,512]{1,0:T(8,128)(2,1)S(1)} collective-permute-done((bf16[1024,512]{1,0:T(8,128)(2,1)}, bf16[1024,512]{1,0:T(8,128)(2,1)S(1)}, u32[]{:S(2)}, u32[]{:S(2)}) %collective-permute-start.8) | collective-permute-done | bytes 1048608 | tf_op jit(solution)/shard_map/ppermute | solution.py:182
  33.2 0.0 copy-done
  33.2 0.0 copy-done.2
  33.2 4.1 %shard_map.170.refs_5_ = bf16[16,64,1024]{2,1,0:T(8,128)(2,1)} custom-call(bf16[128,1024]{1,0:T(8,128)(2,1)S(1)} %copy-done.2, bf16[128,1024]{1,0:T(8,128)(2,1)S(1)} %collective-permute-done.2.refs_1_, bf16[128,1024]{1,0:T(8,128)(2,1)S(1)} %collective-permute-done.5.refs_2_, bf16[1024,512]{1,0:T(8,128)(2,1)S(1)} %copy-done, ...), custom_call_target="tpu_custom_call" | custom-call | bytes 1024 | tf_op jit(solution)/shard_map/pallas_call | solution.py:249
  37.3 2.9 %collective-permute-done.3.refs_0_ = bf16[128,1024]{1,0:T(8,128)(2,1)S(1)} collective-permute-done((bf16[128,1024]{1,0:T(8,128)(2,1)S(1)}, bf16[128,1024]{1,0:T(8,128)(2,1)S(1)}, u32[]{:S(2)}, u32[]{:S(2)}) %collective-permute-start.3) | collective-permute-done | bytes 262176 | tf_op jit(solution)/shard_map/ppermute | solution.py:186
  40.3 3.1 %shard_map.171 = bf16[16,64,1024]{2,1,0:T(8,128)(2,1)} custom-call(bf16[128,1024]{1,0:T(8,128)(2,1)S(1)} %collective-permute-done.3.refs_0_, bf16[1024,512]{1,0:T(8,128)(2,1)S(1)} %copy-done, bf16[1024,512]{1,0:T(8,128)(2,1)} %collective-permute-done.1.refs_2_.refs_4_, bf16[1024,512]{1,0:T(8,128)(2,1)} %shard_map.169.refs_5_.refs_3_, ...), custom_call_target="tpu_custom_call", output_to_operand_aliasing={{}: (5, {})} | custom-call | bytes 1024 | tf_op jit(solution)/shard_map/pallas_call | solution.py:249
  43.4 0.0 copy-start.7
  43.4 6.2 %all-to-all-start = ((bf16[16,64,1024]{2,1,0:T(8,128)(2,1)}), bf16[16,64,1024]{2,1,0:T(8,128)(2,1)S(1)}, u32[]{:S(2)}, u32[]{:S(2)}) async-start(bf16[16,64,1024]{2,1,0:T(8,128)(2,1)} %shard_map.171), calls=%async_computation | async-start | bytes 4194304 | tf_op jit(solution)/shard_map/all_to_all | solution.py:518
  49.6 0.0 copy-done.7
  49.6 0.1 collective-permute-start.9
  49.7 1.2 collective-permute-done.9.gain_par
  50.9 29.1 %all-to-all-done.parts = bf16[16,64,1024]{2,1,0:T(8,128)(2,1)S(1)} async-done(((bf16[16,64,1024]{2,1,0:T(8,128)(2,1)}), bf16[16,64,1024]{2,1,0:T(8,128)(2,1)S(1)}, u32[]{:S(2)}, u32[]{:S(2)}) %all-to-all-start) | async-done | bytes 2097184 | tf_op jit(solution)/shard_map/all_to_all | solution.py:518
  80.0 5.4 %shard_map.172 = (bf16[128,512]{1,0:T(8,128)(2,1)S(1)}, bf16[128,512]{1,0:T(8,128)(2,1)S(1)}, bf16[128,4224]{1,0:T(8,128)(2,1)}) custom-call(bf16[16,64,1024]{2,1,0:T(8,128)(2,1)S(1)} %all-to-all-done.parts, bf16[256,512]{1,0:T(8,128)(2,1)S(1)} %copy-done.3, bf16[128,512]{1,0:T(8,128)(2,1)S(1)} %collective-permute-done.6.extra, ...), custom_call_target="tpu_custom_call" | custom-call | flops 1024 | bytes 1024 | tf_op jit(solution)/shard_map/pallas_call | solution.py:323
  85.4 0.0 copy-start.6
  85.4 0.0 copy-start.4
  85.4 0.0 copy-start.5
  85.4 3.7 %all-to-all-start.1 = ((bf16[8,16,4224]{2,1,0:T(8,128)(2,1)}), bf16[8,16,4224]{2,1,0:T(8,128)(2,1)S(1)}, u32[]{:S(2)}, u32[]{:S(2)}) async-start(bf16[8,16,4224]{2,1,0:T(8,128)(2,1)} %bitcast.6), calls=%async_computation.1 | async-start | bytes 2162688 | tf_op jit(solution)/shard_map/all_to_all | solution.py:520
  89.2 0.1 collective-permute-start.10
  89.3 1.3 %collective-permute-done.10 = bf16[128,512]{1,0:T(8,128)(2,1)S(1)} collective-permute-done((bf16[128,512]{1,0:T(8,128)(2,1)S(1)}, bf16[128,512]{1,0:T(8,128)(2,1)S(1)}, u32[]{:S(2)}, u32[]{:S(2)}) %collective-permute-start.10) | collective-permute-done | bytes 131104 | tf_op jit(solution)/shard_map/ppermute | solution.py:182
  90.6 0.6 collective-permute-start.11
  91.3 0.0 copy-done.6
  91.3 5.0 %collective-permute-done.11 = bf16[64,1024]{1,0:T(8,128)(2,1)S(1)} collective-permute-done((bf16[64,1024]{1,0:T(8,128)(2,1)S(1)}, bf16[64,1024]{1,0:T(8,128)(2,1)S(1)}, u32[]{:S(2)}, u32[]{:S(2)}) %collective-permute-start.11) | collective-permute-done | bytes 131104 | tf_op jit(solution)/shard_map/ppermute | solution.py:182
  96.3 8.0 %all-to-all-done.1.got_hbm = bf16[8,16,4224]{2,1,0:T(8,128)(2,1)S(1)} async-done(((bf16[8,16,4224]{2,1,0:T(8,128)(2,1)}), bf16[8,16,4224]{2,1,0:T(8,128)(2,1)S(1)}, u32[]{:S(2)}, u32[]{:S(2)}) %all-to-all-start.1) | async-done | bytes 1081376 | tf_op jit(solution)/shard_map/all_to_all | solution.py:520
  104.3 0.0 copy-done.4
  104.3 0.0 copy-done.5
  104.3 1.2 %shard_map.173 = f32[128,1,128]{2,1,0:T(1,128)} custom-call(bf16[8,16,4224]{2,1,0:T(8,128)(2,1)S(1)} %all-to-all-done.1.got_hbm, bf16[1,4096]{1,0:T(2,128)(2,1)S(1)} %reshape.45.head_hbm, s32[1,128]{1,0:T(1,128)S(1)} %bitcast.11, s32[1,128]{1,0:T(1,128)S(1)} %bitcast.12), custom_call_target="tpu_custom_call" | custom-call | flops 1024 | bytes 1024 | tf_op jit(solution)/shard_map/pallas_call | solution.py:385
  105.5 4.6 %all-to-all-start.2 = ((f32[128,1,128]{2,1,0:T(1,128)}), f32[128,1,128]{2,1,0:T(1,128)S(1)}, u32[]{:S(2)}, u32[]{:S(2)}) async-start(f32[128,1,128]{2,1,0:T(1,128)} %shard_map.173), calls=%async_computation.2 | async-start | bytes 131072 | tf_op jit(solution)/shard_map/all_to_all | solution.py:535
  110.1 0.8 maximum_select_fusion.1
  110.9 8.5 %all-to-all-done.2.all_hbm = f32[128,1,128]{2,1,0:T(1,128)S(1)} async-done(((f32[128,1,128]{2,1,0:T(1,128)}), f32[128,1,128]{2,1,0:T(1,128)S(1)}, u32[]{:S(2)}, u32[]{:S(2)}) %all-to-all-start.2) | async-done | bytes 65568 | tf_op jit(solution)/shard_map/all_to_all | solution.py:535
  119.4 1.1 shard_map.174
  (15 shorter events, 0.2 us)
Async XLA Ops:
  0.6 17.4 %collective-permute-start = (bf16[512,4096]{1,0:T(8,128)(2,1)}, bf16[512,4096]{1,0:T(8,128)(2,1)}, u32[]{:S(2)}, u32[]{:S(2)}) collective-permute-start(bf16[512,4096]{1,0:T(8,128)(2,1)} %up_mine.1), channel_id=1, source_target_pairs={{0,8},{8,0},{1,9},{9,1},{2,10},{10,2},{3,11},{11,3},{4,12},{12,4},... | collective-permute-start | bytes 12582920 | tf_op jit(solution)/shard_map/ppermute | solution.py:182
  0.7 17.3 %collective-permute-start.1 = (bf16[1024,512]{1,0:T(8,128)(2,1)}, bf16[1024,512]{1,0:T(8,128)(2,1)}, u32[]{:S(2)}, u32[]{:S(2)}) collective-permute-start(bf16[1024,512]{1,0:T(8,128)(2,1)} %refs_1_.1), channel_id=1, source_target_pairs={{0,8},{8,0},{1,9},{9,1},{2,10},{10,2},{3,11},{11,3},{4,12},{12,4},... | collective-permute-start | bytes 3145736 | tf_op jit(solution)/shard_map/ppermute | solution.py:182
  1.2 27.0 %collective-permute-start.4 = (bf16[1024,512]{1,0:T(8,128)(2,1)}, bf16[1024,512]{1,0:T(8,128)(2,1)}, u32[]{:S(2)}, u32[]{:S(2)}) collective-permute-start(bf16[1024,512]{1,0:T(8,128)(2,1)} %refs_1_.1), channel_id=1, source_target_pairs={{0,16},{16,0},{1,17},{17,1},{2,18},{18,2},{3,19},{19,3},{4,20},{20... | collective-permute-start | bytes 3145736 | tf_op jit(solution)/shard_map/ppermute | solution.py:182
  4.3 13.6 %copy-start.3 = (bf16[256,512]{1,0:T(8,128)(2,1)S(1)}, bf16[256,512]{1,0:T(8,128)(2,1)}, u32[]{:S(2)}) copy-start(bf16[256,512]{1,0:T(8,128)(2,1)} %res.1) | copy-start | bytes 786436
  18.0 1.0 copy-start.1
  19.0 14.2 %copy-start = (bf16[1024,512]{1,0:T(8,128)(2,1)S(1)}, bf16[1024,512]{1,0:T(8,128)(2,1)}, u32[]{:S(2)}) copy-start(bf16[1024,512]{1,0:T(8,128)(2,1)} %refs_1_.1) | copy-start | bytes 3145732
  19.0 14.2 %copy-start.2 = (bf16[128,1024]{1,0:T(8,128)(2,1)S(1)}, bf16[128,1024]{1,0:T(8,128)(2,1)}, u32[]{:S(2)}) copy-start(bf16[128,1024]{1,0:T(8,128)(2,1)} %shard_map.167.refs_1_.refs_0_) | copy-start | bytes 786436
  19.0 4.3 %collective-permute-start.6 = (bf16[128,512]{1,0:T(8,128)(2,1)S(1)}, bf16[128,512]{1,0:T(8,128)(2,1)S(1)}, u32[]{:S(2)}, u32[]{:S(2)}) collective-permute-start(bf16[128,512]{1,0:T(8,128)(2,1)S(1)} %constant_dynamic-slice_fusion.5), channel_id=1, source_target_pairs={{0,8},{8,0},{1,9},{9,1},{2,10},{10,2},{3,11},{11,3},{4,12},{12,4},... | collective-permute-start | bytes 393224 | tf_op jit(solution)/shard_map/ppermute | solution.py:182
  19.1 11.2 %collective-permute-start.2 = (bf16[128,1024]{1,0:T(8,128)(2,1)}, bf16[128,1024]{1,0:T(8,128)(2,1)S(1)}, u32[]{:S(2)}, u32[]{:S(2)}) collective-permute-start(bf16[128,1024]{1,0:T(8,128)(2,1)} %shard_map.167.refs_1_.refs_0_), channel_id=1, source_target_pairs={{0,32},{32,64},{64,96},{96,0},{1,33},{33,65},{65,97},{97,1},{2,34}... | collective-permute-start | bytes 786440 | tf_op jit(solution)/shard_map/ppermute | solution.py:186
  21.1 9.2 %collective-permute-start.5 = (bf16[128,1024]{1,0:T(8,128)(2,1)}, bf16[128,1024]{1,0:T(8,128)(2,1)S(1)}, u32[]{:S(2)}, u32[]{:S(2)}) collective-permute-start(bf16[128,1024]{1,0:T(8,128)(2,1)} %shard_map.167.refs_1_.refs_0_), channel_id=1, source_target_pairs={{0,96},{32,0},{64,32},{96,64},{1,97},{33,1},{65,33},{97,65},{2,98}... | collective-permute-start | bytes 786440 | tf_op jit(solution)/shard_map/ppermute | solution.py:186
  23.4 5.5 %collective-permute-start.7 = (bf16[64,1024]{1,0:T(8,128)(2,1)S(1)}, bf16[64,1024]{1,0:T(8,128)(2,1)S(1)}, u32[]{:S(2)}, u32[]{:S(2)}) collective-permute-start(bf16[64,1024]{1,0:T(8,128)(2,1)S(1)} %pad_maximum_fusion), channel_id=1, source_target_pairs={{0,1},{1,0},{2,3},{3,2},{4,5},{5,4},{6,7},{7,6},{8,9},{9,8},{10,11... | collective-permute-start | bytes 393224 | tf_op jit(solution)/shard_map/ppermute | solution.py:182
  30.3 2.9 %collective-permute-start.8 = (bf16[1024,512]{1,0:T(8,128)(2,1)}, bf16[1024,512]{1,0:T(8,128)(2,1)S(1)}, u32[]{:S(2)}, u32[]{:S(2)}) collective-permute-start(bf16[1024,512]{1,0:T(8,128)(2,1)} %shard_map.169.refs_5_.refs_3_), channel_id=1, source_target_pairs={{0,8},{8,0},{1,9},{9,1},{2,10},{10,2},{3,11},{11,3},{4,12},{12,4},... | collective-permute-start | bytes 3145736 | tf_op jit(solution)/shard_map/ppermute | solution.py:182
  30.3 9.9 %collective-permute-start.3 = (bf16[128,1024]{1,0:T(8,128)(2,1)S(1)}, bf16[128,1024]{1,0:T(8,128)(2,1)S(1)}, u32[]{:S(2)}, u32[]{:S(2)}) collective-permute-start(bf16[128,1024]{1,0:T(8,128)(2,1)S(1)} %collective-permute-done.2.refs_1_), channel_id=1, source_target_pairs={{0,32},{32,64},{64,96},{96,0},{1,33},{33,65},{65,97},{97,1},{2,34}... | collective-permute-start | bytes 786440 | tf_op jit(solution)/shard_map/ppermute | solution.py:186
  43.4 6.2 %copy-start.7 = (bf16[512]{0:T(512)(128)(2,1)S(1)}, bf16[512]{0:T(512)(128)(2,1)}, u32[]{:S(2)}) copy-start(bf16[512]{0:T(512)(128)(2,1)} %param.27) | copy-start | bytes 3076
  43.4 36.6 %all-to-all-start = ((bf16[16,64,1024]{2,1,0:T(8,128)(2,1)}), bf16[16,64,1024]{2,1,0:T(8,128)(2,1)S(1)}, u32[]{:S(2)}, u32[]{:S(2)}) async-start(bf16[16,64,1024]{2,1,0:T(8,128)(2,1)} %shard_map.171), calls=%async_computation | async-start | bytes 4194304 | tf_op jit(solution)/shard_map/all_to_all | solution.py:518
  49.6 1.3 %collective-permute-start.9 = (bf16[16,512]{1,0:T(8,128)(2,1)S(1)}, bf16[16,512]{1,0:T(8,128)(2,1)S(1)}, u32[]{:S(2)}, u32[]{:S(2)}) collective-permute-start(bf16[16,512]{1,0:T(8,128)(2,1)S(1)} %broadcast_in_dim.2.gain), channel_id=1, source_target_pairs={{0,8},{8,0},{1,9},{9,1},{2,10},{10,2},{3,11},{11,3},{4,12},{12,4},... | collective-permute-start | bytes 49160 | tf_op jit(solution)/shard_map/ppermute | solution.py:182
  85.4 5.8 %copy-start.6 = (bf16[4096]{0:T(1024)(128)(2,1)S(1)}, bf16[4096]{0:T(1024)(128)(2,1)}, u32[]{:S(2)}) copy-start(bf16[4096]{0:T(1024)(128)(2,1)} %param.29) | copy-start | bytes 24580
  85.4 18.9 %copy-start.4 = (s32[128]{0:T(128)S(1)}, s32[128]{0:T(128)}, u32[]{:S(2)}) copy-start(s32[128]{0:T(128)} %ids_hbm.1) | copy-start | bytes 1540
  85.4 18.9 %copy-start.5 = (s32[128]{0:T(128)S(1)}, s32[128]{0:T(128)}, u32[]{:S(2)}) copy-start(s32[128]{0:T(128)} %param.24) | copy-start | bytes 1540
  85.4 18.8 %all-to-all-start.1 = ((bf16[8,16,4224]{2,1,0:T(8,128)(2,1)}), bf16[8,16,4224]{2,1,0:T(8,128)(2,1)S(1)}, u32[]{:S(2)}, u32[]{:S(2)}) async-start(bf16[8,16,4224]{2,1,0:T(8,128)(2,1)} %bitcast.6), calls=%async_computation.1 | async-start | bytes 2162688 | tf_op jit(solution)/shard_map/all_to_all | solution.py:520
  89.2 1.4 %collective-permute-start.10 = (bf16[128,512]{1,0:T(8,128)(2,1)S(1)}, bf16[128,512]{1,0:T(8,128)(2,1)S(1)}, u32[]{:S(2)}, u32[]{:S(2)}) collective-permute-start(bf16[128,512]{1,0:T(8,128)(2,1)S(1)} %get-tuple-element.9), channel_id=1, source_target_pairs={{0,8},{8,0},{1,9},{9,1},{2,10},{10,2},{3,11},{11,3},{4,12},{12,4},... | collective-permute-start | bytes 393224 | tf_op jit(solution)/shard_map/ppermute | solution.py:182
  90.6 5.6 %collective-permute-start.11 = (bf16[64,1024]{1,0:T(8,128)(2,1)S(1)}, bf16[64,1024]{1,0:T(8,128)(2,1)S(1)}, u32[]{:S(2)}, u32[]{:S(2)}) collective-permute-start(bf16[64,1024]{1,0:T(8,128)(2,1)S(1)} %pad_maximum_fusion.1), channel_id=1, source_target_pairs={{0,1},{1,0},{2,3},{3,2},{4,5},{5,4},{6,7},{7,6},{8,9},{9,8},{10,11... | collective-permute-start | bytes 393224 | tf_op jit(solution)/shard_map/ppermute | solution.py:182
  105.5 13.9 %all-to-all-start.2 = ((f32[128,1,128]{2,1,0:T(1,128)}), f32[128,1,128]{2,1,0:T(1,128)S(1)}, u32[]{:S(2)}, u32[]{:S(2)}) async-start(f32[128,1,128]{2,1,0:T(1,128)} %shard_map.173), calls=%async_computation.2 | async-start | bytes 131072 | tf_op jit(solution)/shard_map/all_to_all | solution.py:535

commit v5 on v4

--- a/solution.py
+++ b/solution.py
@@ -212,7 +212,8 @@
 
 def proj_kernel(steps, *refs):
     count = len(steps)
-    rows, weights = refs[:count], refs[count : count + 4]
+    given = len(refs) - 8 - (count == 1)
+    rows, weights = refs[:given], refs[given : given + 4]
     out, w, chunks, sems = refs[-4:]
     loads = [
         pltpu.make_async_copy(src, w.at[:, j * 512 : (j + 1) * 512], sems.at[j])
@@ -243,15 +244,16 @@
 
 def project(steps, *ins):
     count = len(steps)
-    more = len(ins) > count + 4
+    more = count == 1
+    given = len(ins) - 4 - more
     V = pl.BlockSpec(memory_space=pltpu.VMEM)
     A = pl.BlockSpec(memory_space=pl.ANY)
     return pl.pallas_call(
         functools.partial(proj_kernel, steps),
         out_shape=jax.ShapeDtypeStruct((16, 64, 1024), BF),
-        in_specs=[V] * count + [A] * (len(ins) - count),
+        in_specs=[V] * given + [A] * (len(ins) - given),
         out_specs=A,
-        input_output_aliases={count + 4: 0} if more else {},
+        input_output_aliases={given + 4: 0} if more else {},
         scratch_shapes=[
             pltpu.VMEM((1024, 2048), BF),
             pltpu.VMEM((2, count, 2, 64, 1024), BF),
@@ -263,7 +265,7 @@
 
 def up_kernel(
     parts, res, extra, res_y, gain, gain_par, up_mine, up_par,
-    hm_ref, hp_ref, sent_ref, parts_v, res_v, gain_v, gain2_v, w, sems,
+    hm_ref, hp_ref, sent_ref, res_v, gain_v, gain2_v, w, sent, sems,
 ):
     c = lax.axis_index("c")
     yl = lax.axis_index("yl")
@@ -272,15 +274,12 @@
     small = [
         pltpu.make_async_copy(src, dst, sems.at[i // 4, i % 4])
         for i, (src, dst) in enumerate((
-            (parts.at[:8], parts_v.at[:8]), (parts.at[8:], parts_v.at[8:]),
             (res.at[pl.ds(pl.multiple_of(c * 128 + yl * 64, 64), 64)], res_v.at[here, :512]),
             (extra.at[here], res_v.at[here, 512:]),
             (res_y, res_v.at[there]),
             (gain, gain_v), (gain_par, gain2_v),
         ))
     ]
-    for copy in small:
-        copy.start()
     loads = []
     for j in range(4):
         cols = slice(j * 1024, (j + 1) * 1024)
@@ -290,13 +289,16 @@
         ))
         for load in loads[-1]:
             load.start()
+        if j == 0:
+            for copy in small:
+                copy.start()
     for copy in small:
         copy.wait()
 
     def summed(first):
-        total = parts_v[first].astype(F32)
+        total = parts[first].astype(F32)
         for i in range(1, 8):
-            total = total + parts_v[first + i].astype(F32)
+            total = total + parts[first + i].astype(F32)
         return total
 
     mixed = jnp.concatenate([summed(0), summed(8)], axis=0)
@@ -307,14 +309,20 @@
     squares = jnp.sum(wide * wide, axis=1, keepdims=True)
     hi = squares.astype(BF).astype(F32)
     lane = lax.broadcasted_iota(jnp.int32, (128, 128), 1)
-    sent_ref[:, 4096:] = jnp.where(lane == 0, hi, jnp.where(lane == 1, squares - hi, 0.0)).astype(BF)
+    sent[:, 4096:] = jnp.where(lane == 0, hi, jnp.where(lane == 1, squares - hi, 0.0)).astype(BF)
     gains = jnp.concatenate([gain_v[0:1], gain2_v[0:1]], axis=1).astype(F32)
     gained = (wide * gains).astype(BF)
+    leave = []
     for j in range(4):
         cols = slice(j * 1024, (j + 1) * 1024)
         for load in loads[j]:
             load.wait()
-        sent_ref[:, cols] = jnp.dot(gained, w[:, cols], preferred_element_type=F32).astype(BF)
+        sent[:, cols] = jnp.dot(gained, w[:, cols], preferred_element_type=F32).astype(BF)
+        out = slice(j * 1024, (j + 1) * 1024 + (128 if j == 3 else 0))
+        leave.append(pltpu.make_async_copy(sent.at[:, out], sent_ref.at[:, out], sems.at[4, j]))
+        leave[-1].start()
+    for copy in leave:
+        copy.wait()
 
 
 def verify_up(*ins):
@@ -327,15 +335,15 @@
             jax.ShapeDtypeStruct((128, 512), BF),
             jax.ShapeDtypeStruct((128, 4096 + 128), BF),
         ),
-        in_specs=[A] * 8,
-        out_specs=(V, V, V),
+        in_specs=[V] + [A] * 7,
+        out_specs=(V, V, A),
         scratch_shapes=[
-            pltpu.VMEM((16, 64, 1024), BF),
             pltpu.VMEM((128, 1024), BF),
             pltpu.VMEM((16, 512), BF),
             pltpu.VMEM((16, 512), BF),
             pltpu.VMEM((1024, 4096), BF),
-            pltpu.SemaphoreType.DMA((4, 4)),
+            pltpu.VMEM((128, 4096 + 128), BF),
+            pltpu.SemaphoreType.DMA((5, 4)),
         ],
         **tiny(48),
     )(*ins)
@@ -498,7 +506,7 @@
 
     part = hold(part, up_par, w01, mib=63)
     before, after = shift(part, 1), shift(part, 3)
-    far = shift(before, 1)
+    far = (shift(before[:64], 1), shift(after[64:], 3))
     gain = jnp.broadcast_to(norm_gain[None, :], (16, 512))
     gain_par = swap(gain, "c")
     later = hold(residual, part)
@@ -514,7 +522,7 @@
 
     weights = (out_weight, w01, w10, w11)
     partial = project((0, 1, 3), part, before, after, *weights)
-    partial = project((2,), far, *weights, partial)
+    partial = project((2,), *far, *weights, partial)
     parts = lax.all_to_all(partial, ("xh", "xl", "yh", "yl"), 0, 0, tiled=True)
     hid_mine, hid_par, sent = verify_up(parts, residual, extra, res_y, gain, gain_par, up_weight, up_par)
     got = lax.all_to_all(sent.reshape(8, 16, 4096 + 128), ("z", "xh"), 0, 0, tiled=True)

time: 122 us -> 120 us (0.984)
  waiting for transfers between devices: 62.9 us -> 59.6 us
  starting transfers between devices: 26.2 us -> 28.4 us
    ppermute x3 -> x4, waiting for transfers between devices: 4.37 us -> 1.43 us  [shift(): return lax.ppermute(x, 'z', [(i, (i + by) % 4) for i in range(4)])]
    ppermute x3 -> x4, starting transfers between devices: 5.46 us -> 7.57 us  [shift(): return lax.ppermute(x, 'z', [(i, (i + by) % 4) for i in range(4)])]
    ppermute x9, waiting for transfers between devices: 12.9 us -> 11.4 us  [swap(): return lax.ppermute(x, axis, [(0, 1), (1, 0)])]
  transfers between devices with their start and end apart: 15 -> 16, of which waited for: 11 -> 9; matrix products, arithmetic and copies ran while one was open for 1% -> 1% of each run, Pallas kernels for 15% -> 15%
where the time goes in v5:
time: 120 us; the launch traced here: 119 us
  waiting for transfers between devices  59.6 us (50%)
  starting transfers between devices  28.4 us (24%)
  Pallas kernels  28 us (23%)
    all_to_all x1, waiting for transfers between devices, body(): parts = lax.all_to_all(partial, ('xh', 'xl', 'yh', 'yl'), 0, 0, tiled=True)  29.8 us
    pallas_call x1, Pallas kernels, attend(): pl.pallas_call(functools.partial(attn_kernel, rows, tile), out_shape=jax....  13.6 us
    ppermute x9, waiting for transfers between devices, swap(): return lax.ppermute(x, axis, [(0, 1), (1, 0)])  11.4 us
    all_to_all x1, waiting for transfers between devices, body(): lax.all_to_all(sent.reshape(8, 16, 4096 + 128), ('z', 'xh'), 0, 0, tiled=...  8.57 us
    all_to_all x1, waiting for transfers between devices, body(): scores, votes = tally(lax.all_to_all(line, AXES, 0, 0, tiled=True))  8.45 us
    ppermute x4, starting transfers between devices, shift(): return lax.ppermute(x, 'z', [(i, (i + by) % 4) for i in range(4)])  7.57 us
    pallas_call x2, Pallas kernels, project(): pl.pallas_call(functools.partial(proj_kernel, steps), out_shape=jax.Shape...  7.19 us
    ppermute x9, starting transfers between devices, swap(): return lax.ppermute(x, axis, [(0, 1), (1, 0)])  6.15 us
  transfers between devices with their start and end apart: 16, of which 9 were waited for; matrix products, arithmetic and copies ran while one was open for 1% of the time, Pallas kernels for 15%

profile of v5, /device:TPU:0, one launch (start us, length us, event | category | flops | bytes accessed | tf_op | source)
XLA Modules:
  0.0 118.9 jit_solution(16656397142920028551)
XLA Ops:
  0.6 0.1 collective-permute-start
  0.7 0.5 collective-permute-start.1
  1.2 3.1 %collective-permute-start.6 = (bf16[1024,512]{1,0:T(8,128)(2,1)}, bf16[1024,512]{1,0:T(8,128)(2,1)}, u32[]{:S(2)}, u32[]{:S(2)}) collective-permute-start(bf16[1024,512]{1,0:T(8,128)(2,1)} %refs_2_.1), channel_id=1, source_target_pairs={{0,16},{16,0},{1,17},{17,1},{2,18},{18,2},{3,19},{19,3},{4,20},{20... | collective-permute-start | bytes 3145736 | tf_op jit(solution)/shard_map/ppermute | solution.py:182
  4.3 0.0 copy-start.3
  4.3 13.6 %shard_map.166.refs_0_ = bf16[128,1024]{1,0:T(8,128)(2,1)} custom-call(s32[128]{0:T(128)} %ids_hbm.1, s32[1,128]{1,0:T(1,128)} %bitcast.10, s32[1,128]{1,0:T(1,128)} %bitcast.19, bf16[128,1024]{1,0:T(8,128)(2,1)} %q_hbm.1, bf16[128,128]{1,0:T(8,128)(2,1)} %nk_hbm.1, bf16[128,128]{1,0:T(8,128)(2,1)} %nv_hbm.1, bf16[2,2048,128]{2,1,0:T(8,128)(2,1)} %bitcast.15, ...), custom_call_target="tpu_custom_call" | custom-call | flops 16000000000 | bytes 11534336 | tf_op jit(solution)/shard_map/pallas_call | solution.py:159
  18.0 0.0 copy-done.3
  18.0 0.0 collective-permute-done.1.refs_2_.refs_4_.refs_3_
  18.0 0.0 collective-permute-done.refs_1_.up_par
  18.0 0.0 copy-start.1
  18.1 0.9 copy-done.1
  19.0 0.0 copy-start
  19.0 0.0 copy-start.2
  19.0 0.1 collective-permute-start.7
  19.1 2.0 %collective-permute-start.2 = (bf16[128,1024]{1,0:T(8,128)(2,1)}, bf16[128,1024]{1,0:T(8,128)(2,1)S(1)}, u32[]{:S(2)}, u32[]{:S(2)}) collective-permute-start(bf16[128,1024]{1,0:T(8,128)(2,1)} %shard_map.167.refs_1_.refs_0_), channel_id=1, source_target_pairs={{0,32},{32,64},{64,96},{96,0},{1,33},{33,65},{65,97},{97,1},{2,34}... | collective-permute-start | bytes 786440 | tf_op jit(solution)/shard_map/ppermute | solution.py:186
  21.1 2.2 %collective-permute-start.4 = (bf16[128,1024]{1,0:T(8,128)(2,1)}, bf16[128,1024]{1,0:T(8,128)(2,1)S(1)}, u32[]{:S(2)}, u32[]{:S(2)}) collective-permute-start(bf16[128,1024]{1,0:T(8,128)(2,1)} %shard_map.167.refs_1_.refs_0_), channel_id=1, source_target_pairs={{0,96},{32,0},{64,32},{96,64},{1,97},{33,1},{65,33},{97,65},{2,98}... | collective-permute-start | bytes 786440 | tf_op jit(solution)/shard_map/ppermute | solution.py:186
  23.3 0.0 collective-permute-done.7.extra
  23.4 1.6 %collective-permute-start.8 = (bf16[64,1024]{1,0:T(8,128)(2,1)S(1)}, bf16[64,1024]{1,0:T(8,128)(2,1)S(1)}, u32[]{:S(2)}, u32[]{:S(2)}) collective-permute-start(bf16[64,1024]{1,0:T(8,128)(2,1)S(1)} %pad_maximum_fusion), channel_id=1, source_target_pairs={{0,1},{1,0},{2,3},{3,2},{4,5},{5,4},{6,7},{7,6},{8,9},{9,8},{10,11... | collective-permute-start | bytes 393224 | tf_op jit(solution)/shard_map/ppermute | solution.py:182
  25.0 3.2 %collective-permute-done.6.refs_0_ = bf16[1024,512]{1,0:T(8,128)(2,1)} collective-permute-done((bf16[1024,512]{1,0:T(8,128)(2,1)}, bf16[1024,512]{1,0:T(8,128)(2,1)}, u32[]{:S(2)}, u32[]{:S(2)}) %collective-permute-start.6) | collective-permute-done | bytes 1048608 | tf_op jit(solution)/shard_map/ppermute | solution.py:182
  28.2 0.7 collective-permute-done.8.refs_3_.res_y
  28.9 1.4 %collective-permute-done.2.refs_1_ = bf16[128,1024]{1,0:T(8,128)(2,1)S(1)} collective-permute-done((bf16[128,1024]{1,0:T(8,128)(2,1)}, bf16[128,1024]{1,0:T(8,128)(2,1)S(1)}, u32[]{:S(2)}, u32[]{:S(2)}) %collective-permute-start.2) | collective-permute-done | bytes 262176 | tf_op jit(solution)/shard_map/ppermute | solution.py:186
  30.3 0.0 collective-permute-done.4.refs_2_
  30.3 0.0 collective-permute-start.9
  30.4 1.3 %collective-permute-start.3 = (bf16[64,1024]{1,0:T(8,128)(2,1)S(1)}, bf16[64,1024]{1,0:T(8,128)(2,1)S(1)}, u32[]{:S(2)}, u32[]{:S(2)}) collective-permute-start(bf16[64,1024]{1,0:T(8,128)(2,1)S(1)} %slice.16), channel_id=1, source_target_pairs={{0,32},{32,64},{64,96},{96,0},{1,33},{33,65},{65,97},{97,1},{2,34}... | collective-permute-start | bytes 393224 | tf_op jit(solution)/shard_map/ppermute | solution.py:186
  31.7 2.0 %collective-permute-start.5 = (bf16[64,1024]{1,0:T(8,128)(2,1)S(1)}, bf16[64,1024]{1,0:T(8,128)(2,1)S(1)}, u32[]{:S(2)}, u32[]{:S(2)}) collective-permute-start(bf16[64,1024]{1,0:T(8,128)(2,1)S(1)} %slice.17), channel_id=1, source_target_pairs={{0,96},{32,0},{64,32},{96,64},{1,97},{33,1},{65,33},{97,65},{2,98}... | collective-permute-start | bytes 393224 | tf_op jit(solution)/shard_map/ppermute | solution.py:186
  33.7 0.0 collective-permute-done.9.refs_6_.refs_5_
  33.7 0.0 copy-done
  33.7 0.0 copy-done.2
  33.8 4.1 %shard_map.170.refs_6_ = bf16[16,64,1024]{2,1,0:T(8,128)(2,1)} custom-call(bf16[128,1024]{1,0:T(8,128)(2,1)S(1)} %copy-done.2, bf16[128,1024]{1,0:T(8,128)(2,1)S(1)} %collective-permute-done.2.refs_1_, bf16[128,1024]{1,0:T(8,128)(2,1)S(1)} %collective-permute-done.4.refs_2_, bf16[1024,512]{1,0:T(8,128)(2,1)S(1)} %copy-done, ...), custom_call_target="tpu_custom_call" | custom-call | bytes 1024 | tf_op jit(solution)/shard_map/pallas_call | solution.py:251
  37.9 0.0 collective-permute-done.3.refs_0_
  37.9 0.0 collective-permute-done.5.refs_1_
  37.9 3.1 %shard_map.171 = bf16[16,64,1024]{2,1,0:T(8,128)(2,1)} custom-call(bf16[64,1024]{1,0:T(8,128)(2,1)S(1)} %collective-permute-done.3.refs_0_, bf16[64,1024]{1,0:T(8,128)(2,1)S(1)} %collective-permute-done.5.refs_1_, bf16[1024,512]{1,0:T(8,128)(2,1)S(1)} %copy-done, ...), custom_call_target="tpu_custom_call", output_to_operand_aliasing={{}: (6, {})} | custom-call | bytes 1024 | tf_op jit(solution)/shard_map/pallas_call | solution.py:251
  41.0 0.0 copy-start.7
  41.0 6.0 %all-to-all-start = ((bf16[16,64,1024]{2,1,0:T(8,128)(2,1)}), bf16[16,64,1024]{2,1,0:T(8,128)(2,1)S(1)}, u32[]{:S(2)}, u32[]{:S(2)}) async-start(bf16[16,64,1024]{2,1,0:T(8,128)(2,1)} %shard_map.171), calls=%async_computation | async-start | bytes 4194304 | tf_op jit(solution)/shard_map/all_to_all | solution.py:526
  47.0 0.0 copy-done.7
  47.0 0.1 collective-permute-start.10
  47.1 1.2 collective-permute-done.10.gain_par
  48.3 29.8 %all-to-all-done.parts = bf16[16,64,1024]{2,1,0:T(8,128)(2,1)S(1)} async-done(((bf16[16,64,1024]{2,1,0:T(8,128)(2,1)}), bf16[16,64,1024]{2,1,0:T(8,128)(2,1)S(1)}, u32[]{:S(2)}, u32[]{:S(2)}) %all-to-all-start) | async-done | bytes 2097184 | tf_op jit(solution)/shard_map/all_to_all | solution.py:526
  78.1 4.9 %shard_map.172 = (bf16[128,512]{1,0:T(8,128)(2,1)S(1)}, bf16[128,512]{1,0:T(8,128)(2,1)S(1)}, bf16[128,4224]{1,0:T(8,128)(2,1)}) custom-call(bf16[16,64,1024]{2,1,0:T(8,128)(2,1)S(1)} %all-to-all-done.parts, bf16[256,512]{1,0:T(8,128)(2,1)S(1)} %copy-done.3, bf16[128,512]{1,0:T(8,128)(2,1)S(1)} %collective-permute-done.7.extra, ...), custom_call_target="tpu_custom_call" | custom-call | flops 1024 | bytes 1024 | tf_op jit(solution)/shard_map/pallas_call | solution.py:331
  83.0 0.0 copy-start.6
  83.0 0.0 copy-start.4
  83.1 0.0 copy-start.5
  83.1 4.1 %all-to-all-start.1 = ((bf16[8,16,4224]{2,1,0:T(8,128)(2,1)}), bf16[8,16,4224]{2,1,0:T(8,128)(2,1)S(1)}, u32[]{:S(2)}, u32[]{:S(2)}) async-start(bf16[8,16,4224]{2,1,0:T(8,128)(2,1)} %bitcast.6), calls=%async_computation.1 | async-start | bytes 2162688 | tf_op jit(solution)/shard_map/all_to_all | solution.py:528
  87.1 0.0 collective-permute-start.11
  87.2 1.3 %collective-permute-done.11 = bf16[128,512]{1,0:T(8,128)(2,1)S(1)} collective-permute-done((bf16[128,512]{1,0:T(8,128)(2,1)S(1)}, bf16[128,512]{1,0:T(8,128)(2,1)S(1)}, u32[]{:S(2)}, u32[]{:S(2)}) %collective-permute-start.11) | collective-permute-done | bytes 131104 | tf_op jit(solution)/shard_map/ppermute | solution.py:182
  88.5 0.6 collective-permute-start.12
  89.2 0.0 copy-done.6
  89.2 5.0 %collective-permute-done.12 = bf16[64,1024]{1,0:T(8,128)(2,1)S(1)} collective-permute-done((bf16[64,1024]{1,0:T(8,128)(2,1)S(1)}, bf16[64,1024]{1,0:T(8,128)(2,1)S(1)}, u32[]{:S(2)}, u32[]{:S(2)}) %collective-permute-start.12) | collective-permute-done | bytes 131104 | tf_op jit(solution)/shard_map/ppermute | solution.py:182
  94.2 8.6 %all-to-all-done.1.got_hbm = bf16[8,16,4224]{2,1,0:T(8,128)(2,1)S(1)} async-done(((bf16[8,16,4224]{2,1,0:T(8,128)(2,1)}), bf16[8,16,4224]{2,1,0:T(8,128)(2,1)S(1)}, u32[]{:S(2)}, u32[]{:S(2)}) %all-to-all-start.1) | async-done | bytes 1081376 | tf_op jit(solution)/shard_map/all_to_all | solution.py:528
  102.8 0.0 copy-done.4
  102.8 0.0 copy-done.5
  102.8 1.2 %shard_map.173 = f32[128,1,128]{2,1,0:T(1,128)} custom-call(bf16[8,16,4224]{2,1,0:T(8,128)(2,1)S(1)} %all-to-all-done.1.got_hbm, bf16[1,4096]{1,0:T(2,128)(2,1)S(1)} %reshape.45.head_hbm, s32[1,128]{1,0:T(1,128)S(1)} %bitcast.11, s32[1,128]{1,0:T(1,128)S(1)} %bitcast.12), custom_call_target="tpu_custom_call" | custom-call | flops 1024 | bytes 1024 | tf_op jit(solution)/shard_map/pallas_call | solution.py:393
  104.0 4.6 %all-to-all-start.2 = ((f32[128,1,128]{2,1,0:T(1,128)}), f32[128,1,128]{2,1,0:T(1,128)S(1)}, u32[]{:S(2)}, u32[]{:S(2)}) async-start(f32[128,1,128]{2,1,0:T(1,128)} %shard_map.173), calls=%async_computation.2 | async-start | bytes 131072 | tf_op jit(solution)/shard_map/all_to_all | solution.py:543
  108.7 0.8 maximum_select_fusion.1
  109.4 8.4 %all-to-all-done.2.all_hbm = f32[128,1,128]{2,1,0:T(1,128)S(1)} async-done(((f32[128,1,128]{2,1,0:T(1,128)}), f32[128,1,128]{2,1,0:T(1,128)S(1)}, u32[]{:S(2)}, u32[]{:S(2)}) %all-to-all-start.2) | async-done | bytes 65568 | tf_op jit(solution)/shard_map/all_to_all | solution.py:543
  117.9 1.1 shard_map.174
  (17 shorter events, 0.2 us)
Async XLA Ops:
  0.6 17.4 %collective-permute-start = (bf16[512,4096]{1,0:T(8,128)(2,1)}, bf16[512,4096]{1,0:T(8,128)(2,1)}, u32[]{:S(2)}, u32[]{:S(2)}) collective-permute-start(bf16[512,4096]{1,0:T(8,128)(2,1)} %up_mine.1), channel_id=1, source_target_pairs={{0,8},{8,0},{1,9},{9,1},{2,10},{10,2},{3,11},{11,3},{4,12},{12,4},... | collective-permute-start | bytes 12582920 | tf_op jit(solution)/shard_map/ppermute | solution.py:182
  0.7 17.3 %collective-permute-start.1 = (bf16[1024,512]{1,0:T(8,128)(2,1)}, bf16[1024,512]{1,0:T(8,128)(2,1)}, u32[]{:S(2)}, u32[]{:S(2)}) collective-permute-start(bf16[1024,512]{1,0:T(8,128)(2,1)} %refs_2_.1), channel_id=1, source_target_pairs={{0,8},{8,0},{1,9},{9,1},{2,10},{10,2},{3,11},{11,3},{4,12},{12,4},... | collective-permute-start | bytes 3145736 | tf_op jit(solution)/shard_map/ppermute | solution.py:182
  1.2 27.0 %collective-permute-start.6 = (bf16[1024,512]{1,0:T(8,128)(2,1)}, bf16[1024,512]{1,0:T(8,128)(2,1)}, u32[]{:S(2)}, u32[]{:S(2)}) collective-permute-start(bf16[1024,512]{1,0:T(8,128)(2,1)} %refs_2_.1), channel_id=1, source_target_pairs={{0,16},{16,0},{1,17},{17,1},{2,18},{18,2},{3,19},{19,3},{4,20},{20... | collective-permute-start | bytes 3145736 | tf_op jit(solution)/shard_map/ppermute | solution.py:182
  4.3 13.6 %copy-start.3 = (bf16[256,512]{1,0:T(8,128)(2,1)S(1)}, bf16[256,512]{1,0:T(8,128)(2,1)}, u32[]{:S(2)}) copy-start(bf16[256,512]{1,0:T(8,128)(2,1)} %res.1) | copy-start | bytes 786436
  18.0 1.0 copy-start.1
  19.0 14.7 %copy-start = (bf16[1024,512]{1,0:T(8,128)(2,1)S(1)}, bf16[1024,512]{1,0:T(8,128)(2,1)}, u32[]{:S(2)}) copy-start(bf16[1024,512]{1,0:T(8,128)(2,1)} %refs_2_.1) | copy-start | bytes 3145732
  19.0 14.7 %copy-start.2 = (bf16[128,1024]{1,0:T(8,128)(2,1)S(1)}, bf16[128,1024]{1,0:T(8,128)(2,1)}, u32[]{:S(2)}) copy-start(bf16[128,1024]{1,0:T(8,128)(2,1)} %shard_map.167.refs_1_.refs_0_) | copy-start | bytes 786436
  19.0 4.3 %collective-permute-start.7 = (bf16[128,512]{1,0:T(8,128)(2,1)S(1)}, bf16[128,512]{1,0:T(8,128)(2,1)S(1)}, u32[]{:S(2)}, u32[]{:S(2)}) collective-permute-start(bf16[128,512]{1,0:T(8,128)(2,1)S(1)} %constant_dynamic-slice_fusion.5), channel_id=1, source_target_pairs={{0,8},{8,0},{1,9},{9,1},{2,10},{10,2},{3,11},{11,3},{4,12},{12,4},... | collective-permute-start | bytes 393224 | tf_op jit(solution)/shard_map/ppermute | solution.py:182
  19.1 11.2 %collective-permute-start.2 = (bf16[128,1024]{1,0:T(8,128)(2,1)}, bf16[128,1024]{1,0:T(8,128)(2,1)S(1)}, u32[]{:S(2)}, u32[]{:S(2)}) collective-permute-start(bf16[128,1024]{1,0:T(8,128)(2,1)} %shard_map.167.refs_1_.refs_0_), channel_id=1, source_target_pairs={{0,32},{32,64},{64,96},{96,0},{1,33},{33,65},{65,97},{97,1},{2,34}... | collective-permute-start | bytes 786440 | tf_op jit(solution)/shard_map/ppermute | solution.py:186
  21.1 9.2 %collective-permute-start.4 = (bf16[128,1024]{1,0:T(8,128)(2,1)}, bf16[128,1024]{1,0:T(8,128)(2,1)S(1)}, u32[]{:S(2)}, u32[]{:S(2)}) collective-permute-start(bf16[128,1024]{1,0:T(8,128)(2,1)} %shard_map.167.refs_1_.refs_0_), channel_id=1, source_target_pairs={{0,96},{32,0},{64,32},{96,64},{1,97},{33,1},{65,33},{97,65},{2,98}... | collective-permute-start | bytes 786440 | tf_op jit(solution)/shard_map/ppermute | solution.py:186
  23.4 5.5 %collective-permute-start.8 = (bf16[64,1024]{1,0:T(8,128)(2,1)S(1)}, bf16[64,1024]{1,0:T(8,128)(2,1)S(1)}, u32[]{:S(2)}, u32[]{:S(2)}) collective-permute-start(bf16[64,1024]{1,0:T(8,128)(2,1)S(1)} %pad_maximum_fusion), channel_id=1, source_target_pairs={{0,1},{1,0},{2,3},{3,2},{4,5},{5,4},{6,7},{7,6},{8,9},{9,8},{10,11... | collective-permute-start | bytes 393224 | tf_op jit(solution)/shard_map/ppermute | solution.py:182
  30.3 3.4 %collective-permute-start.9 = (bf16[1024,512]{1,0:T(8,128)(2,1)}, bf16[1024,512]{1,0:T(8,128)(2,1)S(1)}, u32[]{:S(2)}, u32[]{:S(2)}) collective-permute-start(bf16[1024,512]{1,0:T(8,128)(2,1)} %shard_map.169.refs_5_.refs_4_), channel_id=1, source_target_pairs={{0,8},{8,0},{1,9},{9,1},{2,10},{10,2},{3,11},{11,3},{4,12},{12,4},... | collective-permute-start | bytes 3145736 | tf_op jit(solution)/shard_map/ppermute | solution.py:182
  30.4 7.5 %collective-permute-start.3 = (bf16[64,1024]{1,0:T(8,128)(2,1)S(1)}, bf16[64,1024]{1,0:T(8,128)(2,1)S(1)}, u32[]{:S(2)}, u32[]{:S(2)}) collective-permute-start(bf16[64,1024]{1,0:T(8,128)(2,1)S(1)} %slice.16), channel_id=1, source_target_pairs={{0,32},{32,64},{64,96},{96,0},{1,33},{33,65},{65,97},{97,1},{2,34}... | collective-permute-start | bytes 393224 | tf_op jit(solution)/shard_map/ppermute | solution.py:186
  31.7 6.2 %collective-permute-start.5 = (bf16[64,1024]{1,0:T(8,128)(2,1)S(1)}, bf16[64,1024]{1,0:T(8,128)(2,1)S(1)}, u32[]{:S(2)}, u32[]{:S(2)}) collective-permute-start(bf16[64,1024]{1,0:T(8,128)(2,1)S(1)} %slice.17), channel_id=1, source_target_pairs={{0,96},{32,0},{64,32},{96,64},{1,97},{33,1},{65,33},{97,65},{2,98}... | collective-permute-start | bytes 393224 | tf_op jit(solution)/shard_map/ppermute | solution.py:186
  41.0 6.0 %copy-start.7 = (bf16[512]{0:T(512)(128)(2,1)S(1)}, bf16[512]{0:T(512)(128)(2,1)}, u32[]{:S(2)}) copy-start(bf16[512]{0:T(512)(128)(2,1)} %param.27) | copy-start | bytes 3076
  41.0 37.1 %all-to-all-start = ((bf16[16,64,1024]{2,1,0:T(8,128)(2,1)}), bf16[16,64,1024]{2,1,0:T(8,128)(2,1)S(1)}, u32[]{:S(2)}, u32[]{:S(2)}) async-start(bf16[16,64,1024]{2,1,0:T(8,128)(2,1)} %shard_map.171), calls=%async_computation | async-start | bytes 4194304 | tf_op jit(solution)/shard_map/all_to_all | solution.py:526
  47.0 1.3 %collective-permute-start.10 = (bf16[16,512]{1,0:T(8,128)(2,1)S(1)}, bf16[16,512]{1,0:T(8,128)(2,1)S(1)}, u32[]{:S(2)}, u32[]{:S(2)}) collective-permute-start(bf16[16,512]{1,0:T(8,128)(2,1)S(1)} %broadcast_in_dim.2.gain), channel_id=1, source_target_pairs={{0,8},{8,0},{1,9},{9,1},{2,10},{10,2},{3,11},{11,3},{4,12},{12,4},... | collective-permute-start | bytes 49160 | tf_op jit(solution)/shard_map/ppermute | solution.py:182
  83.0 6.1 %copy-start.6 = (bf16[4096]{0:T(1024)(128)(2,1)S(1)}, bf16[4096]{0:T(1024)(128)(2,1)}, u32[]{:S(2)}) copy-start(bf16[4096]{0:T(1024)(128)(2,1)} %param.29) | copy-start | bytes 24580
  83.0 19.8 %copy-start.4 = (s32[128]{0:T(128)S(1)}, s32[128]{0:T(128)}, u32[]{:S(2)}) copy-start(s32[128]{0:T(128)} %ids_hbm.1) | copy-start | bytes 1540
  83.1 19.8 %copy-start.5 = (s32[128]{0:T(128)S(1)}, s32[128]{0:T(128)}, u32[]{:S(2)}) copy-start(s32[128]{0:T(128)} %param.24) | copy-start | bytes 1540
  83.1 19.7 %all-to-all-start.1 = ((bf16[8,16,4224]{2,1,0:T(8,128)(2,1)}), bf16[8,16,4224]{2,1,0:T(8,128)(2,1)S(1)}, u32[]{:S(2)}, u32[]{:S(2)}) async-start(bf16[8,16,4224]{2,1,0:T(8,128)(2,1)} %bitcast.6), calls=%async_computation.1 | async-start | bytes 2162688 | tf_op jit(solution)/shard_map/all_to_all | solution.py:528
  87.1 1.3 %collective-permute-start.11 = (bf16[128,512]{1,0:T(8,128)(2,1)S(1)}, bf16[128,512]{1,0:T(8,128)(2,1)S(1)}, u32[]{:S(2)}, u32[]{:S(2)}) collective-permute-start(bf16[128,512]{1,0:T(8,128)(2,1)S(1)} %get-tuple-element.9), channel_id=1, source_target_pairs={{0,8},{8,0},{1,9},{9,1},{2,10},{10,2},{3,11},{11,3},{4,12},{12,4},... | collective-permute-start | bytes 393224 | tf_op jit(solution)/shard_map/ppermute | solution.py:182
  88.5 5.6 %collective-permute-start.12 = (bf16[64,1024]{1,0:T(8,128)(2,1)S(1)}, bf16[64,1024]{1,0:T(8,128)(2,1)S(1)}, u32[]{:S(2)}, u32[]{:S(2)}) collective-permute-start(bf16[64,1024]{1,0:T(8,128)(2,1)S(1)} %pad_maximum_fusion.1), channel_id=1, source_target_pairs={{0,1},{1,0},{2,3},{3,2},{4,5},{5,4},{6,7},{7,6},{8,9},{9,8},{10,11... | collective-permute-start | bytes 393224 | tf_op jit(solution)/shard_map/ppermute | solution.py:182
  104.0 13.9 %all-to-all-start.2 = ((f32[128,1,128]{2,1,0:T(1,128)}), f32[128,1,128]{2,1,0:T(1,128)S(1)}, u32[]{:S(2)}, u32[]{:S(2)}) async-start(f32[128,1,128]{2,1,0:T(1,128)} %shard_map.173), calls=%async_computation.2 | async-start | bytes 131072 | tf_op jit(solution)/shard_map/all_to_all | solution.py:543

commit v6 on v5

--- a/solution.py
+++ b/solution.py
@@ -507,9 +507,9 @@
     part = hold(part, up_par, w01, mib=63)
     before, after = shift(part, 1), shift(part, 3)
     far = (shift(before[:64], 1), shift(after[64:], 3))
-    gain = jnp.broadcast_to(norm_gain[None, :], (16, 512))
+    later = hold(residual, part)
+    gain = norm_gain[None, :] + later[:16] * 0
     gain_par = swap(gain, "c")
-    later = hold(residual, part)
     extra = swap(rows_of(later, (1 - c) * 128, 128), "c")
     res_y = swap(
         jnp.concatenate(
@@ -517,7 +517,7 @@
         ),
         "yl",
     )
-    w10 = hold(w10, before, after, res_y)
+    w10 = hold(w10, before, after, res_y, gain_par)
     w11 = swap(w10, "c")
 
     weights = (out_weight, w01, w10, w11)

time: 120 us -> 119 us (level)
  blocking collectives: 0 us -> 34.7 us
  waiting for transfers between devices: 59.6 us -> 29.4 us
  starting transfers between devices: 28.4 us -> 22.9 us
    all_to_all x0 -> x1, blocking collectives: none -> 34.7 us  [body(): parts = lax.all_to_all(partial, ('xh', 'xl', 'yh', 'yl'), 0, 0, tiled=True)]
    all_to_all x1 -> x0, waiting for transfers between devices: 29.8 us -> none  [body(): parts = lax.all_to_all(partial, ('xh', 'xl', 'yh', 'yl'), 0, 0, tiled=True)]
    all_to_all x1 -> x0, starting transfers between devices: 5.98 us -> none  [body(): parts = lax.all_to_all(partial, ('xh', 'xl', 'yh', 'yl'), 0, 0, tiled=True)]
  transfers between devices with their start and end apart: 16 -> 15, of which waited for: 9 -> 7; matrix products, arithmetic and copies ran while one was open for 1% -> 1% of each run, Pallas kernels for 15% -> 15%
where the time goes in v6:
time: 119 us; the launch traced here: 118 us
  blocking collectives  34.7 us (29%)
  waiting for transfers between devices  29.4 us (25%)
  Pallas kernels  28 us (24%)
  starting transfers between devices  22.9 us (19%)
    all_to_all x1, blocking collectives, body(): parts = lax.all_to_all(partial, ('xh', 'xl', 'yh', 'yl'), 0, 0, tiled=True)  34.7 us
    pallas_call x1, Pallas kernels, attend(): pl.pallas_call(functools.partial(attn_kernel, rows, tile), out_shape=jax....  13.6 us
    ppermute x9, waiting for transfers between devices, swap(): return lax.ppermute(x, axis, [(0, 1), (1, 0)])  10.4 us
    all_to_all x1, waiting for transfers between devices, body(): lax.all_to_all(sent.reshape(8, 16, 4096 + 128), ('z', 'xh'), 0, 0, tiled=...  8.99 us
    all_to_all x1, waiting for transfers between devices, body(): scores, votes = tally(lax.all_to_all(line, AXES, 0, 0, tiled=True))  8.54 us
    ppermute x4, starting transfers between devices, shift(): return lax.ppermute(x, 'z', [(i, (i + by) % 4) for i in range(4)])  7.57 us
    pallas_call x2, Pallas kernels, project(): pl.pallas_call(functools.partial(proj_kernel, steps), out_shape=jax.Shape...  7.19 us
    ppermute x9, starting transfers between devices, swap(): return lax.ppermute(x, axis, [(0, 1), (1, 0)])  5.83 us
  transfers between devices with their start and end apart: 15, of which 7 were waited for; matrix products, arithmetic and copies ran while one was open for 1% of the time, Pallas kernels for 15%

profile of v6, /device:TPU:0, one launch (start us, length us, event | category | flops | bytes accessed | tf_op | source)
XLA Modules:
  0.0 117.8 jit_solution(16541743961946331633)
XLA Ops:
  0.6 0.1 collective-permute-start
  0.7 0.5 collective-permute-start.1
  1.2 3.1 %collective-permute-start.6 = (bf16[1024,512]{1,0:T(8,128)(2,1)}, bf16[1024,512]{1,0:T(8,128)(2,1)}, u32[]{:S(2)}, u32[]{:S(2)}) collective-permute-start(bf16[1024,512]{1,0:T(8,128)(2,1)} %refs_2_.1), channel_id=1, source_target_pairs={{0,16},{16,0},{1,17},{17,1},{2,18},{18,2},{3,19},{19,3},{4,20},{20... | collective-permute-start | bytes 3145736 | tf_op jit(solution)/shard_map/ppermute | solution.py:182
  4.3 0.0 copy-start.3
  4.3 13.6 %shard_map.166.refs_0_ = bf16[128,1024]{1,0:T(8,128)(2,1)} custom-call(s32[128]{0:T(128)} %ids_hbm.1, s32[1,128]{1,0:T(1,128)} %bitcast.10, s32[1,128]{1,0:T(1,128)} %bitcast.19, bf16[128,1024]{1,0:T(8,128)(2,1)} %q_hbm.1, bf16[128,128]{1,0:T(8,128)(2,1)} %nk_hbm.1, bf16[128,128]{1,0:T(8,128)(2,1)} %nv_hbm.1, bf16[2,2048,128]{2,1,0:T(8,128)(2,1)} %bitcast.15, ...), custom_call_target="tpu_custom_call" | custom-call | flops 16000000000 | bytes 11534336 | tf_op jit(solution)/shard_map/pallas_call | solution.py:159
  18.0 0.0 copy-done.3
  18.0 0.0 copy-start.7
  18.0 0.0 collective-permute-done.1.refs_2_.refs_4_.refs_3_
  18.0 0.0 collective-permute-done.refs_1_.up_par
  18.1 0.0 copy-start.1
  18.1 0.9 copy-done.1
  19.0 0.0 copy-start
  19.0 0.0 copy-start.2
  19.0 0.1 collective-permute-start.7
  19.1 2.0 %collective-permute-start.2 = (bf16[128,1024]{1,0:T(8,128)(2,1)}, bf16[128,1024]{1,0:T(8,128)(2,1)S(1)}, u32[]{:S(2)}, u32[]{:S(2)}) collective-permute-start(bf16[128,1024]{1,0:T(8,128)(2,1)} %shard_map.167.refs_1_.refs_0_), channel_id=1, source_target_pairs={{0,32},{32,64},{64,96},{96,0},{1,33},{33,65},{65,97},{97,1},{2,34}... | collective-permute-start | bytes 786440 | tf_op jit(solution)/shard_map/ppermute | solution.py:186
  21.1 2.2 %collective-permute-start.4 = (bf16[128,1024]{1,0:T(8,128)(2,1)}, bf16[128,1024]{1,0:T(8,128)(2,1)S(1)}, u32[]{:S(2)}, u32[]{:S(2)}) collective-permute-start(bf16[128,1024]{1,0:T(8,128)(2,1)} %shard_map.167.refs_1_.refs_0_), channel_id=1, source_target_pairs={{0,96},{32,0},{64,32},{96,64},{1,97},{33,1},{65,33},{97,65},{2,98}... | collective-permute-start | bytes 786440 | tf_op jit(solution)/shard_map/ppermute | solution.py:186
  23.3 0.0 collective-permute-done.7.extra
  23.4 1.6 %collective-permute-start.8 = (bf16[64,1024]{1,0:T(8,128)(2,1)S(1)}, bf16[64,1024]{1,0:T(8,128)(2,1)S(1)}, u32[]{:S(2)}, u32[]{:S(2)}) collective-permute-start(bf16[64,1024]{1,0:T(8,128)(2,1)S(1)} %pad_maximum_fusion), channel_id=1, source_target_pairs={{0,1},{1,0},{2,3},{3,2},{4,5},{5,4},{6,7},{7,6},{8,9},{9,8},{10,11... | collective-permute-start | bytes 393224 | tf_op jit(solution)/shard_map/ppermute | solution.py:182
  25.0 0.0 copy-done.7
  25.0 0.0 collective-permute-start.9
  25.0 3.2 %collective-permute-done.6.refs_0_ = bf16[1024,512]{1,0:T(8,128)(2,1)} collective-permute-done((bf16[1024,512]{1,0:T(8,128)(2,1)}, bf16[1024,512]{1,0:T(8,128)(2,1)}, u32[]{:S(2)}, u32[]{:S(2)}) %collective-permute-start.6) | collective-permute-done | bytes 1048608 | tf_op jit(solution)/shard_map/ppermute | solution.py:182
  28.2 0.0 collective-permute-done.9.refs_4_.gain_par
  28.2 0.7 collective-permute-done.8.refs_3_.res_y
  28.9 1.4 %collective-permute-done.2.refs_1_ = bf16[128,1024]{1,0:T(8,128)(2,1)S(1)} collective-permute-done((bf16[128,1024]{1,0:T(8,128)(2,1)}, bf16[128,1024]{1,0:T(8,128)(2,1)S(1)}, u32[]{:S(2)}, u32[]{:S(2)}) %collective-permute-start.2) | collective-permute-done | bytes 262176 | tf_op jit(solution)/shard_map/ppermute | solution.py:186
  30.3 0.0 collective-permute-done.4.refs_2_
  30.3 0.0 collective-permute-start.10
  30.4 1.3 %collective-permute-start.3 = (bf16[64,1024]{1,0:T(8,128)(2,1)S(1)}, bf16[64,1024]{1,0:T(8,128)(2,1)S(1)}, u32[]{:S(2)}, u32[]{:S(2)}) collective-permute-start(bf16[64,1024]{1,0:T(8,128)(2,1)S(1)} %slice.20), channel_id=1, source_target_pairs={{0,32},{32,64},{64,96},{96,0},{1,33},{33,65},{65,97},{97,1},{2,34}... | collective-permute-start | bytes 393224 | tf_op jit(solution)/shard_map/ppermute | solution.py:186
  31.7 2.0 %collective-permute-start.5 = (bf16[64,1024]{1,0:T(8,128)(2,1)S(1)}, bf16[64,1024]{1,0:T(8,128)(2,1)S(1)}, u32[]{:S(2)}, u32[]{:S(2)}) collective-permute-start(bf16[64,1024]{1,0:T(8,128)(2,1)S(1)} %slice.21), channel_id=1, source_target_pairs={{0,96},{32,0},{64,32},{96,64},{1,97},{33,1},{65,33},{97,65},{2,98}... | collective-permute-start | bytes 393224 | tf_op jit(solution)/shard_map/ppermute | solution.py:186
  33.8 0.0 collective-permute-done.10.refs_6_.refs_5_
  33.8 0.0 copy-done
  33.8 0.0 copy-done.2
  33.8 4.1 %shard_map.170.refs_6_ = bf16[16,64,1024]{2,1,0:T(8,128)(2,1)} custom-call(bf16[128,1024]{1,0:T(8,128)(2,1)S(1)} %copy-done.2, bf16[128,1024]{1,0:T(8,128)(2,1)S(1)} %collective-permute-done.2.refs_1_, bf16[128,1024]{1,0:T(8,128)(2,1)S(1)} %collective-permute-done.4.refs_2_, bf16[1024,512]{1,0:T(8,128)(2,1)S(1)} %copy-done, ...), custom_call_target="tpu_custom_call" | custom-call | bytes 1024 | tf_op jit(solution)/shard_map/pallas_call | solution.py:251
  37.9 0.0 collective-permute-done.3.refs_0_
  37.9 0.0 collective-permute-done.5.refs_1_
  37.9 3.1 %shard_map.171 = bf16[16,64,1024]{2,1,0:T(8,128)(2,1)} custom-call(bf16[64,1024]{1,0:T(8,128)(2,1)S(1)} %collective-permute-done.3.refs_0_, bf16[64,1024]{1,0:T(8,128)(2,1)S(1)} %collective-permute-done.5.refs_1_, bf16[1024,512]{1,0:T(8,128)(2,1)S(1)} %copy-done, ...), custom_call_target="tpu_custom_call", output_to_operand_aliasing={{}: (6, {})} | custom-call | bytes 1024 | tf_op jit(solution)/shard_map/pallas_call | solution.py:251
  41.0 34.7 %all_to_all.15.parts = bf16[16,64,1024]{2,1,0:T(8,128)(2,1)S(1)} all-to-all(bf16[16,64,1024]{2,1,0:T(8,128)(2,1)} %shard_map.171), channel_id=1, replica_groups=mesh['z'=4,'xh'=2,'c'=2,'xl'=2,'yh'=2,'yl'=2] {'xh','xl','yh','yl'}, dimensions={0} | all-to-all | bytes 4194304 | tf_op jit(solution)/shard_map/all_to_all | solution.py:526
  75.7 4.9 %shard_map.172 = (bf16[128,512]{1,0:T(8,128)(2,1)S(1)}, bf16[128,512]{1,0:T(8,128)(2,1)S(1)}, bf16[128,4224]{1,0:T(8,128)(2,1)}) custom-call(bf16[16,64,1024]{2,1,0:T(8,128)(2,1)S(1)} %all_to_all.15.parts, bf16[256,512]{1,0:T(8,128)(2,1)S(1)} %copy-done.3, bf16[128,512]{1,0:T(8,128)(2,1)S(1)} %collective-permute-done.7.extra, ...), custom_call_target="tpu_custom_call" | custom-call | flops 1024 | bytes 1024 | tf_op jit(solution)/shard_map/pallas_call | solution.py:331
  80.6 0.0 copy-start.6
  80.6 0.0 copy-start.4
  80.7 0.0 copy-start.5
  80.7 4.5 %all-to-all-start.1 = ((bf16[8,16,4224]{2,1,0:T(8,128)(2,1)}), bf16[8,16,4224]{2,1,0:T(8,128)(2,1)S(1)}, u32[]{:S(2)}, u32[]{:S(2)}) async-start(bf16[8,16,4224]{2,1,0:T(8,128)(2,1)} %bitcast.6), calls=%async_computation.1 | async-start | bytes 2162688 | tf_op jit(solution)/shard_map/all_to_all | solution.py:528
  85.2 0.0 collective-permute-start.11
  85.2 1.3 %collective-permute-done.11 = bf16[128,512]{1,0:T(8,128)(2,1)S(1)} collective-permute-done((bf16[128,512]{1,0:T(8,128)(2,1)S(1)}, bf16[128,512]{1,0:T(8,128)(2,1)S(1)}, u32[]{:S(2)}, u32[]{:S(2)}) %collective-permute-start.11) | collective-permute-done | bytes 131104 | tf_op jit(solution)/shard_map/ppermute | solution.py:182
  86.6 0.4 collective-permute-start.12
  87.0 0.0 copy-done.6
  87.0 5.2 %collective-permute-done.12 = bf16[64,1024]{1,0:T(8,128)(2,1)S(1)} collective-permute-done((bf16[64,1024]{1,0:T(8,128)(2,1)S(1)}, bf16[64,1024]{1,0:T(8,128)(2,1)S(1)}, u32[]{:S(2)}, u32[]{:S(2)}) %collective-permute-start.12) | collective-permute-done | bytes 131104 | tf_op jit(solution)/shard_map/ppermute | solution.py:182
  92.3 9.0 %all-to-all-done.1.got_hbm = bf16[8,16,4224]{2,1,0:T(8,128)(2,1)S(1)} async-done(((bf16[8,16,4224]{2,1,0:T(8,128)(2,1)}), bf16[8,16,4224]{2,1,0:T(8,128)(2,1)S(1)}, u32[]{:S(2)}, u32[]{:S(2)}) %all-to-all-start.1) | async-done | bytes 1081376 | tf_op jit(solution)/shard_map/all_to_all | solution.py:528
  101.3 0.0 copy-done.4
  101.3 0.0 copy-done.5
  101.3 1.2 %shard_map.173 = f32[128,1,128]{2,1,0:T(1,128)} custom-call(bf16[8,16,4224]{2,1,0:T(8,128)(2,1)S(1)} %all-to-all-done.1.got_hbm, bf16[1,4096]{1,0:T(2,128)(2,1)S(1)} %reshape.45.head_hbm, s32[1,128]{1,0:T(1,128)S(1)} %bitcast.11, s32[1,128]{1,0:T(1,128)S(1)} %bitcast.12), custom_call_target="tpu_custom_call" | custom-call | flops 1024 | bytes 1024 | tf_op jit(solution)/shard_map/pallas_call | solution.py:393
  102.5 5.0 %all-to-all-start.2 = ((f32[128,1,128]{2,1,0:T(1,128)}), f32[128,1,128]{2,1,0:T(1,128)S(1)}, u32[]{:S(2)}, u32[]{:S(2)}) async-start(f32[128,1,128]{2,1,0:T(1,128)} %shard_map.173), calls=%async_computation.2 | async-start | bytes 131072 | tf_op jit(solution)/shard_map/all_to_all | solution.py:543
  107.5 0.8 maximum_select_fusion.1
  108.2 8.5 %all-to-all-done.2.all_hbm = f32[128,1,128]{2,1,0:T(1,128)S(1)} async-done(((f32[128,1,128]{2,1,0:T(1,128)}), f32[128,1,128]{2,1,0:T(1,128)S(1)}, u32[]{:S(2)}, u32[]{:S(2)}) %all-to-all-start.2) | async-done | bytes 65568 | tf_op jit(solution)/shard_map/all_to_all | solution.py:543
  116.8 1.1 shard_map.174
  (17 shorter events, 0.2 us)
Async XLA Ops:
  0.6 17.4 %collective-permute-start = (bf16[512,4096]{1,0:T(8,128)(2,1)}, bf16[512,4096]{1,0:T(8,128)(2,1)}, u32[]{:S(2)}, u32[]{:S(2)}) collective-permute-start(bf16[512,4096]{1,0:T(8,128)(2,1)} %up_mine.1), channel_id=1, source_target_pairs={{0,8},{8,0},{1,9},{9,1},{2,10},{10,2},{3,11},{11,3},{4,12},{12,4},... | collective-permute-start | bytes 12582920 | tf_op jit(solution)/shard_map/ppermute | solution.py:182
  0.7 17.3 %collective-permute-start.1 = (bf16[1024,512]{1,0:T(8,128)(2,1)}, bf16[1024,512]{1,0:T(8,128)(2,1)}, u32[]{:S(2)}, u32[]{:S(2)}) collective-permute-start(bf16[1024,512]{1,0:T(8,128)(2,1)} %refs_2_.1), channel_id=1, source_target_pairs={{0,8},{8,0},{1,9},{9,1},{2,10},{10,2},{3,11},{11,3},{4,12},{12,4},... | collective-permute-start | bytes 3145736 | tf_op jit(solution)/shard_map/ppermute | solution.py:182
  1.2 27.0 %collective-permute-start.6 = (bf16[1024,512]{1,0:T(8,128)(2,1)}, bf16[1024,512]{1,0:T(8,128)(2,1)}, u32[]{:S(2)}, u32[]{:S(2)}) collective-permute-start(bf16[1024,512]{1,0:T(8,128)(2,1)} %refs_2_.1), channel_id=1, source_target_pairs={{0,16},{16,0},{1,17},{17,1},{2,18},{18,2},{3,19},{19,3},{4,20},{20... | collective-permute-start | bytes 3145736 | tf_op jit(solution)/shard_map/ppermute | solution.py:182
  4.3 13.6 %copy-start.3 = (bf16[256,512]{1,0:T(8,128)(2,1)S(1)}, bf16[256,512]{1,0:T(8,128)(2,1)}, u32[]{:S(2)}) copy-start(bf16[256,512]{1,0:T(8,128)(2,1)} %res.1) | copy-start | bytes 786436
  18.0 7.0 %copy-start.7 = (bf16[512]{0:T(512)(128)(2,1)S(1)}, bf16[512]{0:T(512)(128)(2,1)}, u32[]{:S(2)}) copy-start(bf16[512]{0:T(512)(128)(2,1)} %param.27) | copy-start | bytes 3076
  18.1 1.0 copy-start.1
  19.0 14.7 %copy-start = (bf16[1024,512]{1,0:T(8,128)(2,1)S(1)}, bf16[1024,512]{1,0:T(8,128)(2,1)}, u32[]{:S(2)}) copy-start(bf16[1024,512]{1,0:T(8,128)(2,1)} %refs_2_.1) | copy-start | bytes 3145732
  19.0 14.7 %copy-start.2 = (bf16[128,1024]{1,0:T(8,128)(2,1)S(1)}, bf16[128,1024]{1,0:T(8,128)(2,1)}, u32[]{:S(2)}) copy-start(bf16[128,1024]{1,0:T(8,128)(2,1)} %shard_map.167.refs_1_.refs_0_) | copy-start | bytes 786436
  19.0 4.3 %collective-permute-start.7 = (bf16[128,512]{1,0:T(8,128)(2,1)S(1)}, bf16[128,512]{1,0:T(8,128)(2,1)S(1)}, u32[]{:S(2)}, u32[]{:S(2)}) collective-permute-start(bf16[128,512]{1,0:T(8,128)(2,1)S(1)} %constant_dynamic-slice_fusion.5), channel_id=1, source_target_pairs={{0,8},{8,0},{1,9},{9,1},{2,10},{10,2},{3,11},{11,3},{4,12},{12,4},... | collective-permute-start | bytes 393224 | tf_op jit(solution)/shard_map/ppermute | solution.py:182
  19.1 11.2 %collective-permute-start.2 = (bf16[128,1024]{1,0:T(8,128)(2,1)}, bf16[128,1024]{1,0:T(8,128)(2,1)S(1)}, u32[]{:S(2)}, u32[]{:S(2)}) collective-permute-start(bf16[128,1024]{1,0:T(8,128)(2,1)} %shard_map.167.refs_1_.refs_0_), channel_id=1, source_target_pairs={{0,32},{32,64},{64,96},{96,0},{1,33},{33,65},{65,97},{97,1},{2,34}... | collective-permute-start | bytes 786440 | tf_op jit(solution)/shard_map/ppermute | solution.py:186
  21.1 9.2 %collective-permute-start.4 = (bf16[128,1024]{1,0:T(8,128)(2,1)}, bf16[128,1024]{1,0:T(8,128)(2,1)S(1)}, u32[]{:S(2)}, u32[]{:S(2)}) collective-permute-start(bf16[128,1024]{1,0:T(8,128)(2,1)} %shard_map.167.refs_1_.refs_0_), channel_id=1, source_target_pairs={{0,96},{32,0},{64,32},{96,64},{1,97},{33,1},{65,33},{97,65},{2,98}... | collective-permute-start | bytes 786440 | tf_op jit(solution)/shard_map/ppermute | solution.py:186
  23.4 5.5 %collective-permute-start.8 = (bf16[64,1024]{1,0:T(8,128)(2,1)S(1)}, bf16[64,1024]{1,0:T(8,128)(2,1)S(1)}, u32[]{:S(2)}, u32[]{:S(2)}) collective-permute-start(bf16[64,1024]{1,0:T(8,128)(2,1)S(1)} %pad_maximum_fusion), channel_id=1, source_target_pairs={{0,1},{1,0},{2,3},{3,2},{4,5},{5,4},{6,7},{7,6},{8,9},{9,8},{10,11... | collective-permute-start | bytes 393224 | tf_op jit(solution)/shard_map/ppermute | solution.py:182
  25.0 3.2 %collective-permute-start.9 = (bf16[16,512]{1,0:T(8,128)(2,1)S(1)}, bf16[16,512]{1,0:T(8,128)(2,1)S(1)}, u32[]{:S(2)}, u32[]{:S(2)}) collective-permute-start(bf16[16,512]{1,0:T(8,128)(2,1)S(1)} %fusion.gain), channel_id=1, source_target_pairs={{0,8},{8,0},{1,9},{9,1},{2,10},{10,2},{3,11},{11,3},{4,12},{12,4},... | collective-permute-start | bytes 49160 | tf_op jit(solution)/shard_map/ppermute | solution.py:182
  30.3 3.4 %collective-permute-start.10 = (bf16[1024,512]{1,0:T(8,128)(2,1)}, bf16[1024,512]{1,0:T(8,128)(2,1)S(1)}, u32[]{:S(2)}, u32[]{:S(2)}) collective-permute-start(bf16[1024,512]{1,0:T(8,128)(2,1)} %shard_map.169.refs_5_.refs_4_), channel_id=1, source_target_pairs={{0,8},{8,0},{1,9},{9,1},{2,10},{10,2},{3,11},{11,3},{4,12},{12,4},... | collective-permute-start | bytes 3145736 | tf_op jit(solution)/shard_map/ppermute | solution.py:182
  30.4 7.5 %collective-permute-start.3 = (bf16[64,1024]{1,0:T(8,128)(2,1)S(1)}, bf16[64,1024]{1,0:T(8,128)(2,1)S(1)}, u32[]{:S(2)}, u32[]{:S(2)}) collective-permute-start(bf16[64,1024]{1,0:T(8,128)(2,1)S(1)} %slice.20), channel_id=1, source_target_pairs={{0,32},{32,64},{64,96},{96,0},{1,33},{33,65},{65,97},{97,1},{2,34}... | collective-permute-start | bytes 393224 | tf_op jit(solution)/shard_map/ppermute | solution.py:186
  31.7 6.2 %collective-permute-start.5 = (bf16[64,1024]{1,0:T(8,128)(2,1)S(1)}, bf16[64,1024]{1,0:T(8,128)(2,1)S(1)}, u32[]{:S(2)}, u32[]{:S(2)}) collective-permute-start(bf16[64,1024]{1,0:T(8,128)(2,1)S(1)} %slice.21), channel_id=1, source_target_pairs={{0,96},{32,0},{64,32},{96,64},{1,97},{33,1},{65,33},{97,65},{2,98}... | collective-permute-start | bytes 393224 | tf_op jit(solution)/shard_map/ppermute | solution.py:186
  80.6 6.3 %copy-start.6 = (bf16[4096]{0:T(1024)(128)(2,1)S(1)}, bf16[4096]{0:T(1024)(128)(2,1)}, u32[]{:S(2)}) copy-start(bf16[4096]{0:T(1024)(128)(2,1)} %param.29) | copy-start | bytes 24580
  80.6 20.6 %copy-start.4 = (s32[128]{0:T(128)S(1)}, s32[128]{0:T(128)}, u32[]{:S(2)}) copy-start(s32[128]{0:T(128)} %ids_hbm.1) | copy-start | bytes 1540
  80.7 20.6 %copy-start.5 = (s32[128]{0:T(128)S(1)}, s32[128]{0:T(128)}, u32[]{:S(2)}) copy-start(s32[128]{0:T(128)} %param.24) | copy-start | bytes 1540
  80.7 20.6 %all-to-all-start.1 = ((bf16[8,16,4224]{2,1,0:T(8,128)(2,1)}), bf16[8,16,4224]{2,1,0:T(8,128)(2,1)S(1)}, u32[]{:S(2)}, u32[]{:S(2)}) async-start(bf16[8,16,4224]{2,1,0:T(8,128)(2,1)} %bitcast.6), calls=%async_computation.1 | async-start | bytes 2162688 | tf_op jit(solution)/shard_map/all_to_all | solution.py:528
  85.2 1.3 %collective-permute-start.11 = (bf16[128,512]{1,0:T(8,128)(2,1)S(1)}, bf16[128,512]{1,0:T(8,128)(2,1)S(1)}, u32[]{:S(2)}, u32[]{:S(2)}) collective-permute-start(bf16[128,512]{1,0:T(8,128)(2,1)S(1)} %get-tuple-element.9), channel_id=1, source_target_pairs={{0,8},{8,0},{1,9},{9,1},{2,10},{10,2},{3,11},{11,3},{4,12},{12,4},... | collective-permute-start | bytes 393224 | tf_op jit(solution)/shard_map/ppermute | solution.py:182
  86.6 5.6 %collective-permute-start.12 = (bf16[64,1024]{1,0:T(8,128)(2,1)S(1)}, bf16[64,1024]{1,0:T(8,128)(2,1)S(1)}, u32[]{:S(2)}, u32[]{:S(2)}) collective-permute-start(bf16[64,1024]{1,0:T(8,128)(2,1)S(1)} %pad_maximum_fusion.1), channel_id=1, source_target_pairs={{0,1},{1,0},{2,3},{3,2},{4,5},{5,4},{6,7},{7,6},{8,9},{9,8},{10,11... | collective-permute-start | bytes 393224 | tf_op jit(solution)/shard_map/ppermute | solution.py:182
  102.5 14.3 %all-to-all-start.2 = ((f32[128,1,128]{2,1,0:T(1,128)}), f32[128,1,128]{2,1,0:T(1,128)S(1)}, u32[]{:S(2)}, u32[]{:S(2)}) async-start(f32[128,1,128]{2,1,0:T(1,128)} %shard_map.173), calls=%async_computation.2 | async-start | bytes 131072 | tf_op jit(solution)/shard_map/all_to_all | solution.py:543

commit v7 on v6

--- a/solution.py
+++ b/solution.py
@@ -374,7 +374,7 @@
     for j in range(0, 4096, 512):
         cols = slice(j, j + 512)
         up = summed(cols) * factor
-        acc = acc + up / (1.0 + jnp.exp(-up)) * head[0:1, cols].astype(F32)
+        acc = acc + up / (1.0 + jnp.exp(-up)) * head[0:1, cols]
     scores = jnp.sum(acc, axis=1, keepdims=True)
     row = lax.broadcasted_iota(jnp.int32, (16, 128), 0)
     lane = lax.broadcasted_iota(jnp.int32, (16, 128), 1)
@@ -397,13 +397,13 @@
         out_specs=V,
         scratch_shapes=[
             pltpu.VMEM((8, 16, 4096 + 128), BF),
-            pltpu.VMEM((1, 4096), BF),
+            pltpu.VMEM((1, 4096), F32),
             pltpu.VMEM((1, 128), jnp.int32),
             pltpu.VMEM((1, 128), jnp.int32),
             pltpu.SemaphoreType.DMA((4,)),
         ],
         **tiny(40),
-    )(got, head_weight.reshape(1, 4096), prompt_ids.reshape(1, 128), cluster_ids.reshape(1, 128))
+    )(got, head_weight.astype(F32).reshape(1, 4096), prompt_ids.reshape(1, 128), cluster_ids.reshape(1, 128))
 
 
 def vote_kernel(all_hbm, scores_ref, votes_ref, x3, x, vals, ids, votes, sem):

time: 119 us -> 119 us (level)
  no operation moved by 1% of the time
where the time goes in v7:
time: 119 us; the launch traced here: 118 us
  blocking collectives  34.7 us (29%)
  waiting for transfers between devices  29.4 us (25%)
  Pallas kernels  28 us (24%)
  starting transfers between devices  22.9 us (19%)
    all_to_all x1, blocking collectives, body(): parts = lax.all_to_all(partial, ('xh', 'xl', 'yh', 'yl'), 0, 0, tiled=True)  34.7 us
    pallas_call x1, Pallas kernels, attend(): pl.pallas_call(functools.partial(attn_kernel, rows, tile), out_shape=jax....  13.6 us
    ppermute x9, waiting for transfers between devices, swap(): return lax.ppermute(x, axis, [(0, 1), (1, 0)])  10.4 us
    all_to_all x1, waiting for transfers between devices, body(): lax.all_to_all(sent.reshape(8, 16, 4096 + 128), ('z', 'xh'), 0, 0, tiled=...  8.99 us
    all_to_all x1, waiting for transfers between devices, body(): scores, votes = tally(lax.all_to_all(line, AXES, 0, 0, tiled=True))  8.54 us
    ppermute x4, starting transfers between devices, shift(): return lax.ppermute(x, 'z', [(i, (i + by) % 4) for i in range(4)])  7.57 us
    pallas_call x2, Pallas kernels, project(): pl.pallas_call(functools.partial(proj_kernel, steps), out_shape=jax.Shape...  7.19 us
    ppermute x9, starting transfers between devices, swap(): return lax.ppermute(x, axis, [(0, 1), (1, 0)])  5.83 us
  transfers between devices with their start and end apart: 15, of which 7 were waited for; matrix products, arithmetic and copies ran while one was open for 1% of the time, Pallas kernels for 15%

profile of v7, /device:TPU:0, one launch (start us, length us, event | category | flops | bytes accessed | tf_op | source)
XLA Modules:
  0.0 117.8 jit_solution(3121488412115822324)
XLA Ops:
  0.6 0.1 collective-permute-start
  0.7 0.5 collective-permute-start.1
  1.2 3.1 %collective-permute-start.6 = (bf16[1024,512]{1,0:T(8,128)(2,1)}, bf16[1024,512]{1,0:T(8,128)(2,1)}, u32[]{:S(2)}, u32[]{:S(2)}) collective-permute-start(bf16[1024,512]{1,0:T(8,128)(2,1)} %refs_2_.1), channel_id=1, source_target_pairs={{0,16},{16,0},{1,17},{17,1},{2,18},{18,2},{3,19},{19,3},{4,20},{20... | collective-permute-start | bytes 3145736 | tf_op jit(solution)/shard_map/ppermute | solution.py:182
  4.3 0.0 copy-start.3
  4.3 13.6 %shard_map.166.refs_0_ = bf16[128,1024]{1,0:T(8,128)(2,1)} custom-call(s32[128]{0:T(128)} %ids_hbm.1, s32[1,128]{1,0:T(1,128)} %bitcast.12, s32[1,128]{1,0:T(1,128)} %bitcast.21, bf16[128,1024]{1,0:T(8,128)(2,1)} %q_hbm.1, bf16[128,128]{1,0:T(8,128)(2,1)} %nk_hbm.1, bf16[128,128]{1,0:T(8,128)(2,1)} %nv_hbm.1, bf16[2,2048,128]{2,1,0:T(8,128)(2,1)} %bitcast.17, ...), custom_call_target="tpu_custom_call" | custom-call | flops 16000000000 | bytes 11534336 | tf_op jit(solution)/shard_map/pallas_call | solution.py:159
  18.0 0.0 copy-done.3
  18.0 0.0 copy-start.7
  18.0 0.0 collective-permute-done.1.refs_2_.refs_4_.refs_3_
  18.0 0.0 collective-permute-done.refs_1_.up_par
  18.1 0.0 copy-start.1
  18.1 0.9 copy-done.1
  19.0 0.0 copy-start
  19.0 0.0 copy-start.2
  19.0 0.1 collective-permute-start.7
  19.1 2.0 %collective-permute-start.2 = (bf16[128,1024]{1,0:T(8,128)(2,1)}, bf16[128,1024]{1,0:T(8,128)(2,1)S(1)}, u32[]{:S(2)}, u32[]{:S(2)}) collective-permute-start(bf16[128,1024]{1,0:T(8,128)(2,1)} %shard_map.167.refs_1_.refs_0_), channel_id=1, source_target_pairs={{0,32},{32,64},{64,96},{96,0},{1,33},{33,65},{65,97},{97,1},{2,34}... | collective-permute-start | bytes 786440 | tf_op jit(solution)/shard_map/ppermute | solution.py:186
  21.1 2.2 %collective-permute-start.4 = (bf16[128,1024]{1,0:T(8,128)(2,1)}, bf16[128,1024]{1,0:T(8,128)(2,1)S(1)}, u32[]{:S(2)}, u32[]{:S(2)}) collective-permute-start(bf16[128,1024]{1,0:T(8,128)(2,1)} %shard_map.167.refs_1_.refs_0_), channel_id=1, source_target_pairs={{0,96},{32,0},{64,32},{96,64},{1,97},{33,1},{65,33},{97,65},{2,98}... | collective-permute-start | bytes 786440 | tf_op jit(solution)/shard_map/ppermute | solution.py:186
  23.3 0.0 collective-permute-done.7.extra
  23.4 1.6 %collective-permute-start.8 = (bf16[64,1024]{1,0:T(8,128)(2,1)S(1)}, bf16[64,1024]{1,0:T(8,128)(2,1)S(1)}, u32[]{:S(2)}, u32[]{:S(2)}) collective-permute-start(bf16[64,1024]{1,0:T(8,128)(2,1)S(1)} %pad_maximum_fusion), channel_id=1, source_target_pairs={{0,1},{1,0},{2,3},{3,2},{4,5},{5,4},{6,7},{7,6},{8,9},{9,8},{10,11... | collective-permute-start | bytes 393224 | tf_op jit(solution)/shard_map/ppermute | solution.py:182
  25.0 0.0 copy-done.7
  25.0 0.0 collective-permute-start.9
  25.0 3.2 %collective-permute-done.6.refs_0_ = bf16[1024,512]{1,0:T(8,128)(2,1)} collective-permute-done((bf16[1024,512]{1,0:T(8,128)(2,1)}, bf16[1024,512]{1,0:T(8,128)(2,1)}, u32[]{:S(2)}, u32[]{:S(2)}) %collective-permute-start.6) | collective-permute-done | bytes 1048608 | tf_op jit(solution)/shard_map/ppermute | solution.py:182
  28.2 0.0 collective-permute-done.9.refs_4_.gain_par
  28.2 0.7 collective-permute-done.8.refs_3_.res_y
  28.9 1.4 %collective-permute-done.2.refs_1_ = bf16[128,1024]{1,0:T(8,128)(2,1)S(1)} collective-permute-done((bf16[128,1024]{1,0:T(8,128)(2,1)}, bf16[128,1024]{1,0:T(8,128)(2,1)S(1)}, u32[]{:S(2)}, u32[]{:S(2)}) %collective-permute-start.2) | collective-permute-done | bytes 262176 | tf_op jit(solution)/shard_map/ppermute | solution.py:186
  30.3 0.0 collective-permute-done.4.refs_2_
  30.3 0.0 collective-permute-start.10
  30.4 1.3 %collective-permute-start.3 = (bf16[64,1024]{1,0:T(8,128)(2,1)S(1)}, bf16[64,1024]{1,0:T(8,128)(2,1)S(1)}, u32[]{:S(2)}, u32[]{:S(2)}) collective-permute-start(bf16[64,1024]{1,0:T(8,128)(2,1)S(1)} %slice.20), channel_id=1, source_target_pairs={{0,32},{32,64},{64,96},{96,0},{1,33},{33,65},{65,97},{97,1},{2,34}... | collective-permute-start | bytes 393224 | tf_op jit(solution)/shard_map/ppermute | solution.py:186
  31.7 2.0 %collective-permute-start.5 = (bf16[64,1024]{1,0:T(8,128)(2,1)S(1)}, bf16[64,1024]{1,0:T(8,128)(2,1)S(1)}, u32[]{:S(2)}, u32[]{:S(2)}) collective-permute-start(bf16[64,1024]{1,0:T(8,128)(2,1)S(1)} %slice.21), channel_id=1, source_target_pairs={{0,96},{32,0},{64,32},{96,64},{1,97},{33,1},{65,33},{97,65},{2,98}... | collective-permute-start | bytes 393224 | tf_op jit(solution)/shard_map/ppermute | solution.py:186
  33.8 0.0 collective-permute-done.10.refs_6_.refs_5_
  33.8 0.0 copy-done
  33.8 0.0 copy-done.2
  33.8 4.1 %shard_map.170.refs_6_ = bf16[16,64,1024]{2,1,0:T(8,128)(2,1)} custom-call(bf16[128,1024]{1,0:T(8,128)(2,1)S(1)} %copy-done.2, bf16[128,1024]{1,0:T(8,128)(2,1)S(1)} %collective-permute-done.2.refs_1_, bf16[128,1024]{1,0:T(8,128)(2,1)S(1)} %collective-permute-done.4.refs_2_, bf16[1024,512]{1,0:T(8,128)(2,1)S(1)} %copy-done, ...), custom_call_target="tpu_custom_call" | custom-call | bytes 1024 | tf_op jit(solution)/shard_map/pallas_call | solution.py:251
  37.9 0.0 collective-permute-done.3.refs_0_
  37.9 0.0 collective-permute-done.5.refs_1_
  37.9 3.1 %shard_map.171 = bf16[16,64,1024]{2,1,0:T(8,128)(2,1)} custom-call(bf16[64,1024]{1,0:T(8,128)(2,1)S(1)} %collective-permute-done.3.refs_0_, bf16[64,1024]{1,0:T(8,128)(2,1)S(1)} %collective-permute-done.5.refs_1_, bf16[1024,512]{1,0:T(8,128)(2,1)S(1)} %copy-done, ...), custom_call_target="tpu_custom_call", output_to_operand_aliasing={{}: (6, {})} | custom-call | bytes 1024 | tf_op jit(solution)/shard_map/pallas_call | solution.py:251
  41.0 34.7 %all_to_all.15.parts = bf16[16,64,1024]{2,1,0:T(8,128)(2,1)S(1)} all-to-all(bf16[16,64,1024]{2,1,0:T(8,128)(2,1)} %shard_map.171), channel_id=1, replica_groups=mesh['z'=4,'xh'=2,'c'=2,'xl'=2,'yh'=2,'yl'=2] {'xh','xl','yh','yl'}, dimensions={0} | all-to-all | bytes 4194304 | tf_op jit(solution)/shard_map/all_to_all | solution.py:526
  75.7 4.9 %shard_map.172 = (bf16[128,512]{1,0:T(8,128)(2,1)S(1)}, bf16[128,512]{1,0:T(8,128)(2,1)S(1)}, bf16[128,4224]{1,0:T(8,128)(2,1)}) custom-call(bf16[16,64,1024]{2,1,0:T(8,128)(2,1)S(1)} %all_to_all.15.parts, bf16[256,512]{1,0:T(8,128)(2,1)S(1)} %copy-done.3, bf16[128,512]{1,0:T(8,128)(2,1)S(1)} %collective-permute-done.7.extra, ...), custom_call_target="tpu_custom_call" | custom-call | flops 1024 | bytes 1024 | tf_op jit(solution)/shard_map/pallas_call | solution.py:331
  80.6 0.0 copy-start.6
  80.6 0.0 copy-start.4
  80.7 0.0 copy-start.5
  80.7 4.5 %all-to-all-start.1 = ((bf16[8,16,4224]{2,1,0:T(8,128)(2,1)}), bf16[8,16,4224]{2,1,0:T(8,128)(2,1)S(1)}, u32[]{:S(2)}, u32[]{:S(2)}) async-start(bf16[8,16,4224]{2,1,0:T(8,128)(2,1)} %bitcast.6), calls=%async_computation.1 | async-start | bytes 2162688 | tf_op jit(solution)/shard_map/all_to_all | solution.py:528
  85.2 0.0 collective-permute-start.11
  85.2 1.3 %collective-permute-done.11 = bf16[128,512]{1,0:T(8,128)(2,1)S(1)} collective-permute-done((bf16[128,512]{1,0:T(8,128)(2,1)S(1)}, bf16[128,512]{1,0:T(8,128)(2,1)S(1)}, u32[]{:S(2)}, u32[]{:S(2)}) %collective-permute-start.11) | collective-permute-done | bytes 131104 | tf_op jit(solution)/shard_map/ppermute | solution.py:182
  86.6 0.4 collective-permute-start.12
  87.0 0.0 copy-done.6
  87.0 5.2 %collective-permute-done.12 = bf16[64,1024]{1,0:T(8,128)(2,1)S(1)} collective-permute-done((bf16[64,1024]{1,0:T(8,128)(2,1)S(1)}, bf16[64,1024]{1,0:T(8,128)(2,1)S(1)}, u32[]{:S(2)}, u32[]{:S(2)}) %collective-permute-start.12) | collective-permute-done | bytes 131104 | tf_op jit(solution)/shard_map/ppermute | solution.py:182
  92.3 9.0 %all-to-all-done.1.got_hbm = bf16[8,16,4224]{2,1,0:T(8,128)(2,1)S(1)} async-done(((bf16[8,16,4224]{2,1,0:T(8,128)(2,1)}), bf16[8,16,4224]{2,1,0:T(8,128)(2,1)S(1)}, u32[]{:S(2)}, u32[]{:S(2)}) %all-to-all-start.1) | async-done | bytes 1081376 | tf_op jit(solution)/shard_map/all_to_all | solution.py:528
  101.3 0.0 copy-done.4
  101.3 0.0 copy-done.5
  101.3 1.2 %shard_map.173 = f32[128,1,128]{2,1,0:T(1,128)} custom-call(bf16[8,16,4224]{2,1,0:T(8,128)(2,1)S(1)} %all-to-all-done.1.got_hbm, f32[1,4096]{1,0:T(1,128)S(1)} %bitcast.11, s32[1,128]{1,0:T(1,128)S(1)} %bitcast.13, s32[1,128]{1,0:T(1,128)S(1)} %bitcast.14), custom_call_target="tpu_custom_call" | custom-call | flops 1024 | bytes 1024 | tf_op jit(solution)/shard_map/pallas_call | solution.py:393
  102.5 5.0 %all-to-all-start.2 = ((f32[128,1,128]{2,1,0:T(1,128)}), f32[128,1,128]{2,1,0:T(1,128)S(1)}, u32[]{:S(2)}, u32[]{:S(2)}) async-start(f32[128,1,128]{2,1,0:T(1,128)} %shard_map.173), calls=%async_computation.2 | async-start | bytes 131072 | tf_op jit(solution)/shard_map/all_to_all | solution.py:543
  107.5 0.8 maximum_select_fusion.1
  108.2 8.5 %all-to-all-done.2.all_hbm = f32[128,1,128]{2,1,0:T(1,128)S(1)} async-done(((f32[128,1,128]{2,1,0:T(1,128)}), f32[128,1,128]{2,1,0:T(1,128)S(1)}, u32[]{:S(2)}, u32[]{:S(2)}) %all-to-all-start.2) | async-done | bytes 65568 | tf_op jit(solution)/shard_map/all_to_all | solution.py:543
  116.8 1.1 shard_map.174
  (17 shorter events, 0.2 us)
Async XLA Ops:
  0.6 17.4 %collective-permute-start = (bf16[512,4096]{1,0:T(8,128)(2,1)}, bf16[512,4096]{1,0:T(8,128)(2,1)}, u32[]{:S(2)}, u32[]{:S(2)}) collective-permute-start(bf16[512,4096]{1,0:T(8,128)(2,1)} %up_mine.1), channel_id=1, source_target_pairs={{0,8},{8,0},{1,9},{9,1},{2,10},{10,2},{3,11},{11,3},{4,12},{12,4},... | collective-permute-start | bytes 12582920 | tf_op jit(solution)/shard_map/ppermute | solution.py:182
  0.7 17.3 %collective-permute-start.1 = (bf16[1024,512]{1,0:T(8,128)(2,1)}, bf16[1024,512]{1,0:T(8,128)(2,1)}, u32[]{:S(2)}, u32[]{:S(2)}) collective-permute-start(bf16[1024,512]{1,0:T(8,128)(2,1)} %refs_2_.1), channel_id=1, source_target_pairs={{0,8},{8,0},{1,9},{9,1},{2,10},{10,2},{3,11},{11,3},{4,12},{12,4},... | collective-permute-start | bytes 3145736 | tf_op jit(solution)/shard_map/ppermute | solution.py:182
  1.2 27.0 %collective-permute-start.6 = (bf16[1024,512]{1,0:T(8,128)(2,1)}, bf16[1024,512]{1,0:T(8,128)(2,1)}, u32[]{:S(2)}, u32[]{:S(2)}) collective-permute-start(bf16[1024,512]{1,0:T(8,128)(2,1)} %refs_2_.1), channel_id=1, source_target_pairs={{0,16},{16,0},{1,17},{17,1},{2,18},{18,2},{3,19},{19,3},{4,20},{20... | collective-permute-start | bytes 3145736 | tf_op jit(solution)/shard_map/ppermute | solution.py:182
  4.3 13.6 %copy-start.3 = (bf16[256,512]{1,0:T(8,128)(2,1)S(1)}, bf16[256,512]{1,0:T(8,128)(2,1)}, u32[]{:S(2)}) copy-start(bf16[256,512]{1,0:T(8,128)(2,1)} %res.1) | copy-start | bytes 786436
  18.0 7.0 %copy-start.7 = (bf16[512]{0:T(512)(128)(2,1)S(1)}, bf16[512]{0:T(512)(128)(2,1)}, u32[]{:S(2)}) copy-start(bf16[512]{0:T(512)(128)(2,1)} %param.27) | copy-start | bytes 3076
  18.1 1.0 copy-start.1
  19.0 14.7 %copy-start = (bf16[1024,512]{1,0:T(8,128)(2,1)S(1)}, bf16[1024,512]{1,0:T(8,128)(2,1)}, u32[]{:S(2)}) copy-start(bf16[1024,512]{1,0:T(8,128)(2,1)} %refs_2_.1) | copy-start | bytes 3145732
  19.0 14.7 %copy-start.2 = (bf16[128,1024]{1,0:T(8,128)(2,1)S(1)}, bf16[128,1024]{1,0:T(8,128)(2,1)}, u32[]{:S(2)}) copy-start(bf16[128,1024]{1,0:T(8,128)(2,1)} %shard_map.167.refs_1_.refs_0_) | copy-start | bytes 786436
  19.0 4.3 %collective-permute-start.7 = (bf16[128,512]{1,0:T(8,128)(2,1)S(1)}, bf16[128,512]{1,0:T(8,128)(2,1)S(1)}, u32[]{:S(2)}, u32[]{:S(2)}) collective-permute-start(bf16[128,512]{1,0:T(8,128)(2,1)S(1)} %constant_dynamic-slice_fusion.5), channel_id=1, source_target_pairs={{0,8},{8,0},{1,9},{9,1},{2,10},{10,2},{3,11},{11,3},{4,12},{12,4},... | collective-permute-start | bytes 393224 | tf_op jit(solution)/shard_map/ppermute | solution.py:182
  19.1 11.2 %collective-permute-start.2 = (bf16[128,1024]{1,0:T(8,128)(2,1)}, bf16[128,1024]{1,0:T(8,128)(2,1)S(1)}, u32[]{:S(2)}, u32[]{:S(2)}) collective-permute-start(bf16[128,1024]{1,0:T(8,128)(2,1)} %shard_map.167.refs_1_.refs_0_), channel_id=1, source_target_pairs={{0,32},{32,64},{64,96},{96,0},{1,33},{33,65},{65,97},{97,1},{2,34}... | collective-permute-start | bytes 786440 | tf_op jit(solution)/shard_map/ppermute | solution.py:186
  21.1 9.2 %collective-permute-start.4 = (bf16[128,1024]{1,0:T(8,128)(2,1)}, bf16[128,1024]{1,0:T(8,128)(2,1)S(1)}, u32[]{:S(2)}, u32[]{:S(2)}) collective-permute-start(bf16[128,1024]{1,0:T(8,128)(2,1)} %shard_map.167.refs_1_.refs_0_), channel_id=1, source_target_pairs={{0,96},{32,0},{64,32},{96,64},{1,97},{33,1},{65,33},{97,65},{2,98}... | collective-permute-start | bytes 786440 | tf_op jit(solution)/shard_map/ppermute | solution.py:186
  23.4 5.5 %collective-permute-start.8 = (bf16[64,1024]{1,0:T(8,128)(2,1)S(1)}, bf16[64,1024]{1,0:T(8,128)(2,1)S(1)}, u32[]{:S(2)}, u32[]{:S(2)}) collective-permute-start(bf16[64,1024]{1,0:T(8,128)(2,1)S(1)} %pad_maximum_fusion), channel_id=1, source_target_pairs={{0,1},{1,0},{2,3},{3,2},{4,5},{5,4},{6,7},{7,6},{8,9},{9,8},{10,11... | collective-permute-start | bytes 393224 | tf_op jit(solution)/shard_map/ppermute | solution.py:182
  25.0 3.2 %collective-permute-start.9 = (bf16[16,512]{1,0:T(8,128)(2,1)S(1)}, bf16[16,512]{1,0:T(8,128)(2,1)S(1)}, u32[]{:S(2)}, u32[]{:S(2)}) collective-permute-start(bf16[16,512]{1,0:T(8,128)(2,1)S(1)} %fusion.gain), channel_id=1, source_target_pairs={{0,8},{8,0},{1,9},{9,1},{2,10},{10,2},{3,11},{11,3},{4,12},{12,4},... | collective-permute-start | bytes 49160 | tf_op jit(solution)/shard_map/ppermute | solution.py:182
  30.3 3.4 %collective-permute-start.10 = (bf16[1024,512]{1,0:T(8,128)(2,1)}, bf16[1024,512]{1,0:T(8,128)(2,1)S(1)}, u32[]{:S(2)}, u32[]{:S(2)}) collective-permute-start(bf16[1024,512]{1,0:T(8,128)(2,1)} %shard_map.169.refs_5_.refs_4_), channel_id=1, source_target_pairs={{0,8},{8,0},{1,9},{9,1},{2,10},{10,2},{3,11},{11,3},{4,12},{12,4},... | collective-permute-start | bytes 3145736 | tf_op jit(solution)/shard_map/ppermute | solution.py:182
  30.4 7.5 %collective-permute-start.3 = (bf16[64,1024]{1,0:T(8,128)(2,1)S(1)}, bf16[64,1024]{1,0:T(8,128)(2,1)S(1)}, u32[]{:S(2)}, u32[]{:S(2)}) collective-permute-start(bf16[64,1024]{1,0:T(8,128)(2,1)S(1)} %slice.20), channel_id=1, source_target_pairs={{0,32},{32,64},{64,96},{96,0},{1,33},{33,65},{65,97},{97,1},{2,34}... | collective-permute-start | bytes 393224 | tf_op jit(solution)/shard_map/ppermute | solution.py:186
  31.7 6.2 %collective-permute-start.5 = (bf16[64,1024]{1,0:T(8,128)(2,1)S(1)}, bf16[64,1024]{1,0:T(8,128)(2,1)S(1)}, u32[]{:S(2)}, u32[]{:S(2)}) collective-permute-start(bf16[64,1024]{1,0:T(8,128)(2,1)S(1)} %slice.21), channel_id=1, source_target_pairs={{0,96},{32,0},{64,32},{96,64},{1,97},{33,1},{65,33},{97,65},{2,98}... | collective-permute-start | bytes 393224 | tf_op jit(solution)/shard_map/ppermute | solution.py:186
  80.6 6.3 %copy-start.6 = (bf16[4096]{0:T(1024)(128)(2,1)S(1)}, bf16[4096]{0:T(1024)(128)(2,1)}, u32[]{:S(2)}) copy-start(bf16[4096]{0:T(1024)(128)(2,1)} %param.29) | copy-start | bytes 24580
  80.6 20.6 %copy-start.4 = (s32[128]{0:T(128)S(1)}, s32[128]{0:T(128)}, u32[]{:S(2)}) copy-start(s32[128]{0:T(128)} %ids_hbm.1) | copy-start | bytes 1540
  80.7 20.6 %copy-start.5 = (s32[128]{0:T(128)S(1)}, s32[128]{0:T(128)}, u32[]{:S(2)}) copy-start(s32[128]{0:T(128)} %param.24) | copy-start | bytes 1540
  80.7 20.6 %all-to-all-start.1 = ((bf16[8,16,4224]{2,1,0:T(8,128)(2,1)}), bf16[8,16,4224]{2,1,0:T(8,128)(2,1)S(1)}, u32[]{:S(2)}, u32[]{:S(2)}) async-start(bf16[8,16,4224]{2,1,0:T(8,128)(2,1)} %bitcast.6), calls=%async_computation.1 | async-start | bytes 2162688 | tf_op jit(solution)/shard_map/all_to_all | solution.py:528
  85.2 1.3 %collective-permute-start.11 = (bf16[128,512]{1,0:T(8,128)(2,1)S(1)}, bf16[128,512]{1,0:T(8,128)(2,1)S(1)}, u32[]{:S(2)}, u32[]{:S(2)}) collective-permute-start(bf16[128,512]{1,0:T(8,128)(2,1)S(1)} %get-tuple-element.9), channel_id=1, source_target_pairs={{0,8},{8,0},{1,9},{9,1},{2,10},{10,2},{3,11},{11,3},{4,12},{12,4},... | collective-permute-start | bytes 393224 | tf_op jit(solution)/shard_map/ppermute | solution.py:182
  86.6 5.6 %collective-permute-start.12 = (bf16[64,1024]{1,0:T(8,128)(2,1)S(1)}, bf16[64,1024]{1,0:T(8,128)(2,1)S(1)}, u32[]{:S(2)}, u32[]{:S(2)}) collective-permute-start(bf16[64,1024]{1,0:T(8,128)(2,1)S(1)} %pad_maximum_fusion.1), channel_id=1, source_target_pairs={{0,1},{1,0},{2,3},{3,2},{4,5},{5,4},{6,7},{7,6},{8,9},{9,8},{10,11... | collective-permute-start | bytes 393224 | tf_op jit(solution)/shard_map/ppermute | solution.py:182
  102.5 14.3 %all-to-all-start.2 = ((f32[128,1,128]{2,1,0:T(1,128)}), f32[128,1,128]{2,1,0:T(1,128)S(1)}, u32[]{:S(2)}, u32[]{:S(2)}) async-start(f32[128,1,128]{2,1,0:T(1,128)} %shard_map.173), calls=%async_computation.2 | async-start | bytes 131072 | tf_op jit(solution)/shard_map/all_to_all | solution.py:543
